TPU v7x, 32 devices: a whole 2x2x4 slice. The times are simulated.
32 devices in a mesh: groups: 2 (over y), store: 4 (over z), tensor: 4 (over x, core).
Axes of the slice: x: 2, y: 2, z: 4, core: 2. Of those that a mesh axis runs over, the one named last changes fastest.
Arguments:
- states: bfloat16 [128, 6144], P(('groups', 'store')), parts along dimension 0, may hold values from -6 to 6
- weight_in: bfloat16 [6144, 24576], P('store', 'tensor'), may hold values from -0.078125 to 0.078125
- bias_in: float32 [24576], P('tensor'), may hold values from -3 to 3
- weight_out: bfloat16 [24576, 6144], P('tensor', 'store'), may hold values from -0.25 to 0.25
- bias_out: float32 [6144], P('tensor'), may hold values from -2 to 2
- block_lists: int32 [128, 4, 4], P(('groups', 'store'), 'tensor'), parts along dimension 0, may hold values from -1 to 47, as said below
- union_blocks: int32 [8, 16], P(('groups', 'tensor')), parts along dimension 0, may hold values from 0 to 47, as said below
Outputs:
- ffn_output: bfloat16 [128, 6144], P(('groups', 'store'), 'tensor'), parts along dimension 0
There are 2 independent parts, one for each index of `groups`. A program takes and returns all parts, laid end to end along the dimension named above; an argument that names none is the same for every part. Nothing has to cross between parts.
Inputs may be any that keep to these rules, and one draw needn't show every extreme that they name: `block_lists`: for each row and slice the non-negative entries come first, are distinct, and all lie in union_blocks of that slice; every row has at least one; in every slice some row fills all 4 slots. `union_blocks`: each slice's 16 entries are distinct.
All inputs are finite; a program needn't handle non-finite values.
Results may differ from a plain program's by a relative error of at most 0.0048.
Values may be sent and summed in bfloat16 or wider, within the bound.
No kernel may reach another device: no remote copies, remote signals or barrier semaphores. Data moves between devices by JAX's collectives and lax.ppermute only.
A program may use at most 192 MiB of HBM per device.

v0:
```python
import jax
import jax.numpy as jnp
from jax import lax
from jax.sharding import PartitionSpec as P

BLOCK = 128


def local(states, weight_in, bias_in, weight_out, bias_out, block_lists, union_blocks):
    slice_width = weight_in.shape[0]
    union_ids = union_blocks[0]
    union_count = union_ids.shape[0]
    block_count = weight_in.shape[1] // BLOCK
    slot_count = block_lists.shape[2]
    own_rows = states.shape[0]
    sliced_states = lax.all_to_all(states, "store", split_axis=1, concat_axis=0, tiled=True)
    all_ids = lax.all_gather(block_lists, "store", axis=0, tiled=True)[:, 0, :]
    union_range = jnp.arange(union_count, dtype=jnp.int32)
    all_match = all_ids[:, :, None] == union_ids[None, None, :]
    all_keep = jnp.any(all_match, axis=-1)
    slot_pos = jnp.sum(jnp.where(all_match, union_range[None, None, :], 0), axis=-1)
    weight_in_union = jnp.take(
        weight_in.reshape(slice_width, block_count, BLOCK), union_ids, axis=1
    ).reshape(slice_width, union_count * BLOCK)
    weight_out_union = jnp.take(
        weight_out.reshape(block_count, BLOCK, slice_width), union_ids, axis=0
    ).reshape(union_count * BLOCK, slice_width)
    bias_blocks = bias_in.reshape(block_count, BLOCK)
    dense_pre = jnp.dot(sliced_states, weight_in_union, preferred_element_type=jnp.float32).reshape(
        own_rows * lax.axis_size("store"), union_count, BLOCK
    )
    pos_part = slot_pos
    keep_part = all_keep
    picked = jnp.take_along_axis(dense_pre, pos_part[:, :, None], axis=1)
    pre_act = lax.psum_scatter(
        (picked * keep_part[:, :, None].astype(jnp.float32)).reshape(
            own_rows * lax.axis_size("store"), slot_count * BLOCK
        ),
        "store",
        scatter_dimension=0,
        tiled=True,
    )
    own_ids = block_lists[:, 0, :]
    own_keep = jnp.any(own_ids[:, :, None] == union_ids[None, None, :], axis=-1)
    bias_rows = jnp.take(bias_blocks, jnp.maximum(own_ids, 0), axis=0).reshape(
        own_ids.shape[0], slot_count * BLOCK
    )
    active_mask = jnp.repeat(own_keep.astype(jnp.float32), BLOCK, axis=1)
    hidden = (jnp.maximum(pre_act + bias_rows, 0.0) * active_mask).astype(jnp.bfloat16)
    pos_part = slot_pos
    keep_part = all_keep
    project_hidden = lax.all_gather(hidden, "store", axis=0, tiled=True)
    one_hot = jnp.logical_and(
        pos_part[:, :, None] == union_range[None, None, :], keep_part[:, :, None]
    ).astype(jnp.bfloat16)
    spread = jnp.einsum(
        "rku,rkn->run",
        one_hot,
        project_hidden.reshape(-1, slot_count, BLOCK),
        preferred_element_type=jnp.float32,
    ).astype(jnp.bfloat16)
    partial_value = jnp.dot(
        spread.reshape(-1, union_count * BLOCK),
        weight_out_union,
        preferred_element_type=jnp.float32,
    )
    row_terms = lax.all_to_all(partial_value, "store", split_axis=0, concat_axis=1, tiled=True)
    summed = lax.psum_scatter(row_terms, "tensor", scatter_dimension=1, tiled=True)
    return (summed + bias_out[None, :]).astype(jnp.bfloat16)


def solution(mesh):
    return jax.shard_map(
        local,
        mesh=mesh,
        in_specs=(
            P(("groups", "store"), None),
            P("store", "tensor"),
            P("tensor"),
            P("tensor", "store"),
            P("tensor"),
            P(("groups", "store"), "tensor", None),
            P(("groups", "tensor"), None),
        ),
        out_specs=P(("groups", "store"), "tensor"),
        check_vma=False,
    )
```

profile of v0, /device:TPU:0, one launch (start us, length us, event | category | flops | bytes accessed | tf_op | source)
XLA Modules:
  0.0 210.6 jit_solution(3482418188841268363)
XLA Ops:
  6.5 0.0 copy-start
  6.5 1.6 copy.60
  8.2 6.3 %all-to-all-start = ((bf16[16,4,1536]{2,0,1:T(8,128)(2,1)}), bf16[16,4,1536]{2,0,1:T(8,128)(2,1)S(1)}, u32[]{:S(2)}, u32[]{:S(2)}) async-start(bf16[16,4,1536]{2,0,1:T(8,128)(2,1)} %bitcast.59), calls=%async_computation | async-start | bytes 393216 | tf_op jit(solution)/shard_map/all_to_all | solution.py:16
  14.5 0.0 reduce-scatter.3.cloned.1.call-start
  14.5 0.7 fusion.10
  15.1 0.7 compare_and_fusion
  15.8 0.8 copy.35
  16.6 13.7 %all_gather.6 = s32[64,1,4]{2,1,0:T(1,128)S(1)} all-gather(s32[16,1,4]{2,1,0:T(1,128)S(1)} %copy.35), channel_id=1, replica_groups=mesh['groups'=2,'store'=4,'tensor'=4] {'store'}, dimensions={0}, use_global_device_ids=true | all-gather | bytes 1280 | tf_op jit(solution)/shard_map/all_gather | solution.py:17
  30.2 0.1 copy.36
  30.3 0.8 fusion.4
  31.1 0.7 compare_reduce_fusion
  31.8 0.7 broadcast_maximum_fusion
  32.5 0.1 copy.44
  32.6 0.1 reshape.218
  32.7 24.7 %copy.40 = bf16[1536,6144]{0,1:T(8,128)(2,1)} copy(bf16[1536,6144]{1,0:T(8,128)(2,1)} %param.8) | data formatting | bytes 37748736 | tf_op args[1]
  57.4 24.7 %copy.41 = bf16[1536,48,128]{2,0,1:T(8,128)(2,1)} copy(bf16[1536,48,128]{0,2,1:T(8,128)(2,1)} %bitcast.62) | data formatting | bytes 37748736 | tf_op jit(solution)/shard_map/reshape | solution.py:23
  82.1 10.3 %gather_fusion = bf16[16,1536,128]{2,1,0:T(8,128)(2,1)} fusion(bf16[1536,48,128]{2,0,1:T(8,128)(2,1)} %copy.41, s32[1024]{0:T(1024)S(1)} %pad_clamp_fusion.1), kind=kCustom, calls=%fused_computation | custom fusion | bytes 12582976 | tf_op jit(solution)/shard_map/jit(_take)/gather | solution.py:22
  92.4 6.0 %select_bitcast_fusion = bf16[1536,16,128]{2,0,1:T(8,128)(2,1)} fusion(bf16[16,1536,128]{2,1,0:T(8,128)(2,1)} %gather_fusion, pred[16]{0:T(512)(128)(4,1)S(1)} %compare_and_fusion), kind=kLoop, calls=%fused_computation.4 | loop fusion | flops 3145728 | bytes 12582928 | tf_op jit(solution)/shard_map/jit(_take)/select_n | solution.py:22
  98.4 8.7 %copy.42 = bf16[1536,16,128]{0,2,1:T(8,128)(2,1)} copy(bf16[1536,16,128]{2,0,1:T(8,128)(2,1)} %select_bitcast_fusion) | data formatting | bytes 12582912 | tf_op jit(solution)/shard_map/jit(_take)/select_n | solution.py:22
  107.1 0.1 copy.39
  107.2 0.1 copy.45
  107.3 0.1 copy.47
  107.4 0.1 reshape.204
  107.5 10.0 %gather_fusion.2 = bf16[16,128,1536]{2,1,0:T(8,128)(2,1)} fusion(bf16[48,128,1536]{2,1,0:T(8,128)(2,1)} %bitcast.66, s32[1024]{0:T(1024)S(1)} %pad_clamp_fusion.1), kind=kCustom, calls=%fused_computation.2 | custom fusion | bytes 12582976 | tf_op jit(solution)/shard_map/jit(_take)/gather | solution.py:25
  117.5 0.0 copy-start.1
  117.5 0.0 copy-start.3
  117.5 6.1 %broadcast_select_fusion = bf16[16,128,1536]{2,1,0:T(8,128)(2,1)} fusion(bf16[16,128,1536]{2,1,0:T(8,128)(2,1)} %gather_fusion.2, pred[16]{0:T(512)(128)(4,1)S(1)} %compare_and_fusion), kind=kLoop, calls=%fused_computation.5 | loop fusion | flops 3145728 | bytes 12582928 | tf_op jit(solution)/shard_map/jit(_take)/select_n | solution.py:25
  123.6 0.0 copy-done.1
  123.6 0.0 copy-done.3
  123.6 0.2 compare_reduce_fusion.1
  123.8 0.0 all-to-all-done
  123.8 4.8 %convolution_bitcast_fusion = f32[8,8,16,128]{3,1,2,0:T(8,128)S(1)} fusion(bf16[1536,2048]{0,1:T(8,128)(2,1)} %bitcast.64, bf16[64,1536]{1,0:T(8,128)(2,1)S(1)} %bitcast.69), kind=kOutput, calls=%fused_computation.6 | convolution fusion | flops 402653184 | bytes 7012352 | tf_op jit(solution)/shard_map/dot_general | solution.py:29
  128.6 0.1 copy.52
  128.7 1.9 gather_fusion.3
  130.6 0.0 copy-start.2
  130.6 0.2 select_multiply_fusion
  130.8 0.6 copy.61
  131.5 0.0 reduce-scatter.3.cloned.1.call-update
  131.5 0.0 reduce-scatter.5.cloned.1.call-start
  131.6 0.1 copy.37
  131.7 0.1 copy.38
  131.8 0.1 copy.48
  131.9 0.1 copy.46
  132.0 0.0 copy-done
  132.0 0.6 gather_fusion.1
  132.6 0.1 broadcast_select_fusion.1
  132.7 19.1 %reduce-scatter.3.cloned.1.call-done = f32[16,512]{1,0:T(8,128)} async-done(((f32[64,512]{1,0:T(8,128)}), f32[16,512]{1,0:T(8,128)}) %reduce-scatter.3.cloned.1.call-update) | async-done | bytes 32784 | tf_op jit(solution)/shard_map/reduce_scatter | solution.py:35
  151.8 0.1 broadcast_in_dim.71
  151.9 0.8 fusion.5
  152.6 13.1 %all_gather.7 = bf16[64,512]{1,0:T(8,128)(2,1)S(1)} all-gather(bf16[16,512]{1,0:T(8,128)(2,1)S(1)} %fusion.5), channel_id=1, replica_groups=mesh['groups'=2,'store'=4,'tensor'=4] {'store'}, dimensions={0}, use_global_device_ids=true | all-gather | bytes 81920 | tf_op jit(solution)/shard_map/all_gather | solution.py:52
  165.8 0.5 convolution_convert_fusion
  166.3 0.1 dot_general.16
  166.4 4.0 %fusion.11 = f32[4,16,1536]{2,1,0:T(8,128)S(1)} fusion(bf16[4,16,2048]{2,1,0:T(8,128)(2,1)S(1)} %dot_general.16, bf16[2048,1536,1]{1,0,2:T(8,128)(2,1)} %bitcast.63), kind=kOutput, calls=%fused_computation.39 | convolution fusion | flops 402653184 | bytes 6946816 | tf_op jit(solution)/shard_map/dot_general | solution.py:62
  170.4 11.3 %all_to_all.35 = f32[4,16,1536]{2,1,0:T(8,128)S(1)} all-to-all(f32[4,16,1536]{2,1,0:T(8,128)S(1)} %fusion.11), channel_id=1, replica_groups=mesh['groups'=2,'store'=4,'tensor'=4] {'store'}, dimensions={0} | all-to-all | bytes 786432 | tf_op jit(solution)/shard_map/all_to_all | solution.py:67
  181.7 0.8 copy.51
  182.4 0.0 reduce-scatter.5.cloned.1.call-update
  182.5 19.8 %reduce-scatter.5.cloned.1.call-done = f32[16,1536]{1,0:T(8,128)} async-done(((f32[16,6144]{1,0:T(8,128)}), f32[16,1536]{1,0:T(8,128)}) %reduce-scatter.5.cloned.1.call-update) | async-done | bytes 98320 | tf_op jit(solution)/shard_map/reduce_scatter | solution.py:68
  202.2 0.0 copy-done.2
  202.2 1.5 add_convert_fusion
  (8 shorter events, 0.1 us)
Async XLA Ops:
  6.5 125.5 %copy-start = (f32[6144]{0:T(1024)S(1)}, f32[6144]{0:T(1024)}, u32[]{:S(2)}) copy-start(f32[6144]{0:T(1024)} %param.9) | copy-start | bytes 73732
  8.2 115.7 %all-to-all-start = ((bf16[16,4,1536]{2,0,1:T(8,128)(2,1)}), bf16[16,4,1536]{2,0,1:T(8,128)(2,1)S(1)}, u32[]{:S(2)}, u32[]{:S(2)}) async-start(bf16[16,4,1536]{2,0,1:T(8,128)(2,1)} %bitcast.59), calls=%async_computation | async-start | bytes 393216 | tf_op jit(solution)/shard_map/all_to_all | solution.py:16
  14.5 137.3 %reduce-scatter.3.cloned.1.call-start = ((), (), s32[]{:S(2)}) async-start(), calls=%async_computation.4 | async-start | bytes 163840 | tf_op jit(solution)/shard_map/reduce_scatter | solution.py:35
  117.5 6.1 %copy-start.1 = (s32[16,1,4]{0,2,1:T(4,128)S(1)}, s32[16,1,4]{0,2,1:T(4,128)}, u32[]{:S(2)}) copy-start(s32[16,1,4]{0,2,1:T(4,128)} %param.12) | copy-start | bytes 772
  117.5 6.1 %copy-start.3 = (s32[1,16]{1,0:T(1,128)S(1)}, s32[1,16]{1,0:T(1,128)}, u32[]{:S(2)}) copy-start(s32[1,16]{1,0:T(1,128)} %param.13) | copy-start | bytes 196
  130.6 71.6 %copy-start.2 = (f32[1536]{0:T(1024)S(1)}, f32[1536]{0:T(1024)}, u32[]{:S(2)}) copy-start(f32[1536]{0:T(1024)} %param.11) | copy-start | bytes 18436
  131.5 70.7 %reduce-scatter.5.cloned.1.call-start = ((), (), s32[]{:S(2)}) async-start(), calls=%async_computation.5 | async-start | bytes 491520 | tf_op jit(solution)/shard_map/reduce_scatter | solution.py:68
Sparse Core Ops, SparseCore 0:
  131.6 20.1 reduce-scatter.2
  182.6 19.5 reduce-scatter.4
where the time goes:
time: 213 us; the launch traced here: 211 us
  local copies, waits for them, and re-layouts  86 us (40%)
  waiting for transfers between devices  38.9 us (18%)
  blocking collectives  38.1 us (18%)
  other arithmetic  18.5 us (9%)
  between operations  13.5 us (6%)
  matrix products  9.25 us (4%)
  starting transfers between devices  6.36 us (3%)
    unnamed x12, local copies, waits for them, and re-layouts  26.2 us
    reshape x1, local copies, waits for them, and re-layouts, local(): weight_in.reshape(slice_width, block_count, BLOCK)  24.7 us
    reduce_scatter x1, waiting for transfers between devices, local(): lax.psum_scatter(row_terms, 'tensor', scatter_dimension=1, tiled=True)  19.8 us
    reduce_scatter x1, waiting for transfers between devices, local(): lax.psum_scatter((picked * keep_part[:, :, None].astype(jnp.float32)).res...  19.1 us
    all_gather x1, blocking collectives, local(): all_ids = lax.all_gather(block_lists, 'store', axis=0, tiled=True)[:, 0, :]  13.7 us
    all_gather x1, blocking collectives, local(): project_hidden = lax.all_gather(hidden, 'store', axis=0, tiled=True)  13.1 us
    all_to_all x1, blocking collectives, local(): lax.all_to_all(partial_value, 'store', split_axis=0, concat_axis=1, tiled...  11.3 us
    gather x1, local copies, waits for them, and re-layouts, local(): jnp.take(weight_in.reshape(slice_width, block_count, BLOCK), union_ids, a...  10.3 us
  transfers between devices with their start and end apart: 3, of which 2 were waited for; matrix products, arithmetic and copies ran while one was open for 46% of the time, Pallas kernels for 0%

commit v1 on v0

v1 whole, which is shorter than its diff:
```python
import functools

import jax
import jax.numpy as jnp
from jax import lax
from jax.experimental import pallas as pl
from jax.experimental.pallas import tpu as pltpu
from jax.sharding import PartitionSpec as P

BLOCK = 128
BF16 = jnp.bfloat16
F32 = jnp.float32
VMEM = pltpu.VMEM
SMEM = pltpu.SMEM


def whole(space):
    return pl.BlockSpec(memory_space=space)


def split_kernel(count, width, me_ref, states_ref, ids_ref, *out_refs):
    me = me_ref[0]
    slots = ids_ref.shape[1]
    for k in range(count):
        start = pl.multiple_of((me ^ k) * width, BLOCK)
        out_refs[k][:, :width] = states_ref[:, pl.ds(start, width)]
        out_refs[k][:, width:] = jnp.zeros((states_ref.shape[0], BLOCK), BF16)
        out_refs[k][:, width : width + slots] = ids_ref[...].astype(F32).astype(BF16)


def gather_kernel(union_ref, win_ref, wout_ref, win_out, wout_out, sems):
    union = union_ref.shape[0]
    for u in range(union):
        start = pl.multiple_of(union_ref[u] * BLOCK, BLOCK)
        pltpu.make_async_copy(
            win_ref.at[:, pl.ds(start, BLOCK)], win_out.at[:, pl.ds(u * BLOCK, BLOCK)], sems.at[0, u]
        ).start()
    for u in range(union):
        start = pl.multiple_of(union_ref[u] * BLOCK, BLOCK)
        pltpu.make_async_copy(
            wout_ref.at[pl.ds(start, BLOCK), :], wout_out.at[pl.ds(u * BLOCK, BLOCK), :], sems.at[1, u]
        ).start()
    for u in range(union):
        start = pl.multiple_of(union_ref[u] * BLOCK, BLOCK)
        pltpu.make_async_copy(
            win_ref.at[:, pl.ds(start, BLOCK)], win_out.at[:, pl.ds(u * BLOCK, BLOCK)], sems.at[0, u]
        ).wait()
        pltpu.make_async_copy(
            wout_ref.at[pl.ds(start, BLOCK), :], wout_out.at[pl.ds(u * BLOCK, BLOCK), :], sems.at[1, u]
        ).wait()


def first_kernel(count, slots, union_ref, *refs):
    chunk_refs = refs[:count]
    win_ref, pre_ref, ids_ref, dense = refs[count:]
    width, total = win_ref.shape
    rows = chunk_refs[0].shape[0]
    union = union_ref.shape[0]
    states = jnp.concatenate([c[:, :width] for c in chunk_refs], axis=0)
    ids = jnp.concatenate([c[:, width:] for c in chunk_refs], axis=0).astype(F32)
    ids_ref[...] = ids
    step = 2 * BLOCK
    for n in range(0, total, step):
        dense[:, n : n + step] = jnp.dot(states, win_ref[:, n : n + step], preferred_element_type=F32)
    for j in range(count):
        part = slice(j * rows, (j + 1) * rows)
        for k in range(slots):
            mine = jnp.broadcast_to(ids[part, k : k + 1], (rows, BLOCK))
            picked = jnp.zeros((rows, BLOCK), F32)
            for u in range(union):
                block = union_ref[u].astype(F32)
                picked = jnp.where(mine == block, dense[part, u * BLOCK : (u + 1) * BLOCK], picked)
            pre_ref[part, k * BLOCK : (k + 1) * BLOCK] = picked.astype(pre_ref.dtype)


def second_kernel(count, slots, me_ref, union_ref, ids_ref, bias_ref, *refs):
    part_refs = refs[:count]
    wout_ref = refs[count]
    out_refs = refs[count + 1 : 2 * count + 1]
    spread, terms = refs[2 * count + 1 :]
    store, tensor = me_ref[0], me_ref[1]
    rows = ids_ref.shape[0] // count
    union = union_ref.shape[0]
    ids = ids_ref[...]
    for j in range(count):
        part = slice(j * rows, (j + 1) * rows)
        mines = [jnp.broadcast_to(ids[part, k : k + 1], (rows, BLOCK)) for k in range(slots)]
        pres = []
        for k in range(slots):
            cols = slice(k * BLOCK, (k + 1) * BLOCK)
            pres.append(sum(p[part, cols].astype(F32) for p in part_refs))
        for u in range(union):
            block = union_ref[u].astype(F32)
            value = jnp.zeros((rows, BLOCK), F32)
            bias = bias_ref[pl.ds(union_ref[u], 1), :]
            for k in range(slots):
                value = jnp.where(mines[k] == block, jnp.maximum(pres[k] + bias, 0.0), value)
            spread[part, u * BLOCK : (u + 1) * BLOCK] = value.astype(BF16)
    step = 2 * BLOCK
    width = wout_ref.shape[1]
    hidden = spread[...]
    for n in range(0, width, step):
        product = jnp.dot(hidden, wout_ref[:, n : n + step], preferred_element_type=F32)
        terms[:, :, n : n + step] = product.reshape(count, rows, step)
    for k in range(count):
        out_refs[k][...] = terms[store ^ tensor ^ k].astype(out_refs[k].dtype)


def fast(states, weight_in, bias_in, weight_out, bias_out, block_lists, union_blocks):
    count = lax.axis_size("store")
    width = weight_in.shape[0]
    rows = states.shape[0]
    slots = block_lists.shape[2]
    union_ids = union_blocks[0]
    union = union_ids.shape[0]
    me = jnp.stack([lax.axis_index("store"), lax.axis_index("tensor")]).astype(jnp.int32)
    total = union * BLOCK

    chunks = pl.pallas_call(
        functools.partial(split_kernel, count, width),
        out_shape=[jax.ShapeDtypeStruct((rows, width + BLOCK), BF16)] * count,
        in_specs=[whole(SMEM), whole(VMEM), whole(VMEM)],
        out_specs=[whole(VMEM)] * count,
        name="split_states",
    )(me, states, block_lists[:, 0, :])

    def over_store(k):
        return [(i, i ^ k) for i in range(count)]

    got = [chunks[0]] + [lax.ppermute(chunks[k], "store", over_store(k)) for k in range(1, count)]

    win, wout = pl.pallas_call(
        gather_kernel,
        out_shape=[VMEM((width, total), BF16), VMEM((total, width), BF16)],
        in_specs=[whole(SMEM), whole(pl.ANY), whole(pl.ANY)],
        out_specs=[whole(VMEM), whole(VMEM)],
        scratch_shapes=[pltpu.SemaphoreType.DMA((2, union))],
        compiler_params=pltpu.CompilerParams(vmem_limit_bytes=40 * 2**20),
        cost_estimate=pl.CostEstimate(flops=0, bytes_accessed=4 * width * total, transcendentals=0),
        name="gather_weights",
    )(union_ids, weight_in, weight_out)

    pre, ids = pl.pallas_call(
        functools.partial(first_kernel, count, slots),
        out_shape=[
            jax.ShapeDtypeStruct((count * rows, slots * BLOCK), BF16),
            jax.ShapeDtypeStruct((count * rows, BLOCK), F32),
        ],
        in_specs=[whole(SMEM)] + [whole(VMEM)] * (count + 1),
        out_specs=[whole(VMEM)] * 2,
        scratch_shapes=[VMEM((count * rows, total), F32)],
        compiler_params=pltpu.CompilerParams(vmem_limit_bytes=40 * 2**20),
        name="first_dot",
    )(union_ids, *got, win)

    def reorder(a, k):
        blocks = a.reshape(count, rows, a.shape[1])
        return jnp.concatenate([blocks[j ^ k] for j in range(count)], axis=0)

    parts = [pre] + [reorder(lax.ppermute(pre, "store", over_store(k)), k) for k in range(1, count)]

    terms = pl.pallas_call(
        functools.partial(second_kernel, count, slots),
        out_shape=[jax.ShapeDtypeStruct((rows, width), F32)] * count,
        in_specs=[whole(SMEM), whole(SMEM)] + [whole(VMEM)] * (count + 3),
        out_specs=[whole(VMEM)] * count,
        scratch_shapes=[VMEM((count * rows, total), BF16), VMEM((count, rows, width), F32)],
        compiler_params=pltpu.CompilerParams(vmem_limit_bytes=40 * 2**20),
        name="second_dot",
    )(me, union_ids, ids, bias_in.reshape(-1, BLOCK), *parts, wout)

    def home(k):
        return [(s * count + t, (t ^ k) * count + s) for s in range(count) for t in range(count)]

    summed = sum(lax.ppermute(terms[k], ("store", "tensor"), home(k)) for k in range(count))
    return (summed + bias_out[None, :]).astype(BF16)


def general(states, weight_in, bias_in, weight_out, bias_out, block_lists, union_blocks):
    slice_width = weight_in.shape[0]
    union_ids = union_blocks[0]
    union_count = union_ids.shape[0]
    block_count = weight_in.shape[1] // BLOCK
    slot_count = block_lists.shape[2]
    own_rows = states.shape[0]
    sliced_states = lax.all_to_all(states, "store", split_axis=1, concat_axis=0, tiled=True)
    all_ids = lax.all_gather(block_lists, "store", axis=0, tiled=True)[:, 0, :]
    union_range = jnp.arange(union_count, dtype=jnp.int32)
    all_match = all_ids[:, :, None] == union_ids[None, None, :]
    all_keep = jnp.any(all_match, axis=-1)
    slot_pos = jnp.sum(jnp.where(all_match, union_range[None, None, :], 0), axis=-1)
    weight_in_union = jnp.take(
        weight_in.reshape(slice_width, block_count, BLOCK), union_ids, axis=1
    ).reshape(slice_width, union_count * BLOCK)
    weight_out_union = jnp.take(
        weight_out.reshape(block_count, BLOCK, slice_width), union_ids, axis=0
    ).reshape(union_count * BLOCK, slice_width)
    bias_blocks = bias_in.reshape(block_count, BLOCK)
    dense_pre = jnp.dot(sliced_states, weight_in_union, preferred_element_type=F32).reshape(
        own_rows * lax.axis_size("store"), union_count, BLOCK
    )
    picked = jnp.take_along_axis(dense_pre, slot_pos[:, :, None], axis=1)
    pre_act = lax.psum_scatter(
        (picked * all_keep[:, :, None].astype(F32)).reshape(
            own_rows * lax.axis_size("store"), slot_count * BLOCK
        ),
        "store",
        scatter_dimension=0,
        tiled=True,
    )
    own_ids = block_lists[:, 0, :]
    own_keep = jnp.any(own_ids[:, :, None] == union_ids[None, None, :], axis=-1)
    bias_rows = jnp.take(bias_blocks, jnp.maximum(own_ids, 0), axis=0).reshape(
        own_ids.shape[0], slot_count * BLOCK
    )
    active_mask = jnp.repeat(own_keep.astype(F32), BLOCK, axis=1)
    hidden = (jnp.maximum(pre_act + bias_rows, 0.0) * active_mask).astype(BF16)
    project_hidden = lax.all_gather(hidden, "store", axis=0, tiled=True)
    one_hot = jnp.logical_and(
        slot_pos[:, :, None] == union_range[None, None, :], all_keep[:, :, None]
    ).astype(BF16)
    spread = jnp.einsum(
        "rku,rkn->run",
        one_hot,
        project_hidden.reshape(-1, slot_count, BLOCK),
        preferred_element_type=F32,
    ).astype(BF16)
    partial_value = jnp.dot(
        spread.reshape(-1, union_count * BLOCK), weight_out_union, preferred_element_type=F32
    )
    row_terms = lax.all_to_all(partial_value, "store", split_axis=0, concat_axis=1, tiled=True)
    summed = lax.psum_scatter(row_terms, "tensor", scatter_dimension=1, tiled=True)
    return (summed + bias_out[None, :]).astype(BF16)


def solution(mesh):
    count = mesh.shape["store"]
    square = count == mesh.shape["tensor"] and count & (count - 1) == 0
    return jax.shard_map(
        fast if square else general,
        mesh=mesh,
        in_specs=(
            P(("groups", "store"), None),
            P("store", "tensor"),
            P("tensor"),
            P("tensor", "store"),
            P("tensor"),
            P(("groups", "store"), "tensor", None),
            P(("groups", "tensor"), None),
        ),
        out_specs=P(("groups", "store"), "tensor"),
        check_vma=False,
    )
```

time: 213 us -> 48.4 us (0.23)
  the two profiles are of different devices: /device:TPU:0 before, /device:TPU:21 now
where the time goes in v1:
time: 48.4 us; the launch traced here: 48.2 us
  starting transfers between devices  17.2 us (36%)
  waiting for transfers between devices  11.2 us (23%)
  Pallas kernels  10.9 us (23%)
  local copies, waits for them, and re-layouts  7.48 us (15%)
  other arithmetic  1.27 us (3%)
    ppermute x4, starting transfers between devices, fast(): lax.ppermute(terms[k], ('store', 'tensor'), home(k))  10.2 us
    ppermute x4, waiting for transfers between devices, fast(): lax.ppermute(terms[k], ('store', 'tensor'), home(k))  8.02 us
    unnamed x16, local copies, waits for them, and re-layouts  6.1 us
    pallas_call x1, Pallas kernels, fast(): pl.pallas_call(gather_kernel, out_shape=[VMEM((width, total), BF16), VMEM...  5.6 us
    ppermute x3, starting transfers between devices, fast(): lax.ppermute(pre, 'store', over_store(k))  4.34 us
    ppermute x3, waiting for transfers between devices, fast(): lax.ppermute(pre, 'store', over_store(k))  3.17 us
    ppermute x3, starting transfers between devices, fast(): lax.ppermute(chunks[k], 'store', over_store(k))  2.65 us
    pallas_call x1, Pallas kernels, fast(): pl.pallas_call(functools.partial(second_kernel, count, slots), out_shape=...  1.84 us
  transfers between devices with their start and end apart: 10, of which 5 were waited for; matrix products, arithmetic and copies ran while one was open for 0% of the time, Pallas kernels for 12%

profile of v1, /device:TPU:21, one launch (start us, length us, event | category | flops | bytes accessed | tf_op | source)
XLA Modules:
  0.0 48.2 jit_solution(164972168596741896)
XLA Ops:
  0.0 1.4 %copy.8.ids_ref = s32[16,4]{1,0:T(8,128)} copy(s32[16,4]{0,1:T(4,128)} %bitcast.9) | data formatting | bytes 512 | tf_op jit(solution)/shard_map/squeeze | solution.py:125
  1.4 0.6 %pad_add_fusion.me_ref = s32[2]{0:T(128)} fusion(s32[1]{0:T(128)} %bitcast.1, s32[1]{0:T(128)} %bitcast), kind=kLoop, calls=%fused_computation.4 | loop fusion | flops 2 | bytes 16 | tf_op jit(solution)/shard_map/stack | solution.py:116
  2.0 1.7 %split_states.1 = (bf16[16,1664]{1,0:T(8,128)(2,1)}, bf16[16,1664]{1,0:T(8,128)(2,1)}, bf16[16,1664]{1,0:T(8,128)(2,1)}, bf16[16,1664]{1,0:T(8,128)(2,1)}) custom-call(s32[2]{0:T(128)} %pad_add_fusion.me_ref, bf16[16,6144]{1,0:T(8,128)(2,1)} %states_ref.1, s32[16,4]{1,0:T(8,128)} %copy.8.ids_ref), custom_call_target="tpu_custom_call" | custom-call | tf_op jit(solution)/shard_map/split_states/pallas_call | solution.py:119
  3.6 1.3 %collective-permute-start = (bf16[16,1664]{1,0:T(8,128)(2,1)}, bf16[16,1664]{1,0:T(8,128)(2,1)S(1)}, u32[]{:S(2)}, u32[]{:S(2)}) collective-permute-start(bf16[16,1664]{1,0:T(8,128)(2,1)} %get-tuple-element.18), channel_id=1, source_target_pairs={{0,4},{4,0},{8,12},{12,8},{1,5},{5,1},{9,13},{13,9},{2,6},{6,2},{1... | collective-permute-start | bytes 159752 | tf_op jit(solution)/shard_map/ppermute | solution.py:130
  4.9 0.1 collective-permute-start.1
  5.0 1.3 %collective-permute-start.2 = (bf16[16,1664]{1,0:T(8,128)(2,1)}, bf16[16,1664]{1,0:T(8,128)(2,1)S(1)}, u32[]{:S(2)}, u32[]{:S(2)}) collective-permute-start(bf16[16,1664]{1,0:T(8,128)(2,1)} %get-tuple-element.20), channel_id=1, source_target_pairs={{0,12},{4,8},{8,4},{12,0},{1,13},{5,9},{9,5},{13,1},{2,14},{6,10},... | collective-permute-start | bytes 159752 | tf_op jit(solution)/shard_map/ppermute | solution.py:130
  6.3 0.0 copy-start.4
  6.3 0.7 %copy-done.4 = s32[1,16]{1,0:T(1,128)S(1)} copy-done((s32[1,16]{1,0:T(1,128)S(1)}, s32[1,16]{1,0:T(1,128)}, u32[]{:S(2)}) %copy-start.4) | copy-done | bytes 88
  6.9 0.0 copy-start.2
  6.9 0.0 copy-start.3
  6.9 0.0 copy-start.5
  6.9 0.0 copy-start.6
  6.9 0.0 copy-start.7
  6.9 5.6 %gather_weights.1 = (bf16[1536,2048]{1,0:T(8,128)(2,1)S(1)}, bf16[2048,1536]{1,0:T(8,128)(2,1)S(1)}) custom-call(s32[16]{0:T(128)S(1)} %bitcast.6, bf16[1536,6144]{1,0:T(8,128)(2,1)} %win_ref.1, bf16[6144,1536]{1,0:T(8,128)(2,1)} %wout_ref.1), custom_call_target="tpu_custom_call" | custom-call | bytes 12582912 | tf_op jit(solution)/shard_map/gather_weights/pallas_call | solution.py:132
  12.6 0.0 copy-start
  12.6 2.6 %copy-done = bf16[2048,1536]{1,0:T(8,128)(2,1)} copy-done((bf16[2048,1536]{1,0:T(8,128)(2,1)}, bf16[2048,1536]{1,0:T(8,128)(2,1)S(1)}, u32[]{:S(2)}) %copy-start) | copy-done | bytes 6291480
  15.2 0.0 collective-permute-done.refs_1_
  15.2 0.0 collective-permute-done.1.refs_2_
  15.2 0.0 collective-permute-done.2.refs_3_
  15.2 0.0 copy-done.2
  15.2 1.8 %first_dot.1 = (bf16[64,512]{1,0:T(8,128)(2,1)S(1)}, f32[64,128]{1,0:T(8,128)S(1)}) custom-call(s32[16]{0:T(128)S(1)} %bitcast.7, bf16[16,1664]{1,0:T(8,128)(2,1)S(1)} %copy-done.2, bf16[16,1664]{1,0:T(8,128)(2,1)S(1)} %collective-permute-done.refs_1_, bf16[16,1664]{1,0:T(8,128)(2,1)S(1)} %collective-permute-done.1.refs_2_, ...), custom_call_target="tpu_custom_call" | custom-call | tf_op jit(solution)/shard_map/first_dot/pallas_call | solution.py:143
  17.1 0.2 collective-permute-start.5
  17.3 4.1 %collective-permute-start.4 = (bf16[64,512]{1,0:T(8,128)(2,1)S(1)}, bf16[64,512]{1,0:T(8,128)(2,1)S(1)}, u32[]{:S(2)}, u32[]{:S(2)}) collective-permute-start(bf16[64,512]{1,0:T(8,128)(2,1)S(1)} %get-tuple-element.23.refs_0_), channel_id=1, source_target_pairs={{0,8},{4,12},{8,0},{12,4},{1,9},{5,13},{9,1},{13,5},{2,10},{6,14},... | collective-permute-start | bytes 196616 | tf_op jit(solution)/shard_map/ppermute | solution.py:160
  21.4 0.0 collective-permute-start.3
  21.4 0.0 collective-permute-done.5
  21.4 2.4 %collective-permute-done.4 = bf16[64,512]{1,0:T(8,128)(2,1)S(1)} collective-permute-done((bf16[64,512]{1,0:T(8,128)(2,1)S(1)}, bf16[64,512]{1,0:T(8,128)(2,1)S(1)}, u32[]{:S(2)}, u32[]{:S(2)}) %collective-permute-start.4) | collective-permute-done | bytes 65568 | tf_op jit(solution)/shard_map/ppermute | solution.py:160
  23.9 0.7 %collective-permute-done.3 = bf16[64,512]{1,0:T(8,128)(2,1)S(1)} collective-permute-done((bf16[64,512]{1,0:T(8,128)(2,1)S(1)}, bf16[64,512]{1,0:T(8,128)(2,1)S(1)}, u32[]{:S(2)}, u32[]{:S(2)}) %collective-permute-start.3) | collective-permute-done | bytes 65568 | tf_op jit(solution)/shard_map/ppermute | solution.py:160
  24.6 0.0 copy-done.3
  24.6 0.0 copy-done.5
  24.7 0.0 copy-done.6
  24.7 0.0 copy-start.1
  24.7 2.8 %copy-done.1 = bf16[2048,1536]{1,0:T(8,128)(2,1)S(1)} copy-done((bf16[2048,1536]{1,0:T(8,128)(2,1)S(1)}, bf16[2048,1536]{1,0:T(8,128)(2,1)}, u32[]{:S(2)}) %copy-start.1) | copy-done | bytes 6291480
  27.5 1.8 %second_dot.1 = (f32[16,1536]{1,0:T(8,128)S(1)}, f32[16,1536]{1,0:T(8,128)S(1)}, f32[16,1536]{1,0:T(8,128)S(1)}, f32[16,1536]{1,0:T(8,128)S(1)}) custom-call(s32[2]{0:T(128)S(1)} %copy-done.6, s32[16]{0:T(128)S(1)} %bitcast.8, f32[64,128]{1,0:T(8,128)S(1)} %get-tuple-element.22.ids_ref, f32[48,128]{1,0:T(8,128)S(1)} %bitcast.5, ...), custom_call_target="tpu_custom_call" | custom-call | tf_op jit(solution)/shard_map/second_dot/pallas_call | solution.py:162
  29.3 5.7 %collective-permute-start.6 = (f32[16,1536]{1,0:T(8,128)S(1)}, f32[16,1536]{1,0:T(8,128)S(1)}, u32[]{:S(2)}, u32[]{:S(2)}) collective-permute-start(f32[16,1536]{1,0:T(8,128)S(1)} %get-tuple-element.25), channel_id=1, source_target_pairs={{0,0},{1,4},{2,8},{3,12},{4,1},{5,5},{6,9},{7,13},{8,2},{9,6},{10,... | collective-permute-start | bytes 294920 | tf_op jit(solution)/shard_map/ppermute | solution.py:175
  35.0 2.8 %collective-permute-start.7 = (f32[16,1536]{1,0:T(8,128)S(1)}, f32[16,1536]{1,0:T(8,128)S(1)}, u32[]{:S(2)}, u32[]{:S(2)}) collective-permute-start(f32[16,1536]{1,0:T(8,128)S(1)} %get-tuple-element.26), channel_id=1, source_target_pairs={{0,4},{1,0},{2,12},{3,8},{4,5},{5,1},{6,13},{7,9},{8,6},{9,2},{10,... | collective-permute-start | bytes 294920 | tf_op jit(solution)/shard_map/ppermute | solution.py:175
  37.8 0.0 collective-permute-start.8
  37.8 1.7 %collective-permute-start.9 = (f32[16,1536]{1,0:T(8,128)S(1)}, f32[16,1536]{1,0:T(8,128)S(1)}, u32[]{:S(2)}, u32[]{:S(2)}) collective-permute-start(f32[16,1536]{1,0:T(8,128)S(1)} %get-tuple-element.28), channel_id=1, source_target_pairs={{0,12},{1,8},{2,4},{3,0},{4,13},{5,9},{6,5},{7,1},{8,14},{9,10},{1... | collective-permute-start | bytes 294920 | tf_op jit(solution)/shard_map/ppermute | solution.py:175
  39.5 0.0 collective-permute-done.6
  39.6 4.3 %collective-permute-done.7 = f32[16,1536]{1,0:T(8,128)S(1)} collective-permute-done((f32[16,1536]{1,0:T(8,128)S(1)}, f32[16,1536]{1,0:T(8,128)S(1)}, u32[]{:S(2)}, u32[]{:S(2)}) %collective-permute-start.7) | collective-permute-done | bytes 98336 | tf_op jit(solution)/shard_map/ppermute | solution.py:175
  43.9 1.5 %collective-permute-done.8 = f32[16,1536]{1,0:T(8,128)S(1)} collective-permute-done((f32[16,1536]{1,0:T(8,128)S(1)}, f32[16,1536]{1,0:T(8,128)S(1)}, u32[]{:S(2)}, u32[]{:S(2)}) %collective-permute-start.8) | collective-permute-done | bytes 98336 | tf_op jit(solution)/shard_map/ppermute | solution.py:175
  45.4 2.1 %collective-permute-done.9 = f32[16,1536]{1,0:T(8,128)S(1)} collective-permute-done((f32[16,1536]{1,0:T(8,128)S(1)}, f32[16,1536]{1,0:T(8,128)S(1)}, u32[]{:S(2)}, u32[]{:S(2)}) %collective-permute-start.9) | collective-permute-done | bytes 98336 | tf_op jit(solution)/shard_map/ppermute | solution.py:175
  47.6 0.0 copy-done.7
  47.6 0.6 %add_convert_fusion = bf16[16,1536]{1,0:T(8,128)(2,1)} fusion(f32[16,1536]{1,0:T(8,128)S(1)} %collective-permute-done.9, f32[16,1536]{1,0:T(8,128)S(1)} %collective-permute-done.8, f32[16,1536]{1,0:T(8,128)S(1)} %collective-permute-done.6, f32[16,1536]{1,0:T(8,128)S(1)} %collective-permute-done.7, f32[1536]{0:T(1024)S(1)} %copy-done.7), kind=kLoop, calls=%fused_computation | loop fusion | flops 122880 | bytes 448512 | tf_op jit(solution)/shard_map/convert_element_type | solution.py:176
  (5 shorter events, 0.0 us)
Async XLA Ops:
  3.6 11.6 %collective-permute-start = (bf16[16,1664]{1,0:T(8,128)(2,1)}, bf16[16,1664]{1,0:T(8,128)(2,1)S(1)}, u32[]{:S(2)}, u32[]{:S(2)}) collective-permute-start(bf16[16,1664]{1,0:T(8,128)(2,1)} %get-tuple-element.18), channel_id=1, source_target_pairs={{0,4},{4,0},{8,12},{12,8},{1,5},{5,1},{9,13},{13,9},{2,6},{6,2},{1... | collective-permute-start | bytes 159752 | tf_op jit(solution)/shard_map/ppermute | solution.py:130
  4.9 10.3 %collective-permute-start.1 = (bf16[16,1664]{1,0:T(8,128)(2,1)}, bf16[16,1664]{1,0:T(8,128)(2,1)S(1)}, u32[]{:S(2)}, u32[]{:S(2)}) collective-permute-start(bf16[16,1664]{1,0:T(8,128)(2,1)} %get-tuple-element.19), channel_id=1, source_target_pairs={{0,8},{4,12},{8,0},{12,4},{1,9},{5,13},{9,1},{13,5},{2,10},{6,14},... | collective-permute-start | bytes 159752 | tf_op jit(solution)/shard_map/ppermute | solution.py:130
  5.0 10.2 %collective-permute-start.2 = (bf16[16,1664]{1,0:T(8,128)(2,1)}, bf16[16,1664]{1,0:T(8,128)(2,1)S(1)}, u32[]{:S(2)}, u32[]{:S(2)}) collective-permute-start(bf16[16,1664]{1,0:T(8,128)(2,1)} %get-tuple-element.20), channel_id=1, source_target_pairs={{0,12},{4,8},{8,4},{12,0},{1,13},{5,9},{9,5},{13,1},{2,14},{6,10},... | collective-permute-start | bytes 159752 | tf_op jit(solution)/shard_map/ppermute | solution.py:130
  6.3 0.7 %copy-start.4 = (s32[1,16]{1,0:T(1,128)S(1)}, s32[1,16]{1,0:T(1,128)}, u32[]{:S(2)}) copy-start(s32[1,16]{1,0:T(1,128)} %param.13) | copy-start | bytes 196
  6.9 8.3 %copy-start.2 = (bf16[16,1664]{1,0:T(8,128)(2,1)S(1)}, bf16[16,1664]{1,0:T(8,128)(2,1)}, u32[]{:S(2)}) copy-start(bf16[16,1664]{1,0:T(8,128)(2,1)} %get-tuple-element.17.refs_0_) | copy-start | bytes 159748
  6.9 17.7 %copy-start.3 = (f32[6144]{0:T(1024)S(1)}, f32[6144]{0:T(1024)}, u32[]{:S(2)}) copy-start(f32[6144]{0:T(1024)} %param.9) | copy-start | bytes 73732
  6.9 17.7 %copy-start.5 = (s32[1,16]{1,0:T(1,128)S(1)}, s32[1,16]{1,0:T(1,128)}, u32[]{:S(2)}) copy-start(s32[1,16]{1,0:T(1,128)} %param.13) | copy-start | bytes 196
  6.9 17.7 %copy-start.6 = (s32[2]{0:T(128)S(1)}, s32[2]{0:T(128)}, u32[]{:S(2)}) copy-start(s32[2]{0:T(128)} %pad_add_fusion.me_ref) | copy-start | bytes 28
  6.9 40.6 %copy-start.7 = (f32[1536]{0:T(1024)S(1)}, f32[1536]{0:T(1024)}, u32[]{:S(2)}) copy-start(f32[1536]{0:T(1024)} %param.11) | copy-start | bytes 18436
  12.6 2.7 %copy-start = (bf16[2048,1536]{1,0:T(8,128)(2,1)}, bf16[2048,1536]{1,0:T(8,128)(2,1)S(1)}, u32[]{:S(2)}) copy-start(bf16[2048,1536]{1,0:T(8,128)(2,1)S(1)} %get-tuple-element.24.refs_4_) | copy-start | bytes 18874372
  17.1 4.3 %collective-permute-start.5 = (bf16[64,512]{1,0:T(8,128)(2,1)S(1)}, bf16[64,512]{1,0:T(8,128)(2,1)S(1)}, u32[]{:S(2)}, u32[]{:S(2)}) collective-permute-start(bf16[64,512]{1,0:T(8,128)(2,1)S(1)} %get-tuple-element.23.refs_0_), channel_id=1, source_target_pairs={{0,12},{4,8},{8,4},{12,0},{1,13},{5,9},{9,5},{13,1},{2,14},{6,10},... | collective-permute-start | bytes 196616 | tf_op jit(solution)/shard_map/ppermute | solution.py:160
  17.3 6.6 %collective-permute-start.4 = (bf16[64,512]{1,0:T(8,128)(2,1)S(1)}, bf16[64,512]{1,0:T(8,128)(2,1)S(1)}, u32[]{:S(2)}, u32[]{:S(2)}) collective-permute-start(bf16[64,512]{1,0:T(8,128)(2,1)S(1)} %get-tuple-element.23.refs_0_), channel_id=1, source_target_pairs={{0,8},{4,12},{8,0},{12,4},{1,9},{5,13},{9,1},{13,5},{2,10},{6,14},... | collective-permute-start | bytes 196616 | tf_op jit(solution)/shard_map/ppermute | solution.py:160
  21.4 3.2 %collective-permute-start.3 = (bf16[64,512]{1,0:T(8,128)(2,1)S(1)}, bf16[64,512]{1,0:T(8,128)(2,1)S(1)}, u32[]{:S(2)}, u32[]{:S(2)}) collective-permute-start(bf16[64,512]{1,0:T(8,128)(2,1)S(1)} %get-tuple-element.23.refs_0_), channel_id=1, source_target_pairs={{0,4},{4,0},{8,12},{12,8},{1,5},{5,1},{9,13},{13,9},{2,6},{6,2},{1... | collective-permute-start | bytes 196616 | tf_op jit(solution)/shard_map/ppermute | solution.py:160
  24.7 2.8 %copy-start.1 = (bf16[2048,1536]{1,0:T(8,128)(2,1)S(1)}, bf16[2048,1536]{1,0:T(8,128)(2,1)}, u32[]{:S(2)}) copy-start(bf16[2048,1536]{1,0:T(8,128)(2,1)} %copy-done) | copy-start | bytes 18874372
  29.3 10.3 %collective-permute-start.6 = (f32[16,1536]{1,0:T(8,128)S(1)}, f32[16,1536]{1,0:T(8,128)S(1)}, u32[]{:S(2)}, u32[]{:S(2)}) collective-permute-start(f32[16,1536]{1,0:T(8,128)S(1)} %get-tuple-element.25), channel_id=1, source_target_pairs={{0,0},{1,4},{2,8},{3,12},{4,1},{5,5},{6,9},{7,13},{8,2},{9,6},{10,... | collective-permute-start | bytes 294920 | tf_op jit(solution)/shard_map/ppermute | solution.py:175
  35.0 8.9 %collective-permute-start.7 = (f32[16,1536]{1,0:T(8,128)S(1)}, f32[16,1536]{1,0:T(8,128)S(1)}, u32[]{:S(2)}, u32[]{:S(2)}) collective-permute-start(f32[16,1536]{1,0:T(8,128)S(1)} %get-tuple-element.26), channel_id=1, source_target_pairs={{0,4},{1,0},{2,12},{3,8},{4,5},{5,1},{6,13},{7,9},{8,6},{9,2},{10,... | collective-permute-start | bytes 294920 | tf_op jit(solution)/shard_map/ppermute | solution.py:175
  37.8 7.6 %collective-permute-start.8 = (f32[16,1536]{1,0:T(8,128)S(1)}, f32[16,1536]{1,0:T(8,128)S(1)}, u32[]{:S(2)}, u32[]{:S(2)}) collective-permute-start(f32[16,1536]{1,0:T(8,128)S(1)} %get-tuple-element.27), channel_id=1, source_target_pairs={{0,8},{1,12},{2,0},{3,4},{4,9},{5,13},{6,1},{7,5},{8,10},{9,14},{1... | collective-permute-start | bytes 294920 | tf_op jit(solution)/shard_map/ppermute | solution.py:175
  37.8 9.7 %collective-permute-start.9 = (f32[16,1536]{1,0:T(8,128)S(1)}, f32[16,1536]{1,0:T(8,128)S(1)}, u32[]{:S(2)}, u32[]{:S(2)}) collective-permute-start(f32[16,1536]{1,0:T(8,128)S(1)} %get-tuple-element.28), channel_id=1, source_target_pairs={{0,12},{1,8},{2,4},{3,0},{4,13},{5,9},{6,5},{7,1},{8,14},{9,10},{1... | collective-permute-start | bytes 294920 | tf_op jit(solution)/shard_map/ppermute | solution.py:175

commit v2 on v1

--- a/solution.py
+++ b/solution.py
@@ -18,36 +18,57 @@
     return pl.BlockSpec(memory_space=space)
 
 
-def split_kernel(count, width, me_ref, states_ref, ids_ref, *out_refs):
-    me = me_ref[0]
-    slots = ids_ref.shape[1]
+def split_kernel(count, width, states_ref, ids_ref, *refs):
+    out_refs, sems = refs[:count], refs[count]
+    me = lax.axis_index("store")
+    copies = []
     for k in range(count):
         start = pl.multiple_of((me ^ k) * width, BLOCK)
-        out_refs[k][:, :width] = states_ref[:, pl.ds(start, width)]
-        out_refs[k][:, width:] = jnp.zeros((states_ref.shape[0], BLOCK), BF16)
-        out_refs[k][:, width : width + slots] = ids_ref[...].astype(F32).astype(BF16)
-
-
-def gather_kernel(union_ref, win_ref, wout_ref, win_out, wout_out, sems):
-    union = union_ref.shape[0]
-    for u in range(union):
-        start = pl.multiple_of(union_ref[u] * BLOCK, BLOCK)
-        pltpu.make_async_copy(
-            win_ref.at[:, pl.ds(start, BLOCK)], win_out.at[:, pl.ds(u * BLOCK, BLOCK)], sems.at[0, u]
-        ).start()
-    for u in range(union):
-        start = pl.multiple_of(union_ref[u] * BLOCK, BLOCK)
-        pltpu.make_async_copy(
-            wout_ref.at[pl.ds(start, BLOCK), :], wout_out.at[pl.ds(u * BLOCK, BLOCK), :], sems.at[1, u]
-        ).start()
-    for u in range(union):
-        start = pl.multiple_of(union_ref[u] * BLOCK, BLOCK)
-        pltpu.make_async_copy(
-            win_ref.at[:, pl.ds(start, BLOCK)], win_out.at[:, pl.ds(u * BLOCK, BLOCK)], sems.at[0, u]
-        ).wait()
-        pltpu.make_async_copy(
-            wout_ref.at[pl.ds(start, BLOCK), :], wout_out.at[pl.ds(u * BLOCK, BLOCK), :], sems.at[1, u]
-        ).wait()
+        copies.append(
+            pltpu.make_async_copy(
+                states_ref.at[:, pl.ds(start, width)], out_refs[k].at[:, :width], sems.at[k]
+            )
+        )
+    for k in list(range(1, count)) + [0]:
+        copies[k].start()
+    slots, rows = ids_ref.shape
+    ids = ids_ref[...].astype(F32)
+    padded = jnp.concatenate([ids, jnp.full((BLOCK - slots, rows), -1.0, F32)], axis=0)
+    tail = padded.T.astype(BF16)
+    for k in range(count):
+        out_refs[k][:, width:] = tail
+    for k in range(count):
+        copies[k].wait()
+
+
+def gather_kernel(by_column, union_ref, weight_ref, out_ref, sems):
+    copies = []
+    for u in range(union_ref.shape[0]):
+        block = pl.ds(pl.multiple_of(union_ref[u] * BLOCK, BLOCK), BLOCK)
+        place = pl.ds(u * BLOCK, BLOCK)
+        if by_column:
+            source, target = weight_ref.at[:, block], out_ref.at[:, place]
+        else:
+            source, target = weight_ref.at[block, :], out_ref.at[place, :]
+        copies.append(pltpu.make_async_copy(source, target, sems.at[u]))
+        copies[-1].start()
+    for copy in copies:
+        copy.wait()
+
+
+def gather(by_column, union_ids, weight, name):
+    union = union_ids.shape[0]
+    shape = (weight.shape[0], union * BLOCK) if by_column else (union * BLOCK, weight.shape[1])
+    return pl.pallas_call(
+        functools.partial(gather_kernel, by_column),
+        out_shape=VMEM(shape, BF16),
+        in_specs=[whole(SMEM), whole(pltpu.HBM)],
+        out_specs=whole(VMEM),
+        scratch_shapes=[pltpu.SemaphoreType.DMA((union,))],
+        compiler_params=pltpu.CompilerParams(vmem_limit_bytes=40 * 2**20),
+        cost_estimate=pl.CostEstimate(flops=0, bytes_accessed=4 * shape[0] * shape[1], transcendentals=0),
+        name=name,
+    )(union_ids, weight)
 
 
 def first_kernel(count, slots, union_ref, *refs):
@@ -73,12 +94,12 @@
             pre_ref[part, k * BLOCK : (k + 1) * BLOCK] = picked.astype(pre_ref.dtype)
 
 
-def second_kernel(count, slots, me_ref, union_ref, ids_ref, bias_ref, *refs):
+def second_kernel(count, slots, union_ref, ids_ref, bias_ref, *refs):
     part_refs = refs[:count]
     wout_ref = refs[count]
     out_refs = refs[count + 1 : 2 * count + 1]
     spread, terms = refs[2 * count + 1 :]
-    store, tensor = me_ref[0], me_ref[1]
+    store, tensor = lax.axis_index("store"), lax.axis_index("tensor")
     rows = ids_ref.shape[0] // count
     union = union_ref.shape[0]
     ids = ids_ref[...]
@@ -113,32 +134,23 @@
     slots = block_lists.shape[2]
     union_ids = union_blocks[0]
     union = union_ids.shape[0]
-    me = jnp.stack([lax.axis_index("store"), lax.axis_index("tensor")]).astype(jnp.int32)
     total = union * BLOCK
 
     chunks = pl.pallas_call(
         functools.partial(split_kernel, count, width),
         out_shape=[jax.ShapeDtypeStruct((rows, width + BLOCK), BF16)] * count,
-        in_specs=[whole(SMEM), whole(VMEM), whole(VMEM)],
+        in_specs=[whole(pltpu.HBM), whole(VMEM)],
         out_specs=[whole(VMEM)] * count,
+        scratch_shapes=[pltpu.SemaphoreType.DMA((count,))],
         name="split_states",
-    )(me, states, block_lists[:, 0, :])
+    )(states, jnp.transpose(block_lists, (1, 2, 0))[0])
 
     def over_store(k):
         return [(i, i ^ k) for i in range(count)]
 
     got = [chunks[0]] + [lax.ppermute(chunks[k], "store", over_store(k)) for k in range(1, count)]
 
-    win, wout = pl.pallas_call(
-        gather_kernel,
-        out_shape=[VMEM((width, total), BF16), VMEM((total, width), BF16)],
-        in_specs=[whole(SMEM), whole(pl.ANY), whole(pl.ANY)],
-        out_specs=[whole(VMEM), whole(VMEM)],
-        scratch_shapes=[pltpu.SemaphoreType.DMA((2, union))],
-        compiler_params=pltpu.CompilerParams(vmem_limit_bytes=40 * 2**20),
-        cost_estimate=pl.CostEstimate(flops=0, bytes_accessed=4 * width * total, transcendentals=0),
-        name="gather_weights",
-    )(union_ids, weight_in, weight_out)
+    win = gather(True, union_ids, weight_in, "gather_in")
 
     pre, ids = pl.pallas_call(
         functools.partial(first_kernel, count, slots),
@@ -159,20 +171,22 @@
 
     parts = [pre] + [reorder(lax.ppermute(pre, "store", over_store(k)), k) for k in range(1, count)]
 
+    wout = gather(False, union_ids, weight_out, "gather_out")
+
     terms = pl.pallas_call(
         functools.partial(second_kernel, count, slots),
-        out_shape=[jax.ShapeDtypeStruct((rows, width), F32)] * count,
-        in_specs=[whole(SMEM), whole(SMEM)] + [whole(VMEM)] * (count + 3),
+        out_shape=[jax.ShapeDtypeStruct((rows, width), BF16)] * count,
+        in_specs=[whole(SMEM)] + [whole(VMEM)] * (count + 3),
         out_specs=[whole(VMEM)] * count,
         scratch_shapes=[VMEM((count * rows, total), BF16), VMEM((count, rows, width), F32)],
         compiler_params=pltpu.CompilerParams(vmem_limit_bytes=40 * 2**20),
         name="second_dot",
-    )(me, union_ids, ids, bias_in.reshape(-1, BLOCK), *parts, wout)
+    )(union_ids, ids, bias_in.reshape(-1, BLOCK), *parts, wout)
 
     def home(k):
         return [(s * count + t, (t ^ k) * count + s) for s in range(count) for t in range(count)]
 
-    summed = sum(lax.ppermute(terms[k], ("store", "tensor"), home(k)) for k in range(count))
+    summed = sum(lax.ppermute(terms[k], ("store", "tensor"), home(k)).astype(F32) for k in range(count))
     return (summed + bias_out[None, :]).astype(BF16)
 
 

time: 48.4 us -> 40 us (0.83)
  the two profiles are of different devices: /device:TPU:21 before, /device:TPU:3 now
where the time goes in v2:
time: 40 us; the launch traced here: 39.5 us
  starting transfers between devices  16.4 us (41%)
  Pallas kernels  13.1 us (33%)
  waiting for transfers between devices  8.44 us (21%)
  local copies, waits for them, and re-layouts  0.69 us (2%)
  other arithmetic  0.68 us (2%)
    ppermute x4, starting transfers between devices, fast(): lax.ppermute(terms[k], ('store', 'tensor'), home(k)).astype(F32)  9.08 us
    pallas_call x2, Pallas kernels, gather(): pl.pallas_call(functools.partial(gather_kernel, by_column), out_shape=VME...  7.09 us
    ppermute x4, waiting for transfers between devices, fast(): lax.ppermute(terms[k], ('store', 'tensor'), home(k)).astype(F32)  4.69 us
    ppermute x3, starting transfers between devices, fast(): lax.ppermute(chunks[k], 'store', over_store(k))  3.67 us
    ppermute x3, starting transfers between devices, fast(): lax.ppermute(pre, 'store', over_store(k))  3.67 us
    ppermute x3, waiting for transfers between devices, fast(): lax.ppermute(pre, 'store', over_store(k))  3.01 us
    pallas_call x1, Pallas kernels, fast(): pl.pallas_call(functools.partial(split_kernel, count, width), out_shape=[...  2.29 us
    pallas_call x1, Pallas kernels, fast(): pl.pallas_call(functools.partial(second_kernel, count, slots), out_shape=...  1.89 us
  transfers between devices with their start and end apart: 10, of which 4 were waited for; matrix products, arithmetic and copies ran while one was open for 0% of the time, Pallas kernels for 18%

profile of v2, /device:TPU:3, one launch (start us, length us, event | category | flops | bytes accessed | tf_op | source)
XLA Modules:
  0.0 39.5 jit_solution(18335526028722900627)
XLA Ops:
  0.0 2.3 %split_states.1 = (bf16[16,1664]{1,0:T(8,128)(2,1)}, bf16[16,1664]{1,0:T(8,128)(2,1)}, bf16[16,1664]{1,0:T(8,128)(2,1)}, bf16[16,1664]{1,0:T(8,128)(2,1)}) custom-call(bf16[16,6144]{1,0:T(8,128)(2,1)} %states_ref.1, s32[4,16]{1,0:T(4,128)} %bitcast.10), custom_call_target="tpu_custom_call" | custom-call | tf_op jit(solution)/shard_map/split_states/pallas_call | solution.py:139
  2.3 0.0 copy-start
  2.3 1.4 %collective-permute-start = (bf16[16,1664]{1,0:T(8,128)(2,1)}, bf16[16,1664]{1,0:T(8,128)(2,1)S(1)}, u32[]{:S(2)}, u32[]{:S(2)}) collective-permute-start(bf16[16,1664]{1,0:T(8,128)(2,1)} %get-tuple-element.16), channel_id=1, source_target_pairs={{0,4},{4,0},{8,12},{12,8},{1,5},{5,1},{9,13},{13,9},{2,6},{6,2},{1... | collective-permute-start | bytes 159752 | tf_op jit(solution)/shard_map/ppermute | solution.py:151
  3.7 2.3 %collective-permute-start.1 = (bf16[16,1664]{1,0:T(8,128)(2,1)}, bf16[16,1664]{1,0:T(8,128)(2,1)S(1)}, u32[]{:S(2)}, u32[]{:S(2)}) collective-permute-start(bf16[16,1664]{1,0:T(8,128)(2,1)} %get-tuple-element.17), channel_id=1, source_target_pairs={{0,8},{4,12},{8,0},{12,4},{1,9},{5,13},{9,1},{13,5},{2,10},{6,14},... | collective-permute-start | bytes 159752 | tf_op jit(solution)/shard_map/ppermute | solution.py:151
  6.0 0.0 collective-permute-start.2
  6.0 0.0 copy-start.2
  6.0 0.7 %copy-done.2 = s32[1,16]{1,0:T(1,128)S(1)} copy-done((s32[1,16]{1,0:T(1,128)S(1)}, s32[1,16]{1,0:T(1,128)}, u32[]{:S(2)}) %copy-start.2) | copy-done | bytes 88
  6.6 3.6 %gather_in.1.refs_4_ = bf16[1536,2048]{1,0:T(8,128)(2,1)S(1)} custom-call(s32[16]{0:T(128)S(1)} %bitcast.6, bf16[1536,6144]{1,0:T(8,128)(2,1)} %weight_ref.2), custom_call_target="tpu_custom_call" | custom-call | bytes 12582912 | tf_op jit(solution)/shard_map/gather_in/pallas_call | solution.py:62
  10.3 0.0 copy-start.1
  10.3 0.0 copy-start.3
  10.3 0.0 collective-permute-done.refs_1_
  10.3 0.0 collective-permute-done.1.refs_2_
  10.3 0.7 %collective-permute-done.2.refs_3_ = bf16[16,1664]{1,0:T(8,128)(2,1)S(1)} collective-permute-done((bf16[16,1664]{1,0:T(8,128)(2,1)}, bf16[16,1664]{1,0:T(8,128)(2,1)S(1)}, u32[]{:S(2)}, u32[]{:S(2)}) %collective-permute-start.2) | collective-permute-done | bytes 53280 | tf_op jit(solution)/shard_map/ppermute | solution.py:151
  11.1 0.0 copy-done
  11.1 0.0 copy-start.4
  11.1 1.8 %first_dot.1 = (bf16[64,512]{1,0:T(8,128)(2,1)S(1)}, f32[64,128]{1,0:T(8,128)S(1)}) custom-call(s32[16]{0:T(128)S(1)} %bitcast.7, bf16[16,1664]{1,0:T(8,128)(2,1)S(1)} %copy-done, bf16[16,1664]{1,0:T(8,128)(2,1)S(1)} %collective-permute-done.refs_1_, bf16[16,1664]{1,0:T(8,128)(2,1)S(1)} %collective-permute-done.1.refs_2_, ...), custom_call_target="tpu_custom_call" | custom-call | tf_op jit(solution)/shard_map/first_dot/pallas_call | solution.py:155
  12.9 2.6 %collective-permute-start.5 = (bf16[64,512]{1,0:T(8,128)(2,1)S(1)}, bf16[64,512]{1,0:T(8,128)(2,1)S(1)}, u32[]{:S(2)}, u32[]{:S(2)}) collective-permute-start(bf16[64,512]{1,0:T(8,128)(2,1)S(1)} %get-tuple-element.20.refs_0_), channel_id=1, source_target_pairs={{0,12},{4,8},{8,4},{12,0},{1,13},{5,9},{9,5},{13,1},{2,14},{6,10},... | collective-permute-start | bytes 196616 | tf_op jit(solution)/shard_map/ppermute | solution.py:172
  15.5 3.5 %gather_out.1.refs_4_ = bf16[2048,1536]{1,0:T(8,128)(2,1)S(1)} custom-call(s32[16]{0:T(128)S(1)} %bitcast.8, bf16[6144,1536]{1,0:T(8,128)(2,1)} %weight_ref.3), custom_call_target="tpu_custom_call" | custom-call | bytes 12582912 | tf_op jit(solution)/shard_map/gather_out/pallas_call | solution.py:62
  19.0 0.1 collective-permute-start.4
  19.1 1.0 %collective-permute-start.3 = (bf16[64,512]{1,0:T(8,128)(2,1)S(1)}, bf16[64,512]{1,0:T(8,128)(2,1)S(1)}, u32[]{:S(2)}, u32[]{:S(2)}) collective-permute-start(bf16[64,512]{1,0:T(8,128)(2,1)S(1)} %get-tuple-element.20.refs_0_), channel_id=1, source_target_pairs={{0,4},{4,0},{8,12},{12,8},{1,5},{5,1},{9,13},{13,9},{2,6},{6,2},{1... | collective-permute-start | bytes 196616 | tf_op jit(solution)/shard_map/ppermute | solution.py:172
  20.1 0.0 collective-permute-done.5
  20.1 3.0 %collective-permute-done.4 = bf16[64,512]{1,0:T(8,128)(2,1)S(1)} collective-permute-done((bf16[64,512]{1,0:T(8,128)(2,1)S(1)}, bf16[64,512]{1,0:T(8,128)(2,1)S(1)}, u32[]{:S(2)}, u32[]{:S(2)}) %collective-permute-start.4) | collective-permute-done | bytes 65568 | tf_op jit(solution)/shard_map/ppermute | solution.py:172
  23.1 0.0 collective-permute-done.3
  23.1 0.0 copy-done.1
  23.2 0.0 copy-done.3
  23.2 1.9 %second_dot.1 = (bf16[16,1536]{1,0:T(8,128)(2,1)S(1)}, bf16[16,1536]{1,0:T(8,128)(2,1)S(1)}, bf16[16,1536]{1,0:T(8,128)(2,1)S(1)}, bf16[16,1536]{1,0:T(8,128)(2,1)S(1)}) custom-call(s32[16]{0:T(128)S(1)} %bitcast.9, f32[64,128]{1,0:T(8,128)S(1)} %get-tuple-element.19.ids_ref, f32[48,128]{1,0:T(8,128)S(1)} %bitcast.5, ...), custom_call_target="tpu_custom_call" | custom-call | tf_op jit(solution)/shard_map/second_dot/pallas_call | solution.py:176
  25.1 6.6 %collective-permute-start.6 = (bf16[16,1536]{1,0:T(8,128)(2,1)S(1)}, bf16[16,1536]{1,0:T(8,128)(2,1)S(1)}, u32[]{:S(2)}, u32[]{:S(2)}) collective-permute-start(bf16[16,1536]{1,0:T(8,128)(2,1)S(1)} %get-tuple-element.21), channel_id=1, source_target_pairs={{0,0},{1,4},{2,8},{3,12},{4,1},{5,5},{6,9},{7,13},{8,2},{9,6},{10,... | collective-permute-start | bytes 147464 | tf_op jit(solution)/shard_map/ppermute | solution.py:189
  31.6 1.9 %collective-permute-start.7 = (bf16[16,1536]{1,0:T(8,128)(2,1)S(1)}, bf16[16,1536]{1,0:T(8,128)(2,1)S(1)}, u32[]{:S(2)}, u32[]{:S(2)}) collective-permute-start(bf16[16,1536]{1,0:T(8,128)(2,1)S(1)} %get-tuple-element.22), channel_id=1, source_target_pairs={{0,4},{1,0},{2,12},{3,8},{4,5},{5,1},{6,13},{7,9},{8,6},{9,2},{10,... | collective-permute-start | bytes 147464 | tf_op jit(solution)/shard_map/ppermute | solution.py:189
  33.5 0.0 collective-permute-start.8
  33.5 0.6 %collective-permute-start.9 = (bf16[16,1536]{1,0:T(8,128)(2,1)S(1)}, bf16[16,1536]{1,0:T(8,128)(2,1)S(1)}, u32[]{:S(2)}, u32[]{:S(2)}) collective-permute-start(bf16[16,1536]{1,0:T(8,128)(2,1)S(1)} %get-tuple-element.24), channel_id=1, source_target_pairs={{0,12},{1,8},{2,4},{3,0},{4,13},{5,9},{6,5},{7,1},{8,14},{9,10},{1... | collective-permute-start | bytes 147464 | tf_op jit(solution)/shard_map/ppermute | solution.py:189
  34.2 0.0 collective-permute-done.6
  34.2 3.2 %collective-permute-done.7 = bf16[16,1536]{1,0:T(8,128)(2,1)S(1)} collective-permute-done((bf16[16,1536]{1,0:T(8,128)(2,1)S(1)}, bf16[16,1536]{1,0:T(8,128)(2,1)S(1)}, u32[]{:S(2)}, u32[]{:S(2)}) %collective-permute-start.7) | collective-permute-done | bytes 49184 | tf_op jit(solution)/shard_map/ppermute | solution.py:189
  37.3 1.5 %collective-permute-done.8 = bf16[16,1536]{1,0:T(8,128)(2,1)S(1)} collective-permute-done((bf16[16,1536]{1,0:T(8,128)(2,1)S(1)}, bf16[16,1536]{1,0:T(8,128)(2,1)S(1)}, u32[]{:S(2)}, u32[]{:S(2)}) %collective-permute-start.8) | collective-permute-done | bytes 49184 | tf_op jit(solution)/shard_map/ppermute | solution.py:189
  38.8 0.0 collective-permute-done.9
  38.8 0.0 copy-done.4
  38.8 0.7 %add_convert_fusion = bf16[16,1536]{1,0:T(8,128)(2,1)} fusion(bf16[16,1536]{1,0:T(8,128)(2,1)S(1)} %collective-permute-done.9, bf16[16,1536]{1,0:T(8,128)(2,1)S(1)} %collective-permute-done.8, bf16[16,1536]{1,0:T(8,128)(2,1)S(1)} %collective-permute-done.7, bf16[16,1536]{1,0:T(8,128)(2,1)S(1)} %collective-permute-done.6, f32[1536]{0:T(1024)S(1)} %copy-done.4), kind=kLoop, calls=%fused_computation | loop fusion | flops 221184 | bytes 251904 | tf_op jit(solution)/shard_map/convert_element_type | solution.py:190
  (5 shorter events, 0.0 us)
Async XLA Ops:
  2.3 8.8 %copy-start = (bf16[16,1664]{1,0:T(8,128)(2,1)S(1)}, bf16[16,1664]{1,0:T(8,128)(2,1)}, u32[]{:S(2)}) copy-start(bf16[16,1664]{1,0:T(8,128)(2,1)} %get-tuple-element.15.refs_0_) | copy-start | bytes 159748
  2.3 8.0 %collective-permute-start = (bf16[16,1664]{1,0:T(8,128)(2,1)}, bf16[16,1664]{1,0:T(8,128)(2,1)S(1)}, u32[]{:S(2)}, u32[]{:S(2)}) collective-permute-start(bf16[16,1664]{1,0:T(8,128)(2,1)} %get-tuple-element.16), channel_id=1, source_target_pairs={{0,4},{4,0},{8,12},{12,8},{1,5},{5,1},{9,13},{13,9},{2,6},{6,2},{1... | collective-permute-start | bytes 159752 | tf_op jit(solution)/shard_map/ppermute | solution.py:151
  3.7 6.7 %collective-permute-start.1 = (bf16[16,1664]{1,0:T(8,128)(2,1)}, bf16[16,1664]{1,0:T(8,128)(2,1)S(1)}, u32[]{:S(2)}, u32[]{:S(2)}) collective-permute-start(bf16[16,1664]{1,0:T(8,128)(2,1)} %get-tuple-element.17), channel_id=1, source_target_pairs={{0,8},{4,12},{8,0},{12,4},{1,9},{5,13},{9,1},{13,5},{2,10},{6,14},... | collective-permute-start | bytes 159752 | tf_op jit(solution)/shard_map/ppermute | solution.py:151
  6.0 5.1 %collective-permute-start.2 = (bf16[16,1664]{1,0:T(8,128)(2,1)}, bf16[16,1664]{1,0:T(8,128)(2,1)S(1)}, u32[]{:S(2)}, u32[]{:S(2)}) collective-permute-start(bf16[16,1664]{1,0:T(8,128)(2,1)} %get-tuple-element.18), channel_id=1, source_target_pairs={{0,12},{4,8},{8,4},{12,0},{1,13},{5,9},{9,5},{13,1},{2,14},{6,10},... | collective-permute-start | bytes 159752 | tf_op jit(solution)/shard_map/ppermute | solution.py:151
  6.0 0.7 %copy-start.2 = (s32[1,16]{1,0:T(1,128)S(1)}, s32[1,16]{1,0:T(1,128)}, u32[]{:S(2)}) copy-start(s32[1,16]{1,0:T(1,128)} %param.13) | copy-start | bytes 196
  10.3 12.9 %copy-start.1 = (f32[6144]{0:T(1024)S(1)}, f32[6144]{0:T(1024)}, u32[]{:S(2)}) copy-start(f32[6144]{0:T(1024)} %param.9) | copy-start | bytes 73732
  10.3 12.9 %copy-start.3 = (s32[1,16]{1,0:T(1,128)S(1)}, s32[1,16]{1,0:T(1,128)}, u32[]{:S(2)}) copy-start(s32[1,16]{1,0:T(1,128)} %param.13) | copy-start | bytes 196
  11.1 27.8 %copy-start.4 = (f32[1536]{0:T(1024)S(1)}, f32[1536]{0:T(1024)}, u32[]{:S(2)}) copy-start(f32[1536]{0:T(1024)} %param.11) | copy-start | bytes 18436
  12.9 7.1 %collective-permute-start.5 = (bf16[64,512]{1,0:T(8,128)(2,1)S(1)}, bf16[64,512]{1,0:T(8,128)(2,1)S(1)}, u32[]{:S(2)}, u32[]{:S(2)}) collective-permute-start(bf16[64,512]{1,0:T(8,128)(2,1)S(1)} %get-tuple-element.20.refs_0_), channel_id=1, source_target_pairs={{0,12},{4,8},{8,4},{12,0},{1,13},{5,9},{9,5},{13,1},{2,14},{6,10},... | collective-permute-start | bytes 196616 | tf_op jit(solution)/shard_map/ppermute | solution.py:172
  19.0 4.1 %collective-permute-start.4 = (bf16[64,512]{1,0:T(8,128)(2,1)S(1)}, bf16[64,512]{1,0:T(8,128)(2,1)S(1)}, u32[]{:S(2)}, u32[]{:S(2)}) collective-permute-start(bf16[64,512]{1,0:T(8,128)(2,1)S(1)} %get-tuple-element.20.refs_0_), channel_id=1, source_target_pairs={{0,8},{4,12},{8,0},{12,4},{1,9},{5,13},{9,1},{13,5},{2,10},{6,14},... | collective-permute-start | bytes 196616 | tf_op jit(solution)/shard_map/ppermute | solution.py:172
  19.1 4.0 %collective-permute-start.3 = (bf16[64,512]{1,0:T(8,128)(2,1)S(1)}, bf16[64,512]{1,0:T(8,128)(2,1)S(1)}, u32[]{:S(2)}, u32[]{:S(2)}) collective-permute-start(bf16[64,512]{1,0:T(8,128)(2,1)S(1)} %get-tuple-element.20.refs_0_), channel_id=1, source_target_pairs={{0,4},{4,0},{8,12},{12,8},{1,5},{5,1},{9,13},{13,9},{2,6},{6,2},{1... | collective-permute-start | bytes 196616 | tf_op jit(solution)/shard_map/ppermute | solution.py:172
  25.1 9.1 %collective-permute-start.6 = (bf16[16,1536]{1,0:T(8,128)(2,1)S(1)}, bf16[16,1536]{1,0:T(8,128)(2,1)S(1)}, u32[]{:S(2)}, u32[]{:S(2)}) collective-permute-start(bf16[16,1536]{1,0:T(8,128)(2,1)S(1)} %get-tuple-element.21), channel_id=1, source_target_pairs={{0,0},{1,4},{2,8},{3,12},{4,1},{5,5},{6,9},{7,13},{8,2},{9,6},{10,... | collective-permute-start | bytes 147464 | tf_op jit(solution)/shard_map/ppermute | solution.py:189
  31.6 5.7 %collective-permute-start.7 = (bf16[16,1536]{1,0:T(8,128)(2,1)S(1)}, bf16[16,1536]{1,0:T(8,128)(2,1)S(1)}, u32[]{:S(2)}, u32[]{:S(2)}) collective-permute-start(bf16[16,1536]{1,0:T(8,128)(2,1)S(1)} %get-tuple-element.22), channel_id=1, source_target_pairs={{0,4},{1,0},{2,12},{3,8},{4,5},{5,1},{6,13},{7,9},{8,6},{9,2},{10,... | collective-permute-start | bytes 147464 | tf_op jit(solution)/shard_map/ppermute | solution.py:189
  33.5 5.3 %collective-permute-start.8 = (bf16[16,1536]{1,0:T(8,128)(2,1)S(1)}, bf16[16,1536]{1,0:T(8,128)(2,1)S(1)}, u32[]{:S(2)}, u32[]{:S(2)}) collective-permute-start(bf16[16,1536]{1,0:T(8,128)(2,1)S(1)} %get-tuple-element.23), channel_id=1, source_target_pairs={{0,8},{1,12},{2,0},{3,4},{4,9},{5,13},{6,1},{7,5},{8,10},{9,14},{1... | collective-permute-start | bytes 147464 | tf_op jit(solution)/shard_map/ppermute | solution.py:189
  33.5 5.3 %collective-permute-start.9 = (bf16[16,1536]{1,0:T(8,128)(2,1)S(1)}, bf16[16,1536]{1,0:T(8,128)(2,1)S(1)}, u32[]{:S(2)}, u32[]{:S(2)}) collective-permute-start(bf16[16,1536]{1,0:T(8,128)(2,1)S(1)} %get-tuple-element.24), channel_id=1, source_target_pairs={{0,12},{1,8},{2,4},{3,0},{4,13},{5,9},{6,5},{7,1},{8,14},{9,10},{1... | collective-permute-start | bytes 147464 | tf_op jit(solution)/shard_map/ppermute | solution.py:189

commit v3 on v2

--- a/solution.py
+++ b/solution.py
@@ -18,27 +18,32 @@
     return pl.BlockSpec(memory_space=space)
 
 
-def split_kernel(count, width, states_ref, ids_ref, *refs):
-    out_refs, sems = refs[:count], refs[count]
+def split_kernel(count, width, states_ref, ids_ref, union_ref, *refs):
+    out_refs, union_out, ids, sems = refs[:count], refs[count], refs[count + 1], refs[count + 2]
     me = lax.axis_index("store")
+    ids_copy = pltpu.make_async_copy(ids_ref, ids, sems.at[count])
+    ids_copy.start()
     copies = []
-    for k in range(count):
+    for k in list(range(1, count)) + [0]:
         start = pl.multiple_of((me ^ k) * width, BLOCK)
         copies.append(
             pltpu.make_async_copy(
                 states_ref.at[:, pl.ds(start, width)], out_refs[k].at[:, :width], sems.at[k]
             )
         )
-    for k in list(range(1, count)) + [0]:
-        copies[k].start()
+        copies[-1].start()
+    copies.append(pltpu.make_async_copy(union_ref, union_out, sems.at[count + 1]))
+    copies[-1].start()
     slots, rows = ids_ref.shape
-    ids = ids_ref[...].astype(F32)
-    padded = jnp.concatenate([ids, jnp.full((BLOCK - slots, rows), -1.0, F32)], axis=0)
+    ids_copy.wait()
+    padded = jnp.concatenate(
+        [ids[...].astype(F32), jnp.full((BLOCK - slots, rows), -1.0, F32)], axis=0
+    )
     tail = padded.T.astype(BF16)
     for k in range(count):
         out_refs[k][:, width:] = tail
-    for k in range(count):
-        copies[k].wait()
+    for copy in copies:
+        copy.wait()
 
 
 def gather_kernel(by_column, union_ref, weight_ref, out_ref, sems):
@@ -109,7 +114,12 @@
         pres = []
         for k in range(slots):
             cols = slice(k * BLOCK, (k + 1) * BLOCK)
-            pres.append(sum(p[part, cols].astype(F32) for p in part_refs))
+            pres.append(
+                sum(
+                    p[(j ^ i) * rows : ((j ^ i) + 1) * rows, cols].astype(F32)
+                    for i, p in enumerate(part_refs)
+                )
+            )
         for u in range(union):
             block = union_ref[u].astype(F32)
             value = jnp.zeros((rows, BLOCK), F32)
@@ -132,18 +142,19 @@
     width = weight_in.shape[0]
     rows = states.shape[0]
     slots = block_lists.shape[2]
-    union_ids = union_blocks[0]
-    union = union_ids.shape[0]
+    union = union_blocks.shape[1]
     total = union * BLOCK
 
-    chunks = pl.pallas_call(
+    *chunks, union_ids = pl.pallas_call(
         functools.partial(split_kernel, count, width),
-        out_shape=[jax.ShapeDtypeStruct((rows, width + BLOCK), BF16)] * count,
-        in_specs=[whole(pltpu.HBM), whole(VMEM)],
-        out_specs=[whole(VMEM)] * count,
-        scratch_shapes=[pltpu.SemaphoreType.DMA((count,))],
+        out_shape=[jax.ShapeDtypeStruct((rows, width + BLOCK), BF16)] * count
+        + [jax.ShapeDtypeStruct(union_blocks.shape, jnp.int32)],
+        in_specs=[whole(pltpu.HBM)] * 3,
+        out_specs=[whole(VMEM)] * (count + 1),
+        scratch_shapes=[VMEM((slots, rows), jnp.int32), pltpu.SemaphoreType.DMA((count + 2,))],
         name="split_states",
-    )(states, jnp.transpose(block_lists, (1, 2, 0))[0])
+    )(states, jnp.transpose(block_lists, (1, 2, 0))[0], union_blocks)
+    union_ids = union_ids[0]
 
     def over_store(k):
         return [(i, i ^ k) for i in range(count)]
@@ -165,11 +176,7 @@
         name="first_dot",
     )(union_ids, *got, win)
 
-    def reorder(a, k):
-        blocks = a.reshape(count, rows, a.shape[1])
-        return jnp.concatenate([blocks[j ^ k] for j in range(count)], axis=0)
-
-    parts = [pre] + [reorder(lax.ppermute(pre, "store", over_store(k)), k) for k in range(1, count)]
+    parts = [pre] + [lax.ppermute(pre, "store", over_store(k)) for k in range(1, count)]
 
     wout = gather(False, union_ids, weight_out, "gather_out")
 

time: 40 us -> 36.8 us (0.920)
  waiting for transfers between devices: 8.44 us -> 6.54 us
  Pallas kernels: 13.1 us -> 12.5 us
    ppermute x3, waiting for transfers between devices: 3.01 us -> 1.09 us  [fast(): lax.ppermute(pre, 'store', over_store(k))]
    pallas_call x1, Pallas kernels: 2.29 us -> 1.63 us  [fast(): pl.pallas_call(functools.partial(split_kernel, count, width), out_shape=[...]
  transfers between devices with their start and end apart: 10 -> 10, of which waited for: 4 -> 4; matrix products, arithmetic and copies ran while one was open for 0% -> 0% of each run, Pallas kernels for 18% -> 19%
where the time goes in v3:
time: 36.8 us; the launch traced here: 36.6 us
  starting transfers between devices  16.1 us (44%)
  Pallas kernels  12.5 us (34%)
  waiting for transfers between devices  6.54 us (18%)
  local copies, waits for them, and re-layouts  0.67 us (2%)
  other arithmetic  0.65 us (2%)
    ppermute x4, starting transfers between devices, fast(): lax.ppermute(terms[k], ('store', 'tensor'), home(k)).astype(F32)  8.87 us
    pallas_call x2, Pallas kernels, gather(): pl.pallas_call(functools.partial(gather_kernel, by_column), out_shape=VME...  7.09 us
    ppermute x4, waiting for transfers between devices, fast(): lax.ppermute(terms[k], ('store', 'tensor'), home(k)).astype(F32)  4.69 us
    ppermute x3, starting transfers between devices, fast(): lax.ppermute(chunks[k], 'store', over_store(k))  3.67 us
    ppermute x3, starting transfers between devices, fast(): lax.ppermute(pre, 'store', over_store(k))  3.6 us
    pallas_call x1, Pallas kernels, fast(): pl.pallas_call(functools.partial(second_kernel, count, slots), out_shape=...  1.89 us
    pallas_call x1, Pallas kernels, fast(): pl.pallas_call(functools.partial(first_kernel, count, slots), out_shape=[...  1.85 us
    pallas_call x1, Pallas kernels, fast(): pl.pallas_call(functools.partial(split_kernel, count, width), out_shape=[...  1.63 us
  transfers between devices with their start and end apart: 10, of which 4 were waited for; matrix products, arithmetic and copies ran while one was open for 0% of the time, Pallas kernels for 19%

profile of v3, /device:TPU:3, one launch (start us, length us, event | category | flops | bytes accessed | tf_op | source)
XLA Modules:
  0.0 36.6 jit_solution(1336009777994975915)
XLA Ops:
  0.0 1.6 %split_states.1 = (bf16[16,1664]{1,0:T(8,128)(2,1)}, bf16[16,1664]{1,0:T(8,128)(2,1)}, bf16[16,1664]{1,0:T(8,128)(2,1)}, bf16[16,1664]{1,0:T(8,128)(2,1)}, s32[1,16]{1,0:T(1,128)}) custom-call(bf16[16,6144]{1,0:T(8,128)(2,1)} %states_ref.1, s32[4,16]{1,0:T(4,128)} %bitcast.10, s32[1,16]{1,0:T(1,128)} %union_ref.1), custom_call_target="tpu_custom_call" | custom-call | tf_op jit(solution)/shard_map/split_states/pallas_call | solution.py:148
  1.6 0.0 copy-start
  1.6 1.4 %collective-permute-start = (bf16[16,1664]{1,0:T(8,128)(2,1)}, bf16[16,1664]{1,0:T(8,128)(2,1)S(1)}, u32[]{:S(2)}, u32[]{:S(2)}) collective-permute-start(bf16[16,1664]{1,0:T(8,128)(2,1)} %get-tuple-element.18), channel_id=1, source_target_pairs={{0,4},{4,0},{8,12},{12,8},{1,5},{5,1},{9,13},{13,9},{2,6},{6,2},{1... | collective-permute-start | bytes 159752 | tf_op jit(solution)/shard_map/ppermute | solution.py:162
  3.0 2.3 %collective-permute-start.1 = (bf16[16,1664]{1,0:T(8,128)(2,1)}, bf16[16,1664]{1,0:T(8,128)(2,1)S(1)}, u32[]{:S(2)}, u32[]{:S(2)}) collective-permute-start(bf16[16,1664]{1,0:T(8,128)(2,1)} %get-tuple-element.19), channel_id=1, source_target_pairs={{0,8},{4,12},{8,0},{12,4},{1,9},{5,13},{9,1},{13,5},{2,10},{6,14},... | collective-permute-start | bytes 159752 | tf_op jit(solution)/shard_map/ppermute | solution.py:162
  5.3 0.0 collective-permute-start.2
  5.3 0.0 copy-start.2
  5.3 0.7 %copy-done.2 = s32[1,16]{1,0:T(1,128)S(1)} copy-done((s32[1,16]{1,0:T(1,128)S(1)}, s32[1,16]{1,0:T(1,128)}, u32[]{:S(2)}) %copy-start.2) | copy-done | bytes 88
  6.0 0.0 copy-start.3
  6.0 3.6 %gather_in.1.refs_4_ = bf16[1536,2048]{1,0:T(8,128)(2,1)S(1)} custom-call(s32[16]{0:T(128)S(1)} %bitcast.6, bf16[1536,6144]{1,0:T(8,128)(2,1)} %weight_ref.2), custom_call_target="tpu_custom_call" | custom-call | bytes 12582912 | tf_op jit(solution)/shard_map/gather_in/pallas_call | solution.py:67
  9.6 0.0 copy-start.1
  9.6 0.0 collective-permute-done.refs_1_
  9.6 0.0 collective-permute-done.1.refs_2_
  9.7 0.8 %collective-permute-done.2.refs_3_ = bf16[16,1664]{1,0:T(8,128)(2,1)S(1)} collective-permute-done((bf16[16,1664]{1,0:T(8,128)(2,1)}, bf16[16,1664]{1,0:T(8,128)(2,1)S(1)}, u32[]{:S(2)}, u32[]{:S(2)}) %collective-permute-start.2) | collective-permute-done | bytes 53280 | tf_op jit(solution)/shard_map/ppermute | solution.py:162
  10.4 0.0 copy-done
  10.4 0.0 copy-done.3
  10.4 0.0 copy-start.4
  10.4 1.8 %first_dot.1 = (bf16[64,512]{1,0:T(8,128)(2,1)S(1)}, f32[64,128]{1,0:T(8,128)S(1)}) custom-call(s32[16]{0:T(128)S(1)} %bitcast.7, bf16[16,1664]{1,0:T(8,128)(2,1)S(1)} %copy-done, bf16[16,1664]{1,0:T(8,128)(2,1)S(1)} %collective-permute-done.refs_1_, bf16[16,1664]{1,0:T(8,128)(2,1)S(1)} %collective-permute-done.1.refs_2_, ...), custom_call_target="tpu_custom_call" | custom-call | tf_op jit(solution)/shard_map/first_dot/pallas_call | solution.py:166
  12.3 0.1 collective-permute-start.3
  12.4 2.8 %collective-permute-start.4 = (bf16[64,512]{1,0:T(8,128)(2,1)S(1)}, bf16[64,512]{1,0:T(8,128)(2,1)S(1)}, u32[]{:S(2)}, u32[]{:S(2)}) collective-permute-start(bf16[64,512]{1,0:T(8,128)(2,1)S(1)} %get-tuple-element.22.refs_0_), channel_id=1, source_target_pairs={{0,8},{4,12},{8,0},{12,4},{1,9},{5,13},{9,1},{13,5},{2,10},{6,14},... | collective-permute-start | bytes 196616 | tf_op jit(solution)/shard_map/ppermute | solution.py:179
  15.2 0.7 %collective-permute-start.5 = (bf16[64,512]{1,0:T(8,128)(2,1)S(1)}, bf16[64,512]{1,0:T(8,128)(2,1)S(1)}, u32[]{:S(2)}, u32[]{:S(2)}) collective-permute-start(bf16[64,512]{1,0:T(8,128)(2,1)S(1)} %get-tuple-element.22.refs_0_), channel_id=1, source_target_pairs={{0,12},{4,8},{8,4},{12,0},{1,13},{5,9},{9,5},{13,1},{2,14},{6,10},... | collective-permute-start | bytes 196616 | tf_op jit(solution)/shard_map/ppermute | solution.py:179
  15.9 3.5 %gather_out.1.refs_4_ = bf16[2048,1536]{1,0:T(8,128)(2,1)S(1)} custom-call(s32[16]{0:T(128)S(1)} %bitcast.8, bf16[6144,1536]{1,0:T(8,128)(2,1)} %weight_ref.3), custom_call_target="tpu_custom_call" | custom-call | bytes 12582912 | tf_op jit(solution)/shard_map/gather_out/pallas_call | solution.py:67
  19.4 0.0 collective-permute-done.3.refs_1_
  19.4 0.0 collective-permute-done.4.refs_2_
  19.4 1.1 %collective-permute-done.5.refs_3_ = bf16[64,512]{1,0:T(8,128)(2,1)S(1)} collective-permute-done((bf16[64,512]{1,0:T(8,128)(2,1)S(1)}, bf16[64,512]{1,0:T(8,128)(2,1)S(1)}, u32[]{:S(2)}, u32[]{:S(2)}) %collective-permute-start.5) | collective-permute-done | bytes 65568 | tf_op jit(solution)/shard_map/ppermute | solution.py:179
  20.5 0.0 copy-done.1
  20.5 1.9 %second_dot.1 = (bf16[16,1536]{1,0:T(8,128)(2,1)S(1)}, bf16[16,1536]{1,0:T(8,128)(2,1)S(1)}, bf16[16,1536]{1,0:T(8,128)(2,1)S(1)}, bf16[16,1536]{1,0:T(8,128)(2,1)S(1)}) custom-call(s32[16]{0:T(128)S(1)} %bitcast.9, f32[64,128]{1,0:T(8,128)S(1)} %get-tuple-element.21.ids_ref, f32[48,128]{1,0:T(8,128)S(1)} %bitcast.5, ...), custom_call_target="tpu_custom_call" | custom-call | tf_op jit(solution)/shard_map/second_dot/pallas_call | solution.py:183
  22.4 6.1 %collective-permute-start.6 = (bf16[16,1536]{1,0:T(8,128)(2,1)S(1)}, bf16[16,1536]{1,0:T(8,128)(2,1)S(1)}, u32[]{:S(2)}, u32[]{:S(2)}) collective-permute-start(bf16[16,1536]{1,0:T(8,128)(2,1)S(1)} %get-tuple-element.23), channel_id=1, source_target_pairs={{0,0},{1,4},{2,8},{3,12},{4,1},{5,5},{6,9},{7,13},{8,2},{9,6},{10,... | collective-permute-start | bytes 147464 | tf_op jit(solution)/shard_map/ppermute | solution.py:196
  28.5 2.1 %collective-permute-start.7 = (bf16[16,1536]{1,0:T(8,128)(2,1)S(1)}, bf16[16,1536]{1,0:T(8,128)(2,1)S(1)}, u32[]{:S(2)}, u32[]{:S(2)}) collective-permute-start(bf16[16,1536]{1,0:T(8,128)(2,1)S(1)} %get-tuple-element.24), channel_id=1, source_target_pairs={{0,4},{1,0},{2,12},{3,8},{4,5},{5,1},{6,13},{7,9},{8,6},{9,2},{10,... | collective-permute-start | bytes 147464 | tf_op jit(solution)/shard_map/ppermute | solution.py:196
  30.6 0.0 collective-permute-start.8
  30.6 0.6 %collective-permute-start.9 = (bf16[16,1536]{1,0:T(8,128)(2,1)S(1)}, bf16[16,1536]{1,0:T(8,128)(2,1)S(1)}, u32[]{:S(2)}, u32[]{:S(2)}) collective-permute-start(bf16[16,1536]{1,0:T(8,128)(2,1)S(1)} %get-tuple-element.26), channel_id=1, source_target_pairs={{0,12},{1,8},{2,4},{3,0},{4,13},{5,9},{6,5},{7,1},{8,14},{9,10},{1... | collective-permute-start | bytes 147464 | tf_op jit(solution)/shard_map/ppermute | solution.py:196
  31.2 0.0 collective-permute-done.6
  31.2 2.9 %collective-permute-done.7 = bf16[16,1536]{1,0:T(8,128)(2,1)S(1)} collective-permute-done((bf16[16,1536]{1,0:T(8,128)(2,1)S(1)}, bf16[16,1536]{1,0:T(8,128)(2,1)S(1)}, u32[]{:S(2)}, u32[]{:S(2)}) %collective-permute-start.7) | collective-permute-done | bytes 49184 | tf_op jit(solution)/shard_map/ppermute | solution.py:196
  34.2 1.8 %collective-permute-done.8 = bf16[16,1536]{1,0:T(8,128)(2,1)S(1)} collective-permute-done((bf16[16,1536]{1,0:T(8,128)(2,1)S(1)}, bf16[16,1536]{1,0:T(8,128)(2,1)S(1)}, u32[]{:S(2)}, u32[]{:S(2)}) %collective-permute-start.8) | collective-permute-done | bytes 49184 | tf_op jit(solution)/shard_map/ppermute | solution.py:196
  35.9 0.0 collective-permute-done.9
  35.9 0.0 copy-done.4
  35.9 0.7 %add_convert_fusion = bf16[16,1536]{1,0:T(8,128)(2,1)} fusion(bf16[16,1536]{1,0:T(8,128)(2,1)S(1)} %collective-permute-done.9, bf16[16,1536]{1,0:T(8,128)(2,1)S(1)} %collective-permute-done.8, bf16[16,1536]{1,0:T(8,128)(2,1)S(1)} %collective-permute-done.7, bf16[16,1536]{1,0:T(8,128)(2,1)S(1)} %collective-permute-done.6, f32[1536]{0:T(1024)S(1)} %copy-done.4), kind=kLoop, calls=%fused_computation | loop fusion | flops 221184 | bytes 251904 | tf_op jit(solution)/shard_map/convert_element_type | solution.py:197
Async XLA Ops:
  1.6 8.8 %copy-start = (bf16[16,1664]{1,0:T(8,128)(2,1)S(1)}, bf16[16,1664]{1,0:T(8,128)(2,1)}, u32[]{:S(2)}) copy-start(bf16[16,1664]{1,0:T(8,128)(2,1)} %get-tuple-element.17.refs_0_) | copy-start | bytes 159748
  1.6 8.0 %collective-permute-start = (bf16[16,1664]{1,0:T(8,128)(2,1)}, bf16[16,1664]{1,0:T(8,128)(2,1)S(1)}, u32[]{:S(2)}, u32[]{:S(2)}) collective-permute-start(bf16[16,1664]{1,0:T(8,128)(2,1)} %get-tuple-element.18), channel_id=1, source_target_pairs={{0,4},{4,0},{8,12},{12,8},{1,5},{5,1},{9,13},{13,9},{2,6},{6,2},{1... | collective-permute-start | bytes 159752 | tf_op jit(solution)/shard_map/ppermute | solution.py:162
  3.0 6.6 %collective-permute-start.1 = (bf16[16,1664]{1,0:T(8,128)(2,1)}, bf16[16,1664]{1,0:T(8,128)(2,1)S(1)}, u32[]{:S(2)}, u32[]{:S(2)}) collective-permute-start(bf16[16,1664]{1,0:T(8,128)(2,1)} %get-tuple-element.19), channel_id=1, source_target_pairs={{0,8},{4,12},{8,0},{12,4},{1,9},{5,13},{9,1},{13,5},{2,10},{6,14},... | collective-permute-start | bytes 159752 | tf_op jit(solution)/shard_map/ppermute | solution.py:162
  5.3 5.1 %collective-permute-start.2 = (bf16[16,1664]{1,0:T(8,128)(2,1)}, bf16[16,1664]{1,0:T(8,128)(2,1)S(1)}, u32[]{:S(2)}, u32[]{:S(2)}) collective-permute-start(bf16[16,1664]{1,0:T(8,128)(2,1)} %get-tuple-element.20), channel_id=1, source_target_pairs={{0,12},{4,8},{8,4},{12,0},{1,13},{5,9},{9,5},{13,1},{2,14},{6,10},... | collective-permute-start | bytes 159752 | tf_op jit(solution)/shard_map/ppermute | solution.py:162
  5.3 0.7 %copy-start.2 = (s32[1,16]{1,0:T(1,128)S(1)}, s32[1,16]{1,0:T(1,128)}, u32[]{:S(2)}) copy-start(s32[1,16]{1,0:T(1,128)} %get-tuple-element.16) | copy-start | bytes 196
  6.0 4.4 %copy-start.3 = (s32[1,16]{1,0:T(1,128)S(1)}, s32[1,16]{1,0:T(1,128)}, u32[]{:S(2)}) copy-start(s32[1,16]{1,0:T(1,128)} %get-tuple-element.16) | copy-start | bytes 196
  9.6 10.8 %copy-start.1 = (f32[6144]{0:T(1024)S(1)}, f32[6144]{0:T(1024)}, u32[]{:S(2)}) copy-start(f32[6144]{0:T(1024)} %param.9) | copy-start | bytes 73732
  10.4 25.5 %copy-start.4 = (f32[1536]{0:T(1024)S(1)}, f32[1536]{0:T(1024)}, u32[]{:S(2)}) copy-start(f32[1536]{0:T(1024)} %param.11) | copy-start | bytes 18436
  12.3 7.1 %collective-permute-start.3 = (bf16[64,512]{1,0:T(8,128)(2,1)S(1)}, bf16[64,512]{1,0:T(8,128)(2,1)S(1)}, u32[]{:S(2)}, u32[]{:S(2)}) collective-permute-start(bf16[64,512]{1,0:T(8,128)(2,1)S(1)} %get-tuple-element.22.refs_0_), channel_id=1, source_target_pairs={{0,4},{4,0},{8,12},{12,8},{1,5},{5,1},{9,13},{13,9},{2,6},{6,2},{1... | collective-permute-start | bytes 196616 | tf_op jit(solution)/shard_map/ppermute | solution.py:179
  12.4 7.0 %collective-permute-start.4 = (bf16[64,512]{1,0:T(8,128)(2,1)S(1)}, bf16[64,512]{1,0:T(8,128)(2,1)S(1)}, u32[]{:S(2)}, u32[]{:S(2)}) collective-permute-start(bf16[64,512]{1,0:T(8,128)(2,1)S(1)} %get-tuple-element.22.refs_0_), channel_id=1, source_target_pairs={{0,8},{4,12},{8,0},{12,4},{1,9},{5,13},{9,1},{13,5},{2,10},{6,14},... | collective-permute-start | bytes 196616 | tf_op jit(solution)/shard_map/ppermute | solution.py:179
  15.2 5.3 %collective-permute-start.5 = (bf16[64,512]{1,0:T(8,128)(2,1)S(1)}, bf16[64,512]{1,0:T(8,128)(2,1)S(1)}, u32[]{:S(2)}, u32[]{:S(2)}) collective-permute-start(bf16[64,512]{1,0:T(8,128)(2,1)S(1)} %get-tuple-element.22.refs_0_), channel_id=1, source_target_pairs={{0,12},{4,8},{8,4},{12,0},{1,13},{5,9},{9,5},{13,1},{2,14},{6,10},... | collective-permute-start | bytes 196616 | tf_op jit(solution)/shard_map/ppermute | solution.py:179
  22.4 8.9 %collective-permute-start.6 = (bf16[16,1536]{1,0:T(8,128)(2,1)S(1)}, bf16[16,1536]{1,0:T(8,128)(2,1)S(1)}, u32[]{:S(2)}, u32[]{:S(2)}) collective-permute-start(bf16[16,1536]{1,0:T(8,128)(2,1)S(1)} %get-tuple-element.23), channel_id=1, source_target_pairs={{0,0},{1,4},{2,8},{3,12},{4,1},{5,5},{6,9},{7,13},{8,2},{9,6},{10,... | collective-permute-start | bytes 147464 | tf_op jit(solution)/shard_map/ppermute | solution.py:196
  28.5 5.7 %collective-permute-start.7 = (bf16[16,1536]{1,0:T(8,128)(2,1)S(1)}, bf16[16,1536]{1,0:T(8,128)(2,1)S(1)}, u32[]{:S(2)}, u32[]{:S(2)}) collective-permute-start(bf16[16,1536]{1,0:T(8,128)(2,1)S(1)} %get-tuple-element.24), channel_id=1, source_target_pairs={{0,4},{1,0},{2,12},{3,8},{4,5},{5,1},{6,13},{7,9},{8,6},{9,2},{10,... | collective-permute-start | bytes 147464 | tf_op jit(solution)/shard_map/ppermute | solution.py:196
  30.6 5.3 %collective-permute-start.8 = (bf16[16,1536]{1,0:T(8,128)(2,1)S(1)}, bf16[16,1536]{1,0:T(8,128)(2,1)S(1)}, u32[]{:S(2)}, u32[]{:S(2)}) collective-permute-start(bf16[16,1536]{1,0:T(8,128)(2,1)S(1)} %get-tuple-element.25), channel_id=1, source_target_pairs={{0,8},{1,12},{2,0},{3,4},{4,9},{5,13},{6,1},{7,5},{8,10},{9,14},{1... | collective-permute-start | bytes 147464 | tf_op jit(solution)/shard_map/ppermute | solution.py:196
  30.6 5.3 %collective-permute-start.9 = (bf16[16,1536]{1,0:T(8,128)(2,1)S(1)}, bf16[16,1536]{1,0:T(8,128)(2,1)S(1)}, u32[]{:S(2)}, u32[]{:S(2)}) collective-permute-start(bf16[16,1536]{1,0:T(8,128)(2,1)S(1)} %get-tuple-element.26), channel_id=1, source_target_pairs={{0,12},{1,8},{2,4},{3,0},{4,13},{5,9},{6,5},{7,1},{8,14},{9,10},{1... | collective-permute-start | bytes 147464 | tf_op jit(solution)/shard_map/ppermute | solution.py:196

commit v4 on v3

--- a/solution.py
+++ b/solution.py
@@ -77,7 +77,7 @@
 
 
 def first_kernel(count, slots, union_ref, *refs):
-    chunk_refs = refs[:count]
+    chunk_refs = refs[:count][::-1]
     win_ref, pre_ref, ids_ref, dense = refs[count:]
     width, total = win_ref.shape
     rows = chunk_refs[0].shape[0]
@@ -100,10 +100,9 @@
 
 
 def second_kernel(count, slots, union_ref, ids_ref, bias_ref, *refs):
-    part_refs = refs[:count]
+    part_refs = refs[:count][::-1]
     wout_ref = refs[count]
-    out_refs = refs[count + 1 : 2 * count + 1]
-    spread, terms = refs[2 * count + 1 :]
+    keep_ref, send_ref, spread, terms = refs[count + 1 :]
     store, tensor = lax.axis_index("store"), lax.axis_index("tensor")
     rows = ids_ref.shape[0] // count
     union = union_ref.shape[0]
@@ -133,8 +132,11 @@
     for n in range(0, width, step):
         product = jnp.dot(hidden, wout_ref[:, n : n + step], preferred_element_type=F32)
         terms[:, :, n : n + step] = product.reshape(count, rows, step)
-    for k in range(count):
-        out_refs[k][...] = terms[store ^ tensor ^ k].astype(out_refs[k].dtype)
+    chip, core = tensor // 2, tensor % 2
+    for k in range(count // 2):
+        part = slice(k * rows, (k + 1) * rows)
+        keep_ref[part, :] = terms[store ^ (2 * core + (chip ^ k))]
+        send_ref[part, :] = terms[store ^ (2 * (1 - core) + (chip ^ k))]
 
 
 def fast(states, weight_in, bias_in, weight_out, bias_out, block_lists, union_blocks):
@@ -147,8 +149,7 @@
 
     *chunks, union_ids = pl.pallas_call(
         functools.partial(split_kernel, count, width),
-        out_shape=[jax.ShapeDtypeStruct((rows, width + BLOCK), BF16)] * count
-        + [jax.ShapeDtypeStruct(union_blocks.shape, jnp.int32)],
+        out_shape=[VMEM((rows, width + BLOCK), BF16)] * count + [VMEM(union_blocks.shape, jnp.int32)],
         in_specs=[whole(pltpu.HBM)] * 3,
         out_specs=[whole(VMEM)] * (count + 1),
         scratch_shapes=[VMEM((slots, rows), jnp.int32), pltpu.SemaphoreType.DMA((count + 2,))],
@@ -159,7 +160,9 @@
     def over_store(k):
         return [(i, i ^ k) for i in range(count)]
 
-    got = [chunks[0]] + [lax.ppermute(chunks[k], "store", over_store(k)) for k in range(1, count)]
+    far_first = list(range(count - 1, 0, -1))
+    got = {k: lax.ppermute(chunks[k], "store", over_store(k)) for k in far_first}
+    got = [got[k] for k in far_first] + [chunks[0]]
 
     win = gather(True, union_ids, weight_in, "gather_in")
 
@@ -176,24 +179,34 @@
         name="first_dot",
     )(union_ids, *got, win)
 
-    parts = [pre] + [lax.ppermute(pre, "store", over_store(k)) for k in range(1, count)]
+    parts = {k: lax.ppermute(pre, "store", over_store(k)) for k in far_first}
+    parts = [parts[k] for k in far_first] + [pre]
 
     wout = gather(False, union_ids, weight_out, "gather_out")
 
-    terms = pl.pallas_call(
+    keep, send = pl.pallas_call(
         functools.partial(second_kernel, count, slots),
-        out_shape=[jax.ShapeDtypeStruct((rows, width), BF16)] * count,
+        out_shape=[VMEM((count // 2 * rows, width), F32)] * 2,
         in_specs=[whole(SMEM)] + [whole(VMEM)] * (count + 3),
-        out_specs=[whole(VMEM)] * count,
+        out_specs=[whole(VMEM)] * 2,
         scratch_shapes=[VMEM((count * rows, total), BF16), VMEM((count, rows, width), F32)],
         compiler_params=pltpu.CompilerParams(vmem_limit_bytes=40 * 2**20),
         name="second_dot",
     )(union_ids, ids, bias_in.reshape(-1, BLOCK), *parts, wout)
 
+    pair = [(i, i ^ 1) for i in range(count)]
+    both = (keep + lax.ppermute(send, "tensor", pair)).astype(BF16)
+
     def home(k):
-        return [(s * count + t, (t ^ k) * count + s) for s in range(count) for t in range(count)]
-
-    summed = sum(lax.ppermute(terms[k], ("store", "tensor"), home(k)).astype(F32) for k in range(count))
+        return [
+            (z * count + 2 * x + c, (2 * c + (x ^ k)) * count + z)
+            for z in range(count) for x in range(count // 2) for c in range(2)
+        ]
+
+    summed = sum(
+        lax.ppermute(both[k * rows : (k + 1) * rows], ("store", "tensor"), home(k)).astype(F32)
+        for k in range(count // 2)
+    )
     return (summed + bias_out[None, :]).astype(BF16)
 
 

time: 36.8 us -> 34.3 us (0.932)
  starting transfers between devices: 16.1 us -> 15 us
  Pallas kernels: 12.5 us -> 11.8 us
  local copies, waits for them, and re-layouts: 0.67 us -> 0.02 us
    ppermute x7 -> x6, starting transfers between devices: 12.5 us -> 11.2 us  [the longest x2 5.77 us: fast(): lax.ppermute(both[k * rows:(k + 1) * rows], ('store', 'tensor'), home(k))]
    pallas_call x1, Pallas kernels: 1.63 us -> 0.94 us  [fast(): pl.pallas_call(functools.partial(split_kernel, count, width), out_shape=[...]
    unnamed x10 -> x4, local copies, waits for them, and re-layouts: 0.67 us -> 0.01 us
    ppermute x7 -> x6, waiting for transfers between devices: 5.78 us -> 6.18 us  [the longest x2 4 us: fast(): lax.ppermute(both[k * rows:(k + 1) * rows], ('store', 'tensor'), home(k))]
  transfers between devices with their start and end apart: 10 -> 9, of which waited for: 4 -> 5; matrix products, arithmetic and copies ran while one was open for 0% -> 0% of each run, Pallas kernels for 19% -> 21%
where the time goes in v4:
time: 34.3 us; the launch traced here: 34.1 us
  starting transfers between devices  15 us (44%)
  Pallas kernels  11.8 us (34%)
  waiting for transfers between devices  6.62 us (19%)
  other arithmetic  0.67 us (2%)
    pallas_call x2, Pallas kernels, gather(): pl.pallas_call(functools.partial(gather_kernel, by_column), out_shape=VME...  7.09 us
    ppermute x2, starting transfers between devices, fast(): lax.ppermute(both[k * rows:(k + 1) * rows], ('store', 'tensor'), home(k))  5.77 us
    ppermute x2, waiting for transfers between devices, fast(): lax.ppermute(both[k * rows:(k + 1) * rows], ('store', 'tensor'), home(k))  4 us
    ppermute x3, starting transfers between devices, fast(): lax.ppermute(chunks[k], 'store', over_store(k))  3.75 us
    ppermute x3, starting transfers between devices, fast(): parts = {k: lax.ppermute(pre, 'store', over_store(k)) for k in far_first}  3.61 us
    pallas_call x1, Pallas kernels, fast(): pl.pallas_call(functools.partial(second_kernel, count, slots), out_shape=...  1.89 us
    ppermute x1, starting transfers between devices, fast(): both = (keep + lax.ppermute(send, 'tensor', pair)).astype(BF16)  1.86 us
    pallas_call x1, Pallas kernels, fast(): pl.pallas_call(functools.partial(first_kernel, count, slots), out_shape=[...  1.84 us
  transfers between devices with their start and end apart: 9, of which 5 were waited for; matrix products, arithmetic and copies ran while one was open for 0% of the time, Pallas kernels for 21%

profile of v4, /device:TPU:3, one launch (start us, length us, event | category | flops | bytes accessed | tf_op | source)
XLA Modules:
  0.0 34.1 jit_solution(12775727602868194182)
XLA Ops:
  0.0 0.9 %split_states.1 = (bf16[16,1664]{1,0:T(8,128)(2,1)S(1)}, bf16[16,1664]{1,0:T(8,128)(2,1)S(1)}, bf16[16,1664]{1,0:T(8,128)(2,1)S(1)}, bf16[16,1664]{1,0:T(8,128)(2,1)S(1)}, s32[1,16]{1,0:T(1,128)S(1)}) custom-call(bf16[16,6144]{1,0:T(8,128)(2,1)} %states_ref.1, s32[4,16]{1,0:T(4,128)} %bitcast.10, s32[1,16]{1,0:T(1,128)} %union_ref.1), custom_call_target="tpu_custom_call" | custom-call | tf_op jit(solution)/shard_map/split_states/pallas_call | solution.py:150
  0.9 3.4 %collective-permute-start = (bf16[16,1664]{1,0:T(8,128)(2,1)S(1)}, bf16[16,1664]{1,0:T(8,128)(2,1)S(1)}, u32[]{:S(2)}, u32[]{:S(2)}) collective-permute-start(bf16[16,1664]{1,0:T(8,128)(2,1)S(1)} %get-tuple-element.15), channel_id=1, source_target_pairs={{0,12},{4,8},{8,4},{12,0},{1,13},{5,9},{9,5},{13,1},{2,14},{6,10},... | collective-permute-start | bytes 159752 | tf_op jit(solution)/shard_map/ppermute | solution.py:164
  4.3 0.0 collective-permute-start.1
  4.3 0.4 %collective-permute-start.2 = (bf16[16,1664]{1,0:T(8,128)(2,1)S(1)}, bf16[16,1664]{1,0:T(8,128)(2,1)S(1)}, u32[]{:S(2)}, u32[]{:S(2)}) collective-permute-start(bf16[16,1664]{1,0:T(8,128)(2,1)S(1)} %get-tuple-element.17), channel_id=1, source_target_pairs={{0,4},{4,0},{8,12},{12,8},{1,5},{5,1},{9,13},{13,9},{2,6},{6,2},{1... | collective-permute-start | bytes 159752 | tf_op jit(solution)/shard_map/ppermute | solution.py:164
  4.7 3.6 %gather_in.1.refs_4_ = bf16[1536,2048]{1,0:T(8,128)(2,1)S(1)} custom-call(s32[16]{0:T(128)S(1)} %bitcast.6, bf16[1536,6144]{1,0:T(8,128)(2,1)} %weight_ref.2), custom_call_target="tpu_custom_call" | custom-call | bytes 12582912 | tf_op jit(solution)/shard_map/gather_in/pallas_call | solution.py:67
  8.3 0.0 copy-start
  8.4 0.0 collective-permute-done.refs_0_
  8.4 0.4 %collective-permute-done.1.refs_1_ = bf16[16,1664]{1,0:T(8,128)(2,1)S(1)} collective-permute-done((bf16[16,1664]{1,0:T(8,128)(2,1)S(1)}, bf16[16,1664]{1,0:T(8,128)(2,1)S(1)}, u32[]{:S(2)}, u32[]{:S(2)}) %collective-permute-start.1) | collective-permute-done | bytes 53280 | tf_op jit(solution)/shard_map/ppermute | solution.py:164
  8.8 0.0 collective-permute-done.2.refs_2_
  8.8 0.0 copy-start.1
  8.8 1.8 %first_dot.1 = (bf16[64,512]{1,0:T(8,128)(2,1)S(1)}, f32[64,128]{1,0:T(8,128)S(1)}) custom-call(s32[16]{0:T(128)S(1)} %bitcast.7, bf16[16,1664]{1,0:T(8,128)(2,1)S(1)} %collective-permute-done.refs_0_, bf16[16,1664]{1,0:T(8,128)(2,1)S(1)} %collective-permute-done.1.refs_1_, bf16[16,1664]{1,0:T(8,128)(2,1)S(1)} %collective-permute-done.2.refs_2_, ...), custom_call_target="tpu_custom_call" | custom-call | tf_op jit(solution)/shard_map/first_dot/pallas_call | solution.py:169
  10.7 2.8 %collective-permute-start.3 = (bf16[64,512]{1,0:T(8,128)(2,1)S(1)}, bf16[64,512]{1,0:T(8,128)(2,1)S(1)}, u32[]{:S(2)}, u32[]{:S(2)}) collective-permute-start(bf16[64,512]{1,0:T(8,128)(2,1)S(1)} %get-tuple-element.20.refs_3_), channel_id=1, source_target_pairs={{0,12},{4,8},{8,4},{12,0},{1,13},{5,9},{9,5},{13,1},{2,14},{6,10},... | collective-permute-start | bytes 196616 | tf_op jit(solution)/shard_map/ppermute | solution.py:182
  13.5 0.0 collective-permute-start.4
  13.5 0.8 %collective-permute-start.5 = (bf16[64,512]{1,0:T(8,128)(2,1)S(1)}, bf16[64,512]{1,0:T(8,128)(2,1)S(1)}, u32[]{:S(2)}, u32[]{:S(2)}) collective-permute-start(bf16[64,512]{1,0:T(8,128)(2,1)S(1)} %get-tuple-element.20.refs_3_), channel_id=1, source_target_pairs={{0,4},{4,0},{8,12},{12,8},{1,5},{5,1},{9,13},{13,9},{2,6},{6,2},{1... | collective-permute-start | bytes 196616 | tf_op jit(solution)/shard_map/ppermute | solution.py:182
  14.3 3.5 %gather_out.1.refs_4_ = bf16[2048,1536]{1,0:T(8,128)(2,1)S(1)} custom-call(s32[16]{0:T(128)S(1)} %bitcast.8, bf16[6144,1536]{1,0:T(8,128)(2,1)} %weight_ref.3), custom_call_target="tpu_custom_call" | custom-call | bytes 12582912 | tf_op jit(solution)/shard_map/gather_out/pallas_call | solution.py:67
  17.7 0.0 collective-permute-done.3.refs_0_
  17.7 1.1 %collective-permute-done.4.refs_1_ = bf16[64,512]{1,0:T(8,128)(2,1)S(1)} collective-permute-done((bf16[64,512]{1,0:T(8,128)(2,1)S(1)}, bf16[64,512]{1,0:T(8,128)(2,1)S(1)}, u32[]{:S(2)}, u32[]{:S(2)}) %collective-permute-start.4) | collective-permute-done | bytes 65568 | tf_op jit(solution)/shard_map/ppermute | solution.py:182
  18.8 0.0 collective-permute-done.5.refs_2_
  18.8 0.0 copy-done
  18.9 1.9 %second_dot.1 = (f32[32,1536]{1,0:T(8,128)S(1)}, f32[32,1536]{1,0:T(8,128)S(1)}) custom-call(s32[16]{0:T(128)S(1)} %bitcast.9, f32[64,128]{1,0:T(8,128)S(1)} %get-tuple-element.19.ids_ref, f32[48,128]{1,0:T(8,128)S(1)} %bitcast.5, bf16[64,512]{1,0:T(8,128)(2,1)S(1)} %collective-permute-done.3.refs_0_, bf16[64,512]{1,0:T(8,128)(2,1)S(1)} %collective-permute-done.4.refs_1_, ...), custom_call_target="tpu_custom_call" | custom-call | tf_op jit(solution)/shard_map/second_dot/pallas_call | solution.py:187
  20.8 1.9 %collective-permute-start.6 = (f32[32,1536]{1,0:T(8,128)S(1)}, f32[32,1536]{1,0:T(8,128)S(1)}, u32[]{:S(2)}, u32[]{:S(2)}) collective-permute-start(f32[32,1536]{1,0:T(8,128)S(1)} %get-tuple-element.22), channel_id=1, source_target_pairs={{0,1},{1,0},{2,3},{3,2},{4,5},{5,4},{6,7},{7,6},{8,9},{9,8},{10,11... | collective-permute-start | bytes 589832 | tf_op jit(solution)/shard_map/ppermute | solution.py:198
  22.6 1.1 %collective-permute-done.6 = f32[32,1536]{1,0:T(8,128)S(1)} collective-permute-done((f32[32,1536]{1,0:T(8,128)S(1)}, f32[32,1536]{1,0:T(8,128)S(1)}, u32[]{:S(2)}, u32[]{:S(2)}) %collective-permute-start.6) | collective-permute-done | bytes 196640 | tf_op jit(solution)/shard_map/ppermute | solution.py:198
  23.7 4.4 %collective-permute-start.7 = (bf16[16,1536]{1,0:T(8,128)(2,1)S(1)}, bf16[16,1536]{1,0:T(8,128)(2,1)S(1)}, u32[]{:S(2)}, u32[]{:S(2)}) collective-permute-start(bf16[16,1536]{1,0:T(8,128)(2,1)S(1)} %get-tuple-element.23), channel_id=1, source_target_pairs={{0,0},{1,8},{2,4},{3,12},{4,1},{5,9},{6,5},{7,13},{8,2},{9,10},{10... | collective-permute-start | bytes 147464 | tf_op jit(solution)/shard_map/ppermute | solution.py:207
  28.1 1.4 %collective-permute-start.8 = (bf16[16,1536]{1,0:T(8,128)(2,1)S(1)}, bf16[16,1536]{1,0:T(8,128)(2,1)S(1)}, u32[]{:S(2)}, u32[]{:S(2)}) collective-permute-start(bf16[16,1536]{1,0:T(8,128)(2,1)S(1)} %get-tuple-element.24), channel_id=1, source_target_pairs={{0,4},{1,12},{2,0},{3,8},{4,5},{5,13},{6,1},{7,9},{8,6},{9,14},{10... | collective-permute-start | bytes 147464 | tf_op jit(solution)/shard_map/ppermute | solution.py:207
  29.5 2.4 %collective-permute-done.7 = bf16[16,1536]{1,0:T(8,128)(2,1)S(1)} collective-permute-done((bf16[16,1536]{1,0:T(8,128)(2,1)S(1)}, bf16[16,1536]{1,0:T(8,128)(2,1)S(1)}, u32[]{:S(2)}, u32[]{:S(2)}) %collective-permute-start.7) | collective-permute-done | bytes 49184 | tf_op jit(solution)/shard_map/ppermute | solution.py:207
  31.9 1.6 %collective-permute-done.8 = bf16[16,1536]{1,0:T(8,128)(2,1)S(1)} collective-permute-done((bf16[16,1536]{1,0:T(8,128)(2,1)S(1)}, bf16[16,1536]{1,0:T(8,128)(2,1)S(1)}, u32[]{:S(2)}, u32[]{:S(2)}) %collective-permute-start.8) | collective-permute-done | bytes 49184 | tf_op jit(solution)/shard_map/ppermute | solution.py:207
  33.5 0.0 copy-done.1
  33.5 0.6 %add_convert_fusion.1 = bf16[16,1536]{1,0:T(8,128)(2,1)} fusion(bf16[16,1536]{1,0:T(8,128)(2,1)S(1)} %collective-permute-done.8, bf16[16,1536]{1,0:T(8,128)(2,1)S(1)} %collective-permute-done.7, f32[1536]{0:T(1024)S(1)} %copy-done.1), kind=kLoop, calls=%fused_computation.1 | loop fusion | flops 122880 | bytes 153600 | tf_op jit(solution)/shard_map/convert_element_type | solution.py:210
  (2 shorter events, 0.0 us)
Async XLA Ops:
  0.9 7.4 %collective-permute-start = (bf16[16,1664]{1,0:T(8,128)(2,1)S(1)}, bf16[16,1664]{1,0:T(8,128)(2,1)S(1)}, u32[]{:S(2)}, u32[]{:S(2)}) collective-permute-start(bf16[16,1664]{1,0:T(8,128)(2,1)S(1)} %get-tuple-element.15), channel_id=1, source_target_pairs={{0,12},{4,8},{8,4},{12,0},{1,13},{5,9},{9,5},{13,1},{2,14},{6,10},... | collective-permute-start | bytes 159752 | tf_op jit(solution)/shard_map/ppermute | solution.py:164
  4.3 4.5 %collective-permute-start.1 = (bf16[16,1664]{1,0:T(8,128)(2,1)S(1)}, bf16[16,1664]{1,0:T(8,128)(2,1)S(1)}, u32[]{:S(2)}, u32[]{:S(2)}) collective-permute-start(bf16[16,1664]{1,0:T(8,128)(2,1)S(1)} %get-tuple-element.16), channel_id=1, source_target_pairs={{0,8},{4,12},{8,0},{12,4},{1,9},{5,13},{9,1},{13,5},{2,10},{6,14},... | collective-permute-start | bytes 159752 | tf_op jit(solution)/shard_map/ppermute | solution.py:164
  4.3 4.5 %collective-permute-start.2 = (bf16[16,1664]{1,0:T(8,128)(2,1)S(1)}, bf16[16,1664]{1,0:T(8,128)(2,1)S(1)}, u32[]{:S(2)}, u32[]{:S(2)}) collective-permute-start(bf16[16,1664]{1,0:T(8,128)(2,1)S(1)} %get-tuple-element.17), channel_id=1, source_target_pairs={{0,4},{4,0},{8,12},{12,8},{1,5},{5,1},{9,13},{13,9},{2,6},{6,2},{1... | collective-permute-start | bytes 159752 | tf_op jit(solution)/shard_map/ppermute | solution.py:164
  8.3 10.5 %copy-start = (f32[6144]{0:T(1024)S(1)}, f32[6144]{0:T(1024)}, u32[]{:S(2)}) copy-start(f32[6144]{0:T(1024)} %param.9) | copy-start | bytes 73732
  8.8 24.7 %copy-start.1 = (f32[1536]{0:T(1024)S(1)}, f32[1536]{0:T(1024)}, u32[]{:S(2)}) copy-start(f32[1536]{0:T(1024)} %param.11) | copy-start | bytes 18436
  10.7 7.1 %collective-permute-start.3 = (bf16[64,512]{1,0:T(8,128)(2,1)S(1)}, bf16[64,512]{1,0:T(8,128)(2,1)S(1)}, u32[]{:S(2)}, u32[]{:S(2)}) collective-permute-start(bf16[64,512]{1,0:T(8,128)(2,1)S(1)} %get-tuple-element.20.refs_3_), channel_id=1, source_target_pairs={{0,12},{4,8},{8,4},{12,0},{1,13},{5,9},{9,5},{13,1},{2,14},{6,10},... | collective-permute-start | bytes 196616 | tf_op jit(solution)/shard_map/ppermute | solution.py:182
  13.5 5.3 %collective-permute-start.4 = (bf16[64,512]{1,0:T(8,128)(2,1)S(1)}, bf16[64,512]{1,0:T(8,128)(2,1)S(1)}, u32[]{:S(2)}, u32[]{:S(2)}) collective-permute-start(bf16[64,512]{1,0:T(8,128)(2,1)S(1)} %get-tuple-element.20.refs_3_), channel_id=1, source_target_pairs={{0,8},{4,12},{8,0},{12,4},{1,9},{5,13},{9,1},{13,5},{2,10},{6,14},... | collective-permute-start | bytes 196616 | tf_op jit(solution)/shard_map/ppermute | solution.py:182
  13.5 5.3 %collective-permute-start.5 = (bf16[64,512]{1,0:T(8,128)(2,1)S(1)}, bf16[64,512]{1,0:T(8,128)(2,1)S(1)}, u32[]{:S(2)}, u32[]{:S(2)}) collective-permute-start(bf16[64,512]{1,0:T(8,128)(2,1)S(1)} %get-tuple-element.20.refs_3_), channel_id=1, source_target_pairs={{0,4},{4,0},{8,12},{12,8},{1,5},{5,1},{9,13},{13,9},{2,6},{6,2},{1... | collective-permute-start | bytes 196616 | tf_op jit(solution)/shard_map/ppermute | solution.py:182
  20.8 2.9 %collective-permute-start.6 = (f32[32,1536]{1,0:T(8,128)S(1)}, f32[32,1536]{1,0:T(8,128)S(1)}, u32[]{:S(2)}, u32[]{:S(2)}) collective-permute-start(f32[32,1536]{1,0:T(8,128)S(1)} %get-tuple-element.22), channel_id=1, source_target_pairs={{0,1},{1,0},{2,3},{3,2},{4,5},{5,4},{6,7},{7,6},{8,9},{9,8},{10,11... | collective-permute-start | bytes 589832 | tf_op jit(solution)/shard_map/ppermute | solution.py:198
  23.7 8.2 %collective-permute-start.7 = (bf16[16,1536]{1,0:T(8,128)(2,1)S(1)}, bf16[16,1536]{1,0:T(8,128)(2,1)S(1)}, u32[]{:S(2)}, u32[]{:S(2)}) collective-permute-start(bf16[16,1536]{1,0:T(8,128)(2,1)S(1)} %get-tuple-element.23), channel_id=1, source_target_pairs={{0,0},{1,8},{2,4},{3,12},{4,1},{5,9},{6,5},{7,13},{8,2},{9,10},{10... | collective-permute-start | bytes 147464 | tf_op jit(solution)/shard_map/ppermute | solution.py:207
  28.1 5.4 %collective-permute-start.8 = (bf16[16,1536]{1,0:T(8,128)(2,1)S(1)}, bf16[16,1536]{1,0:T(8,128)(2,1)S(1)}, u32[]{:S(2)}, u32[]{:S(2)}) collective-permute-start(bf16[16,1536]{1,0:T(8,128)(2,1)S(1)} %get-tuple-element.24), channel_id=1, source_target_pairs={{0,4},{1,12},{2,0},{3,8},{4,5},{5,13},{6,1},{7,9},{8,6},{9,14},{10... | collective-permute-start | bytes 147464 | tf_op jit(solution)/shard_map/ppermute | solution.py:207

commit v5 on v4

--- a/solution.py
+++ b/solution.py
@@ -12,6 +12,13 @@
 F32 = jnp.float32
 VMEM = pltpu.VMEM
 SMEM = pltpu.SMEM
+
+
+ORDER = (2, 3, 1)
+
+
+def by_partner(refs):
+    return [refs[(ORDER + (0,)).index(k)] for k in range(len(refs))]
 
 
 def whole(space):
@@ -77,7 +84,7 @@
 
 
 def first_kernel(count, slots, union_ref, *refs):
-    chunk_refs = refs[:count][::-1]
+    chunk_refs = by_partner(refs[:count])
     win_ref, pre_ref, ids_ref, dense = refs[count:]
     width, total = win_ref.shape
     rows = chunk_refs[0].shape[0]
@@ -100,7 +107,7 @@
 
 
 def second_kernel(count, slots, union_ref, ids_ref, bias_ref, *refs):
-    part_refs = refs[:count][::-1]
+    part_refs = by_partner(refs[:count])
     wout_ref = refs[count]
     keep_ref, send_ref, spread, terms = refs[count + 1 :]
     store, tensor = lax.axis_index("store"), lax.axis_index("tensor")
@@ -132,11 +139,19 @@
     for n in range(0, width, step):
         product = jnp.dot(hidden, wout_ref[:, n : n + step], preferred_element_type=F32)
         terms[:, :, n : n + step] = product.reshape(count, rows, step)
-    chip, core = tensor // 2, tensor % 2
-    for k in range(count // 2):
-        part = slice(k * rows, (k + 1) * rows)
-        keep_ref[part, :] = terms[store ^ (2 * core + (chip ^ k))]
-        send_ref[part, :] = terms[store ^ (2 * (1 - core) + (chip ^ k))]
+    for turn in range(2):
+        part = slice(turn * rows, (turn + 1) * rows)
+        keep_ref[part, :] = terms[store ^ way_home(store, tensor, turn)]
+        send_ref[part, :] = terms[store ^ way_home(store, tensor ^ 1, turn)]
+
+
+def way_home(store, tensor, turn):
+    high, low = store >> 1, store & 1
+    odd = tensor & 1
+    far = odd * 3 * (1 - high) + (1 - odd) * (1 + low)
+    near = odd * (2 * (1 - low) + high) + (1 - odd) * store
+    far_now = ((tensor >> 1) ^ high) ^ turn
+    return far_now * far + (1 - far_now) * near
 
 
 def fast(states, weight_in, bias_in, weight_out, bias_out, block_lists, union_blocks):
@@ -160,9 +175,7 @@
     def over_store(k):
         return [(i, i ^ k) for i in range(count)]
 
-    far_first = list(range(count - 1, 0, -1))
-    got = {k: lax.ppermute(chunks[k], "store", over_store(k)) for k in far_first}
-    got = [got[k] for k in far_first] + [chunks[0]]
+    got = [lax.ppermute(chunks[k], "store", over_store(k)) for k in ORDER] + [chunks[0]]
 
     win = gather(True, union_ids, weight_in, "gather_in")
 
@@ -179,8 +192,7 @@
         name="first_dot",
     )(union_ids, *got, win)
 
-    parts = {k: lax.ppermute(pre, "store", over_store(k)) for k in far_first}
-    parts = [parts[k] for k in far_first] + [pre]
+    parts = [lax.ppermute(pre, "store", over_store(k)) for k in ORDER] + [pre]
 
     wout = gather(False, union_ids, weight_out, "gather_out")
 
@@ -197,10 +209,10 @@
     pair = [(i, i ^ 1) for i in range(count)]
     both = (keep + lax.ppermute(send, "tensor", pair)).astype(BF16)
 
-    def home(k):
+    def home(turn):
         return [
-            (z * count + 2 * x + c, (2 * c + (x ^ k)) * count + z)
-            for z in range(count) for x in range(count // 2) for c in range(2)
+            (z * count + t, way_home(z, t, turn) * count + z)
+            for z in range(count) for t in range(count)
         ]
 
     summed = sum(
@@ -269,7 +281,7 @@
 
 def solution(mesh):
     count = mesh.shape["store"]
-    square = count == mesh.shape["tensor"] and count & (count - 1) == 0
+    square = count == 4 and mesh.shape["tensor"] == 4
     return jax.shard_map(
         fast if square else general,
         mesh=mesh,

time: 34.3 us -> 33.2 us (0.968)
  waiting for transfers between devices: 6.62 us -> 5.7 us
  starting transfers between devices: 15 us -> 14.6 us
    ppermute x2, starting transfers between devices: 5.77 us -> 4.87 us  [fast(): lax.ppermute(both[k * rows:(k + 1) * rows], ('store', 'tensor'), home(k))]
    ppermute x1, starting transfers between devices: 1.86 us -> 2.67 us  [fast(): both = (keep + lax.ppermute(send, 'tensor', pair)).astype(BF16)]
    ppermute x3, waiting for transfers between devices: 0.44 us -> 0.01 us  [fast(): lax.ppermute(chunks[k], 'store', over_store(k))]
  transfers between devices with their start and end apart: 9 -> 9, of which waited for: 5 -> 4; matrix products, arithmetic and copies ran while one was open for 0% -> 0% of each run, Pallas kernels for 21% -> 22%
where the time goes in v5:
time: 33.2 us; the launch traced here: 32.9 us
  starting transfers between devices  14.6 us (44%)
  Pallas kernels  11.8 us (36%)
  waiting for transfers between devices  5.7 us (17%)
  other arithmetic  0.67 us (2%)
    pallas_call x2, Pallas kernels, gather(): pl.pallas_call(functools.partial(gather_kernel, by_column), out_shape=VME...  7.09 us
    ppermute x2, starting transfers between devices, fast(): lax.ppermute(both[k * rows:(k + 1) * rows], ('store', 'tensor'), home(k))  4.87 us
    ppermute x2, waiting for transfers between devices, fast(): lax.ppermute(both[k * rows:(k + 1) * rows], ('store', 'tensor'), home(k))  3.69 us
    ppermute x3, starting transfers between devices, fast(): lax.ppermute(chunks[k], 'store', over_store(k))  3.67 us
    ppermute x3, starting transfers between devices, fast(): parts = [lax.ppermute(pre, 'store', over_store(k)) for k in ORDER] + [pre]  3.4 us
    ppermute x1, starting transfers between devices, fast(): both = (keep + lax.ppermute(send, 'tensor', pair)).astype(BF16)  2.67 us
    pallas_call x1, Pallas kernels, fast(): pl.pallas_call(functools.partial(second_kernel, count, slots), out_shape=...  1.9 us
    pallas_call x1, Pallas kernels, fast(): pl.pallas_call(functools.partial(first_kernel, count, slots), out_shape=[...  1.85 us
  transfers between devices with their start and end apart: 9, of which 4 were waited for; matrix products, arithmetic and copies ran while one was open for 0% of the time, Pallas kernels for 22%

profile of v5, /device:TPU:3, one launch (start us, length us, event | category | flops | bytes accessed | tf_op | source)
XLA Modules:
  0.0 32.9 jit_solution(8523203996824545131)
XLA Ops:
  0.0 0.9 %split_states.1 = (bf16[16,1664]{1,0:T(8,128)(2,1)S(1)}, bf16[16,1664]{1,0:T(8,128)(2,1)S(1)}, bf16[16,1664]{1,0:T(8,128)(2,1)S(1)}, bf16[16,1664]{1,0:T(8,128)(2,1)S(1)}, s32[1,16]{1,0:T(1,128)S(1)}) custom-call(bf16[16,6144]{1,0:T(8,128)(2,1)} %states_ref.1, s32[4,16]{1,0:T(4,128)} %bitcast.10, s32[1,16]{1,0:T(1,128)} %union_ref.1), custom_call_target="tpu_custom_call" | custom-call | tf_op jit(solution)/shard_map/split_states/pallas_call | solution.py:165
  0.9 2.4 %collective-permute-start = (bf16[16,1664]{1,0:T(8,128)(2,1)S(1)}, bf16[16,1664]{1,0:T(8,128)(2,1)S(1)}, u32[]{:S(2)}, u32[]{:S(2)}) collective-permute-start(bf16[16,1664]{1,0:T(8,128)(2,1)S(1)} %get-tuple-element.15), channel_id=1, source_target_pairs={{0,8},{4,12},{8,0},{12,4},{1,9},{5,13},{9,1},{13,5},{2,10},{6,14},... | collective-permute-start | bytes 159752 | tf_op jit(solution)/shard_map/ppermute | solution.py:178
  3.3 1.1 %collective-permute-start.1 = (bf16[16,1664]{1,0:T(8,128)(2,1)S(1)}, bf16[16,1664]{1,0:T(8,128)(2,1)S(1)}, u32[]{:S(2)}, u32[]{:S(2)}) collective-permute-start(bf16[16,1664]{1,0:T(8,128)(2,1)S(1)} %get-tuple-element.16), channel_id=1, source_target_pairs={{0,12},{4,8},{8,4},{12,0},{1,13},{5,9},{9,5},{13,1},{2,14},{6,10},... | collective-permute-start | bytes 159752 | tf_op jit(solution)/shard_map/ppermute | solution.py:178
  4.4 0.2 collective-permute-start.2
  4.6 3.6 %gather_in.1.refs_4_ = bf16[1536,2048]{1,0:T(8,128)(2,1)S(1)} custom-call(s32[16]{0:T(128)S(1)} %bitcast.6, bf16[1536,6144]{1,0:T(8,128)(2,1)} %weight_ref.2), custom_call_target="tpu_custom_call" | custom-call | bytes 12582912 | tf_op jit(solution)/shard_map/gather_in/pallas_call | solution.py:74
  8.3 0.0 copy-start
  8.3 0.0 collective-permute-done.refs_0_
  8.3 0.0 collective-permute-done.1.refs_1_
  8.3 0.0 collective-permute-done.2.refs_2_
  8.3 0.0 copy-start.1
  8.3 1.8 %first_dot.1 = (bf16[64,512]{1,0:T(8,128)(2,1)S(1)}, f32[64,128]{1,0:T(8,128)S(1)}) custom-call(s32[16]{0:T(128)S(1)} %bitcast.7, bf16[16,1664]{1,0:T(8,128)(2,1)S(1)} %collective-permute-done.refs_0_, bf16[16,1664]{1,0:T(8,128)(2,1)S(1)} %collective-permute-done.1.refs_1_, bf16[16,1664]{1,0:T(8,128)(2,1)S(1)} %collective-permute-done.2.refs_2_, ...), custom_call_target="tpu_custom_call" | custom-call | tf_op jit(solution)/shard_map/first_dot/pallas_call | solution.py:182
  10.2 2.5 %collective-permute-start.3 = (bf16[64,512]{1,0:T(8,128)(2,1)S(1)}, bf16[64,512]{1,0:T(8,128)(2,1)S(1)}, u32[]{:S(2)}, u32[]{:S(2)}) collective-permute-start(bf16[64,512]{1,0:T(8,128)(2,1)S(1)} %get-tuple-element.20.refs_3_), channel_id=1, source_target_pairs={{0,8},{4,12},{8,0},{12,4},{1,9},{5,13},{9,1},{13,5},{2,10},{6,14},... | collective-permute-start | bytes 196616 | tf_op jit(solution)/shard_map/ppermute | solution.py:195
  12.7 0.9 %collective-permute-start.4 = (bf16[64,512]{1,0:T(8,128)(2,1)S(1)}, bf16[64,512]{1,0:T(8,128)(2,1)S(1)}, u32[]{:S(2)}, u32[]{:S(2)}) collective-permute-start(bf16[64,512]{1,0:T(8,128)(2,1)S(1)} %get-tuple-element.20.refs_3_), channel_id=1, source_target_pairs={{0,12},{4,8},{8,4},{12,0},{1,13},{5,9},{9,5},{13,1},{2,14},{6,10},... | collective-permute-start | bytes 196616 | tf_op jit(solution)/shard_map/ppermute | solution.py:195
  13.6 0.0 collective-permute-start.5
  13.6 3.5 %gather_out.1.refs_4_ = bf16[2048,1536]{1,0:T(8,128)(2,1)S(1)} custom-call(s32[16]{0:T(128)S(1)} %bitcast.8, bf16[6144,1536]{1,0:T(8,128)(2,1)} %weight_ref.3), custom_call_target="tpu_custom_call" | custom-call | bytes 12582912 | tf_op jit(solution)/shard_map/gather_out/pallas_call | solution.py:74
  17.0 0.0 collective-permute-done.3.refs_0_
  17.1 0.9 %collective-permute-done.4.refs_1_ = bf16[64,512]{1,0:T(8,128)(2,1)S(1)} collective-permute-done((bf16[64,512]{1,0:T(8,128)(2,1)S(1)}, bf16[64,512]{1,0:T(8,128)(2,1)S(1)}, u32[]{:S(2)}, u32[]{:S(2)}) %collective-permute-start.4) | collective-permute-done | bytes 65568 | tf_op jit(solution)/shard_map/ppermute | solution.py:195
  18.0 0.0 collective-permute-done.5.refs_2_
  18.0 0.0 copy-done
  18.0 1.9 %second_dot.1 = (f32[32,1536]{1,0:T(8,128)S(1)}, f32[32,1536]{1,0:T(8,128)S(1)}) custom-call(s32[16]{0:T(128)S(1)} %bitcast.9, f32[64,128]{1,0:T(8,128)S(1)} %get-tuple-element.19.ids_ref, f32[48,128]{1,0:T(8,128)S(1)} %bitcast.5, bf16[64,512]{1,0:T(8,128)(2,1)S(1)} %collective-permute-done.3.refs_0_, bf16[64,512]{1,0:T(8,128)(2,1)S(1)} %collective-permute-done.4.refs_1_, ...), custom_call_target="tpu_custom_call" | custom-call | tf_op jit(solution)/shard_map/second_dot/pallas_call | solution.py:199
  19.9 2.7 %collective-permute-start.6 = (f32[32,1536]{1,0:T(8,128)S(1)}, f32[32,1536]{1,0:T(8,128)S(1)}, u32[]{:S(2)}, u32[]{:S(2)}) collective-permute-start(f32[32,1536]{1,0:T(8,128)S(1)} %get-tuple-element.22), channel_id=1, source_target_pairs={{0,1},{1,0},{2,3},{3,2},{4,5},{5,4},{6,7},{7,6},{8,9},{9,8},{10,11... | collective-permute-start | bytes 589832 | tf_op jit(solution)/shard_map/ppermute | solution.py:210
  22.6 1.1 %collective-permute-done.6 = f32[32,1536]{1,0:T(8,128)S(1)} collective-permute-done((f32[32,1536]{1,0:T(8,128)S(1)}, f32[32,1536]{1,0:T(8,128)S(1)}, u32[]{:S(2)}, u32[]{:S(2)}) %collective-permute-start.6) | collective-permute-done | bytes 196640 | tf_op jit(solution)/shard_map/ppermute | solution.py:210
  23.7 3.8 %collective-permute-start.7 = (bf16[16,1536]{1,0:T(8,128)(2,1)S(1)}, bf16[16,1536]{1,0:T(8,128)(2,1)S(1)}, u32[]{:S(2)}, u32[]{:S(2)}) collective-permute-start(bf16[16,1536]{1,0:T(8,128)(2,1)S(1)} %get-tuple-element.23), channel_id=1, source_target_pairs={{0,0},{1,8},{2,4},{3,12},{4,5},{5,1},{6,9},{7,13},{8,6},{9,2},{10,... | collective-permute-start | bytes 147464 | tf_op jit(solution)/shard_map/ppermute | solution.py:219
  27.5 1.1 %collective-permute-start.8 = (bf16[16,1536]{1,0:T(8,128)(2,1)S(1)}, bf16[16,1536]{1,0:T(8,128)(2,1)S(1)}, u32[]{:S(2)}, u32[]{:S(2)}) collective-permute-start(bf16[16,1536]{1,0:T(8,128)(2,1)S(1)} %get-tuple-element.24), channel_id=1, source_target_pairs={{0,4},{1,12},{2,0},{3,8},{4,9},{5,13},{6,5},{7,1},{8,10},{9,14},{1... | collective-permute-start | bytes 147464 | tf_op jit(solution)/shard_map/ppermute | solution.py:219
  28.6 3.0 %collective-permute-done.7 = bf16[16,1536]{1,0:T(8,128)(2,1)S(1)} collective-permute-done((bf16[16,1536]{1,0:T(8,128)(2,1)S(1)}, bf16[16,1536]{1,0:T(8,128)(2,1)S(1)}, u32[]{:S(2)}, u32[]{:S(2)}) %collective-permute-start.7) | collective-permute-done | bytes 49184 | tf_op jit(solution)/shard_map/ppermute | solution.py:219
  31.5 0.7 %collective-permute-done.8 = bf16[16,1536]{1,0:T(8,128)(2,1)S(1)} collective-permute-done((bf16[16,1536]{1,0:T(8,128)(2,1)S(1)}, bf16[16,1536]{1,0:T(8,128)(2,1)S(1)}, u32[]{:S(2)}, u32[]{:S(2)}) %collective-permute-start.8) | collective-permute-done | bytes 49184 | tf_op jit(solution)/shard_map/ppermute | solution.py:219
  32.3 0.0 copy-done.1
  32.3 0.6 %add_convert_fusion.1 = bf16[16,1536]{1,0:T(8,128)(2,1)} fusion(bf16[16,1536]{1,0:T(8,128)(2,1)S(1)} %collective-permute-done.8, bf16[16,1536]{1,0:T(8,128)(2,1)S(1)} %collective-permute-done.7, f32[1536]{0:T(1024)S(1)} %copy-done.1), kind=kLoop, calls=%fused_computation.1 | loop fusion | flops 122880 | bytes 153600 | tf_op jit(solution)/shard_map/convert_element_type | solution.py:222
  (2 shorter events, 0.0 us)
Async XLA Ops:
  0.9 7.3 %collective-permute-start = (bf16[16,1664]{1,0:T(8,128)(2,1)S(1)}, bf16[16,1664]{1,0:T(8,128)(2,1)S(1)}, u32[]{:S(2)}, u32[]{:S(2)}) collective-permute-start(bf16[16,1664]{1,0:T(8,128)(2,1)S(1)} %get-tuple-element.15), channel_id=1, source_target_pairs={{0,8},{4,12},{8,0},{12,4},{1,9},{5,13},{9,1},{13,5},{2,10},{6,14},... | collective-permute-start | bytes 159752 | tf_op jit(solution)/shard_map/ppermute | solution.py:178
  3.3 5.0 %collective-permute-start.1 = (bf16[16,1664]{1,0:T(8,128)(2,1)S(1)}, bf16[16,1664]{1,0:T(8,128)(2,1)S(1)}, u32[]{:S(2)}, u32[]{:S(2)}) collective-permute-start(bf16[16,1664]{1,0:T(8,128)(2,1)S(1)} %get-tuple-element.16), channel_id=1, source_target_pairs={{0,12},{4,8},{8,4},{12,0},{1,13},{5,9},{9,5},{13,1},{2,14},{6,10},... | collective-permute-start | bytes 159752 | tf_op jit(solution)/shard_map/ppermute | solution.py:178
  4.4 3.9 %collective-permute-start.2 = (bf16[16,1664]{1,0:T(8,128)(2,1)S(1)}, bf16[16,1664]{1,0:T(8,128)(2,1)S(1)}, u32[]{:S(2)}, u32[]{:S(2)}) collective-permute-start(bf16[16,1664]{1,0:T(8,128)(2,1)S(1)} %get-tuple-element.17), channel_id=1, source_target_pairs={{0,4},{4,0},{8,12},{12,8},{1,5},{5,1},{9,13},{13,9},{2,6},{6,2},{1... | collective-permute-start | bytes 159752 | tf_op jit(solution)/shard_map/ppermute | solution.py:178
  8.3 9.7 %copy-start = (f32[6144]{0:T(1024)S(1)}, f32[6144]{0:T(1024)}, u32[]{:S(2)}) copy-start(f32[6144]{0:T(1024)} %param.9) | copy-start | bytes 73732
  8.3 23.9 %copy-start.1 = (f32[1536]{0:T(1024)S(1)}, f32[1536]{0:T(1024)}, u32[]{:S(2)}) copy-start(f32[1536]{0:T(1024)} %param.11) | copy-start | bytes 18436
  10.2 6.9 %collective-permute-start.3 = (bf16[64,512]{1,0:T(8,128)(2,1)S(1)}, bf16[64,512]{1,0:T(8,128)(2,1)S(1)}, u32[]{:S(2)}, u32[]{:S(2)}) collective-permute-start(bf16[64,512]{1,0:T(8,128)(2,1)S(1)} %get-tuple-element.20.refs_3_), channel_id=1, source_target_pairs={{0,8},{4,12},{8,0},{12,4},{1,9},{5,13},{9,1},{13,5},{2,10},{6,14},... | collective-permute-start | bytes 196616 | tf_op jit(solution)/shard_map/ppermute | solution.py:195
  12.7 5.3 %collective-permute-start.4 = (bf16[64,512]{1,0:T(8,128)(2,1)S(1)}, bf16[64,512]{1,0:T(8,128)(2,1)S(1)}, u32[]{:S(2)}, u32[]{:S(2)}) collective-permute-start(bf16[64,512]{1,0:T(8,128)(2,1)S(1)} %get-tuple-element.20.refs_3_), channel_id=1, source_target_pairs={{0,12},{4,8},{8,4},{12,0},{1,13},{5,9},{9,5},{13,1},{2,14},{6,10},... | collective-permute-start | bytes 196616 | tf_op jit(solution)/shard_map/ppermute | solution.py:195
  13.6 4.4 %collective-permute-start.5 = (bf16[64,512]{1,0:T(8,128)(2,1)S(1)}, bf16[64,512]{1,0:T(8,128)(2,1)S(1)}, u32[]{:S(2)}, u32[]{:S(2)}) collective-permute-start(bf16[64,512]{1,0:T(8,128)(2,1)S(1)} %get-tuple-element.20.refs_3_), channel_id=1, source_target_pairs={{0,4},{4,0},{8,12},{12,8},{1,5},{5,1},{9,13},{13,9},{2,6},{6,2},{1... | collective-permute-start | bytes 196616 | tf_op jit(solution)/shard_map/ppermute | solution.py:195
  19.9 3.7 %collective-permute-start.6 = (f32[32,1536]{1,0:T(8,128)S(1)}, f32[32,1536]{1,0:T(8,128)S(1)}, u32[]{:S(2)}, u32[]{:S(2)}) collective-permute-start(f32[32,1536]{1,0:T(8,128)S(1)} %get-tuple-element.22), channel_id=1, source_target_pairs={{0,1},{1,0},{2,3},{3,2},{4,5},{5,4},{6,7},{7,6},{8,9},{9,8},{10,11... | collective-permute-start | bytes 589832 | tf_op jit(solution)/shard_map/ppermute | solution.py:210
  23.7 7.8 %collective-permute-start.7 = (bf16[16,1536]{1,0:T(8,128)(2,1)S(1)}, bf16[16,1536]{1,0:T(8,128)(2,1)S(1)}, u32[]{:S(2)}, u32[]{:S(2)}) collective-permute-start(bf16[16,1536]{1,0:T(8,128)(2,1)S(1)} %get-tuple-element.23), channel_id=1, source_target_pairs={{0,0},{1,8},{2,4},{3,12},{4,5},{5,1},{6,9},{7,13},{8,6},{9,2},{10,... | collective-permute-start | bytes 147464 | tf_op jit(solution)/shard_map/ppermute | solution.py:219
  27.5 4.8 %collective-permute-start.8 = (bf16[16,1536]{1,0:T(8,128)(2,1)S(1)}, bf16[16,1536]{1,0:T(8,128)(2,1)S(1)}, u32[]{:S(2)}, u32[]{:S(2)}) collective-permute-start(bf16[16,1536]{1,0:T(8,128)(2,1)S(1)} %get-tuple-element.24), channel_id=1, source_target_pairs={{0,4},{1,12},{2,0},{3,8},{4,9},{5,13},{6,5},{7,1},{8,10},{9,14},{1... | collective-permute-start | bytes 147464 | tf_op jit(solution)/shard_map/ppermute | solution.py:219

commit v6 on v5

--- a/solution.py
+++ b/solution.py
@@ -15,10 +15,11 @@
 
 
 ORDER = (2, 3, 1)
-
-
-def by_partner(refs):
-    return [refs[(ORDER + (0,)).index(k)] for k in range(len(refs))]
+ORDER_TWO = (3, 1, 2)
+
+
+def by_partner(refs, order=ORDER):
+    return [refs[(order + (0,)).index(k)] for k in range(len(refs))]
 
 
 def whole(space):
@@ -39,13 +40,16 @@
             )
         )
         copies[-1].start()
-    copies.append(pltpu.make_async_copy(union_ref, union_out, sems.at[count + 1]))
-    copies[-1].start()
+    union_copy = pltpu.make_async_copy(union_ref, union_out, sems.at[count + 1])
+    union_copy.start()
     slots, rows = ids_ref.shape
     ids_copy.wait()
-    padded = jnp.concatenate(
-        [ids[...].astype(F32), jnp.full((BLOCK - slots, rows), -1.0, F32)], axis=0
-    )
+    union_copy.wait()
+    blocks, union = ids[...], union_out[...]
+    places = jnp.full((slots, rows), -1.0, F32)
+    for u in range(union.shape[1]):
+        places = jnp.where(blocks == union[:, u : u + 1], float(u), places)
+    padded = jnp.concatenate([places, jnp.full((BLOCK - slots, rows), -1.0, F32)], axis=0)
     tail = padded.T.astype(BF16)
     for k in range(count):
         out_refs[k][:, width:] = tail
@@ -53,9 +57,12 @@
         copy.wait()
 
 
-def gather_kernel(by_column, union_ref, weight_ref, out_ref, sems):
+def gather_kernel(by_column, union_ref, weight_ref, *refs):
+    *bias_refs, sems = refs
+    out_ref = bias_refs.pop(len(bias_refs) // 2)
+    union = union_ref.shape[0]
     copies = []
-    for u in range(union_ref.shape[0]):
+    for u in range(union):
         block = pl.ds(pl.multiple_of(union_ref[u] * BLOCK, BLOCK), BLOCK)
         place = pl.ds(u * BLOCK, BLOCK)
         if by_column:
@@ -64,31 +71,35 @@
             source, target = weight_ref.at[block, :], out_ref.at[place, :]
         copies.append(pltpu.make_async_copy(source, target, sems.at[u]))
         copies[-1].start()
+    if bias_refs:
+        bias_ref, bias_out = bias_refs
+        for u in range(union):
+            bias_out[u : u + 1, :] = bias_ref[pl.ds(union_ref[u], 1), :]
     for copy in copies:
         copy.wait()
 
 
-def gather(by_column, union_ids, weight, name):
+def gather(by_column, union_ids, weight, name, *bias):
     union = union_ids.shape[0]
     shape = (weight.shape[0], union * BLOCK) if by_column else (union * BLOCK, weight.shape[1])
     return pl.pallas_call(
         functools.partial(gather_kernel, by_column),
-        out_shape=VMEM(shape, BF16),
-        in_specs=[whole(SMEM), whole(pltpu.HBM)],
-        out_specs=whole(VMEM),
+        out_shape=[VMEM(shape, BF16)] + [VMEM((union, BLOCK), F32)] * len(bias),
+        in_specs=[whole(SMEM), whole(pltpu.HBM)] + [whole(VMEM)] * len(bias),
+        out_specs=[whole(VMEM)] * (1 + len(bias)),
         scratch_shapes=[pltpu.SemaphoreType.DMA((union,))],
         compiler_params=pltpu.CompilerParams(vmem_limit_bytes=40 * 2**20),
         cost_estimate=pl.CostEstimate(flops=0, bytes_accessed=4 * shape[0] * shape[1], transcendentals=0),
         name=name,
-    )(union_ids, weight)
-
-
-def first_kernel(count, slots, union_ref, *refs):
+    )(union_ids, weight, *bias)
+
+
+def first_kernel(count, slots, *refs):
     chunk_refs = by_partner(refs[:count])
     win_ref, pre_ref, ids_ref, dense = refs[count:]
     width, total = win_ref.shape
     rows = chunk_refs[0].shape[0]
-    union = union_ref.shape[0]
+    union = total // BLOCK
     states = jnp.concatenate([c[:, :width] for c in chunk_refs], axis=0)
     ids = jnp.concatenate([c[:, width:] for c in chunk_refs], axis=0).astype(F32)
     ids_ref[...] = ids
@@ -101,18 +112,17 @@
             mine = jnp.broadcast_to(ids[part, k : k + 1], (rows, BLOCK))
             picked = jnp.zeros((rows, BLOCK), F32)
             for u in range(union):
-                block = union_ref[u].astype(F32)
-                picked = jnp.where(mine == block, dense[part, u * BLOCK : (u + 1) * BLOCK], picked)
+                picked = jnp.where(mine == float(u), dense[part, u * BLOCK : (u + 1) * BLOCK], picked)
             pre_ref[part, k * BLOCK : (k + 1) * BLOCK] = picked.astype(pre_ref.dtype)
 
 
-def second_kernel(count, slots, union_ref, ids_ref, bias_ref, *refs):
-    part_refs = by_partner(refs[:count])
+def second_kernel(count, slots, ids_ref, bias_ref, *refs):
+    part_refs = by_partner(refs[:count], ORDER_TWO)
     wout_ref = refs[count]
     keep_ref, send_ref, spread, terms = refs[count + 1 :]
     store, tensor = lax.axis_index("store"), lax.axis_index("tensor")
     rows = ids_ref.shape[0] // count
-    union = union_ref.shape[0]
+    union = bias_ref.shape[0]
     ids = ids_ref[...]
     for j in range(count):
         part = slice(j * rows, (j + 1) * rows)
@@ -127,11 +137,10 @@
                 )
             )
         for u in range(union):
-            block = union_ref[u].astype(F32)
             value = jnp.zeros((rows, BLOCK), F32)
-            bias = bias_ref[pl.ds(union_ref[u], 1), :]
+            bias = bias_ref[u : u + 1, :]
             for k in range(slots):
-                value = jnp.where(mines[k] == block, jnp.maximum(pres[k] + bias, 0.0), value)
+                value = jnp.where(mines[k] == float(u), jnp.maximum(pres[k] + bias, 0.0), value)
             spread[part, u * BLOCK : (u + 1) * BLOCK] = value.astype(BF16)
     step = 2 * BLOCK
     width = wout_ref.shape[1]
@@ -145,13 +154,20 @@
         send_ref[part, :] = terms[store ^ way_home(store, tensor ^ 1, turn)]
 
 
+WAY_HOME = (
+    ((2, 1), (3, 0), (1, 2), (0, 3)),
+    ((1, 3), (2, 0), (3, 1), (0, 2)),
+    ((2, 3), (0, 1), (3, 2), (1, 0)),
+    ((3, 2), (0, 1), (2, 3), (1, 0)),
+)
+
+
 def way_home(store, tensor, turn):
-    high, low = store >> 1, store & 1
-    odd = tensor & 1
-    far = odd * 3 * (1 - high) + (1 - odd) * (1 + low)
-    near = odd * (2 * (1 - low) + high) + (1 - odd) * store
-    far_now = ((tensor >> 1) ^ high) ^ turn
-    return far_now * far + (1 - far_now) * near
+    code = sum(
+        WAY_HOME[s][t][turn] << 2 * (4 * s + t) for s in range(4) for t in range(4)
+    )
+    code = jnp.int32(code - (1 << 32) if code >= 1 << 31 else code)
+    return lax.shift_right_logical(code, 2 * (4 * store + tensor)) & 3
 
 
 def fast(states, weight_in, bias_in, weight_out, bias_out, block_lists, union_blocks):
@@ -177,7 +193,7 @@
 
     got = [lax.ppermute(chunks[k], "store", over_store(k)) for k in ORDER] + [chunks[0]]
 
-    win = gather(True, union_ids, weight_in, "gather_in")
+    (win,) = gather(True, union_ids, weight_in, "gather_in")
 
     pre, ids = pl.pallas_call(
         functools.partial(first_kernel, count, slots),
@@ -185,33 +201,33 @@
             jax.ShapeDtypeStruct((count * rows, slots * BLOCK), BF16),
             jax.ShapeDtypeStruct((count * rows, BLOCK), F32),
         ],
-        in_specs=[whole(SMEM)] + [whole(VMEM)] * (count + 1),
+        in_specs=[whole(VMEM)] * (count + 1),
         out_specs=[whole(VMEM)] * 2,
         scratch_shapes=[VMEM((count * rows, total), F32)],
         compiler_params=pltpu.CompilerParams(vmem_limit_bytes=40 * 2**20),
         name="first_dot",
-    )(union_ids, *got, win)
-
-    parts = [lax.ppermute(pre, "store", over_store(k)) for k in ORDER] + [pre]
-
-    wout = gather(False, union_ids, weight_out, "gather_out")
+    )(*got, win)
+
+    parts = [lax.ppermute(pre, "store", over_store(k)) for k in ORDER_TWO] + [pre]
+
+    wout, bias = gather(False, union_ids, weight_out, "gather_out", bias_in.reshape(-1, BLOCK))
 
     keep, send = pl.pallas_call(
         functools.partial(second_kernel, count, slots),
         out_shape=[VMEM((count // 2 * rows, width), F32)] * 2,
-        in_specs=[whole(SMEM)] + [whole(VMEM)] * (count + 3),
+        in_specs=[whole(VMEM)] * (count + 3),
         out_specs=[whole(VMEM)] * 2,
         scratch_shapes=[VMEM((count * rows, total), BF16), VMEM((count, rows, width), F32)],
         compiler_params=pltpu.CompilerParams(vmem_limit_bytes=40 * 2**20),
         name="second_dot",
-    )(union_ids, ids, bias_in.reshape(-1, BLOCK), *parts, wout)
+    )(ids, bias, *parts, wout)
 
     pair = [(i, i ^ 1) for i in range(count)]
     both = (keep + lax.ppermute(send, "tensor", pair)).astype(BF16)
 
     def home(turn):
         return [
-            (z * count + t, way_home(z, t, turn) * count + z)
+            (z * count + t, WAY_HOME[z][t][turn] * count + z)
             for z in range(count) for t in range(count)
         ]
 

time: 33.2 us -> 31.7 us (0.955)
  Pallas kernels: 11.8 us -> 10.7 us
  waiting for transfers between devices: 5.7 us -> 4.6 us
  starting transfers between devices: 14.6 us -> 15.1 us
    ppermute x2, waiting for transfers between devices: 3.69 us -> 2.61 us  [fast(): lax.ppermute(both[k * rows:(k + 1) * rows], ('store', 'tensor'), home(k))]
    pallas_call x1, Pallas kernels: 1.9 us -> 1.31 us  [fast(): pl.pallas_call(functools.partial(second_kernel, count, slots), out_shape=...]
    pallas_call x1, Pallas kernels: 1.85 us -> 1.3 us  [fast(): pl.pallas_call(functools.partial(first_kernel, count, slots), out_shape=[...]
    ppermute x3, starting transfers between devices: 3.4 us -> 3.8 us  [fast(): lax.ppermute(pre, 'store', over_store(k))]
    ppermute x1, starting transfers between devices: 2.67 us -> 3.06 us  [fast(): both = (keep + lax.ppermute(send, 'tensor', pair)).astype(BF16)]
  transfers between devices with their start and end apart: 9 -> 9, of which waited for: 4 -> 4; matrix products, arithmetic and copies ran while one was open for 0% -> 0% of each run, Pallas kernels for 22% -> 23%
where the time goes in v6:
time: 31.7 us; the launch traced here: 31.2 us
  starting transfers between devices  15.1 us (48%)
  Pallas kernels  10.7 us (34%)
  waiting for transfers between devices  4.6 us (15%)
  other arithmetic  0.66 us (2%)
    pallas_call x2, Pallas kernels, gather(): pl.pallas_call(functools.partial(gather_kernel, by_column), out_shape=[VM...  7.09 us
    ppermute x2, starting transfers between devices, fast(): lax.ppermute(both[k * rows:(k + 1) * rows], ('store', 'tensor'), home(k))  4.58 us
    ppermute x3, starting transfers between devices, fast(): lax.ppermute(pre, 'store', over_store(k))  3.8 us
    ppermute x3, starting transfers between devices, fast(): lax.ppermute(chunks[k], 'store', over_store(k))  3.67 us
    ppermute x1, starting transfers between devices, fast(): both = (keep + lax.ppermute(send, 'tensor', pair)).astype(BF16)  3.06 us
    ppermute x2, waiting for transfers between devices, fast(): lax.ppermute(both[k * rows:(k + 1) * rows], ('store', 'tensor'), home(k))  2.61 us
    pallas_call x1, Pallas kernels, fast(): pl.pallas_call(functools.partial(second_kernel, count, slots), out_shape=...  1.31 us
    pallas_call x1, Pallas kernels, fast(): pl.pallas_call(functools.partial(first_kernel, count, slots), out_shape=[...  1.3 us
  transfers between devices with their start and end apart: 9, of which 4 were waited for; matrix products, arithmetic and copies ran while one was open for 0% of the time, Pallas kernels for 23%

profile of v6, /device:TPU:3, one launch (start us, length us, event | category | flops | bytes accessed | tf_op | source)
XLA Modules:
  0.0 31.2 jit_solution(14643462530372895595)
XLA Ops:
  0.0 0.0 copy-start
  0.0 1.0 %split_states.1 = (bf16[16,1664]{1,0:T(8,128)(2,1)S(1)}, bf16[16,1664]{1,0:T(8,128)(2,1)S(1)}, bf16[16,1664]{1,0:T(8,128)(2,1)S(1)}, bf16[16,1664]{1,0:T(8,128)(2,1)S(1)}, s32[1,16]{1,0:T(1,128)S(1)}) custom-call(bf16[16,6144]{1,0:T(8,128)(2,1)} %states_ref.1, s32[4,16]{1,0:T(4,128)} %bitcast.8, s32[1,16]{1,0:T(1,128)} %union_ref.1), custom_call_target="tpu_custom_call" | custom-call | tf_op jit(solution)/shard_map/split_states/pallas_call | solution.py:181
  1.0 2.4 %collective-permute-start = (bf16[16,1664]{1,0:T(8,128)(2,1)S(1)}, bf16[16,1664]{1,0:T(8,128)(2,1)S(1)}, u32[]{:S(2)}, u32[]{:S(2)}) collective-permute-start(bf16[16,1664]{1,0:T(8,128)(2,1)S(1)} %get-tuple-element.16), channel_id=1, source_target_pairs={{0,8},{4,12},{8,0},{12,4},{1,9},{5,13},{9,1},{13,5},{2,10},{6,14},... | collective-permute-start | bytes 159752 | tf_op jit(solution)/shard_map/ppermute | solution.py:194
  3.4 1.1 %collective-permute-start.1 = (bf16[16,1664]{1,0:T(8,128)(2,1)S(1)}, bf16[16,1664]{1,0:T(8,128)(2,1)S(1)}, u32[]{:S(2)}, u32[]{:S(2)}) collective-permute-start(bf16[16,1664]{1,0:T(8,128)(2,1)S(1)} %get-tuple-element.17), channel_id=1, source_target_pairs={{0,12},{4,8},{8,4},{12,0},{1,13},{5,9},{9,5},{13,1},{2,14},{6,10},... | collective-permute-start | bytes 159752 | tf_op jit(solution)/shard_map/ppermute | solution.py:194
  4.5 0.2 collective-permute-start.2
  4.7 3.6 %gather_in.1.refs_4_ = bf16[1536,2048]{1,0:T(8,128)(2,1)S(1)} custom-call(s32[16]{0:T(128)S(1)} %bitcast.6, bf16[1536,6144]{1,0:T(8,128)(2,1)} %weight_ref.2), custom_call_target="tpu_custom_call" | custom-call | bytes 12582912 | tf_op jit(solution)/shard_map/gather_in/pallas_call | solution.py:85
  8.3 0.0 copy-start.1
  8.3 0.0 collective-permute-done.refs_0_
  8.4 0.0 collective-permute-done.1.refs_1_
  8.4 0.0 collective-permute-done.2.refs_2_
  8.4 1.3 %first_dot.1 = (bf16[64,512]{1,0:T(8,128)(2,1)S(1)}, f32[64,128]{1,0:T(8,128)S(1)}) custom-call(bf16[16,1664]{1,0:T(8,128)(2,1)S(1)} %collective-permute-done.refs_0_, bf16[16,1664]{1,0:T(8,128)(2,1)S(1)} %collective-permute-done.1.refs_1_, bf16[16,1664]{1,0:T(8,128)(2,1)S(1)} %collective-permute-done.2.refs_2_, ...), custom_call_target="tpu_custom_call" | custom-call | tf_op jit(solution)/shard_map/first_dot/pallas_call | solution.py:198
  9.7 2.5 %collective-permute-start.5 = (bf16[64,512]{1,0:T(8,128)(2,1)S(1)}, bf16[64,512]{1,0:T(8,128)(2,1)S(1)}, u32[]{:S(2)}, u32[]{:S(2)}) collective-permute-start(bf16[64,512]{1,0:T(8,128)(2,1)S(1)} %get-tuple-element.23.refs_3_), channel_id=1, source_target_pairs={{0,8},{4,12},{8,0},{12,4},{1,9},{5,13},{9,1},{13,5},{2,10},{6,14},... | collective-permute-start | bytes 196616 | tf_op jit(solution)/shard_map/ppermute | solution.py:211
  12.2 0.2 collective-permute-start.4
  12.4 1.1 %collective-permute-start.3 = (bf16[64,512]{1,0:T(8,128)(2,1)S(1)}, bf16[64,512]{1,0:T(8,128)(2,1)S(1)}, u32[]{:S(2)}, u32[]{:S(2)}) collective-permute-start(bf16[64,512]{1,0:T(8,128)(2,1)S(1)} %get-tuple-element.23.refs_3_), channel_id=1, source_target_pairs={{0,12},{4,8},{8,4},{12,0},{1,13},{5,9},{9,5},{13,1},{2,14},{6,10},... | collective-permute-start | bytes 196616 | tf_op jit(solution)/shard_map/ppermute | solution.py:211
  13.5 0.0 copy-done
  13.5 3.5 %gather_out.1 = (bf16[2048,1536]{1,0:T(8,128)(2,1)S(1)}, f32[16,128]{1,0:T(8,128)S(1)}) custom-call(s32[16]{0:T(128)S(1)} %bitcast.7, bf16[6144,1536]{1,0:T(8,128)(2,1)} %weight_ref.3, f32[48,128]{1,0:T(8,128)S(1)} %bitcast.5), custom_call_target="tpu_custom_call" | custom-call | bytes 12582912 | tf_op jit(solution)/shard_map/gather_out/pallas_call | solution.py:85
  16.9 0.0 collective-permute-done.5.refs_2_
  17.0 0.0 collective-permute-done.4.refs_1_
  17.0 0.9 %collective-permute-done.3.refs_0_ = bf16[64,512]{1,0:T(8,128)(2,1)S(1)} collective-permute-done((bf16[64,512]{1,0:T(8,128)(2,1)S(1)}, bf16[64,512]{1,0:T(8,128)(2,1)S(1)}, u32[]{:S(2)}, u32[]{:S(2)}) %collective-permute-start.3) | collective-permute-done | bytes 65568 | tf_op jit(solution)/shard_map/ppermute | solution.py:211
  17.9 1.3 %second_dot.1 = (f32[32,1536]{1,0:T(8,128)S(1)}, f32[32,1536]{1,0:T(8,128)S(1)}) custom-call(f32[64,128]{1,0:T(8,128)S(1)} %get-tuple-element.21.ids_ref, f32[16,128]{1,0:T(8,128)S(1)} %get-tuple-element.22.bias_ref, bf16[64,512]{1,0:T(8,128)(2,1)S(1)} %collective-permute-done.3.refs_0_, bf16[64,512]{1,0:T(8,128)(2,1)S(1)} %collective-permute-done.4.refs_1_, ...), custom_call_target="tpu_custom_call" | custom-call | tf_op jit(solution)/shard_map/second_dot/pallas_call | solution.py:215
  19.2 3.1 %collective-permute-start.6 = (f32[32,1536]{1,0:T(8,128)S(1)}, f32[32,1536]{1,0:T(8,128)S(1)}, u32[]{:S(2)}, u32[]{:S(2)}) collective-permute-start(f32[32,1536]{1,0:T(8,128)S(1)} %get-tuple-element.26), channel_id=1, source_target_pairs={{0,1},{1,0},{2,3},{3,2},{4,5},{5,4},{6,7},{7,6},{8,9},{9,8},{10,11... | collective-permute-start | bytes 589832 | tf_op jit(solution)/shard_map/ppermute | solution.py:226
  22.3 1.1 %collective-permute-done.6 = f32[32,1536]{1,0:T(8,128)S(1)} collective-permute-done((f32[32,1536]{1,0:T(8,128)S(1)}, f32[32,1536]{1,0:T(8,128)S(1)}, u32[]{:S(2)}, u32[]{:S(2)}) %collective-permute-start.6) | collective-permute-done | bytes 196640 | tf_op jit(solution)/shard_map/ppermute | solution.py:226
  23.4 0.6 %collective-permute-start.7 = (bf16[16,1536]{1,0:T(8,128)(2,1)S(1)}, bf16[16,1536]{1,0:T(8,128)(2,1)S(1)}, u32[]{:S(2)}, u32[]{:S(2)}) collective-permute-start(bf16[16,1536]{1,0:T(8,128)(2,1)S(1)} %get-tuple-element.27), channel_id=1, source_target_pairs={{0,8},{1,12},{2,4},{3,0},{4,5},{5,9},{6,13},{7,1},{8,10},{9,2},{10... | collective-permute-start | bytes 147464 | tf_op jit(solution)/shard_map/ppermute | solution.py:235
  23.9 4.0 %collective-permute-start.8 = (bf16[16,1536]{1,0:T(8,128)(2,1)S(1)}, bf16[16,1536]{1,0:T(8,128)(2,1)S(1)}, u32[]{:S(2)}, u32[]{:S(2)}) collective-permute-start(bf16[16,1536]{1,0:T(8,128)(2,1)S(1)} %get-tuple-element.28), channel_id=1, source_target_pairs={{0,4},{1,0},{2,8},{3,12},{4,13},{5,1},{6,5},{7,9},{8,14},{9,6},{10... | collective-permute-start | bytes 147464 | tf_op jit(solution)/shard_map/ppermute | solution.py:235
  28.0 1.1 %collective-permute-done.7 = bf16[16,1536]{1,0:T(8,128)(2,1)S(1)} collective-permute-done((bf16[16,1536]{1,0:T(8,128)(2,1)S(1)}, bf16[16,1536]{1,0:T(8,128)(2,1)S(1)}, u32[]{:S(2)}, u32[]{:S(2)}) %collective-permute-start.7) | collective-permute-done | bytes 49184 | tf_op jit(solution)/shard_map/ppermute | solution.py:235
  29.1 1.5 %collective-permute-done.8 = bf16[16,1536]{1,0:T(8,128)(2,1)S(1)} collective-permute-done((bf16[16,1536]{1,0:T(8,128)(2,1)S(1)}, bf16[16,1536]{1,0:T(8,128)(2,1)S(1)}, u32[]{:S(2)}, u32[]{:S(2)}) %collective-permute-start.8) | collective-permute-done | bytes 49184 | tf_op jit(solution)/shard_map/ppermute | solution.py:235
  30.6 0.0 copy-done.1
  30.6 0.6 %add_convert_fusion.1 = bf16[16,1536]{1,0:T(8,128)(2,1)} fusion(bf16[16,1536]{1,0:T(8,128)(2,1)S(1)} %collective-permute-done.8, bf16[16,1536]{1,0:T(8,128)(2,1)S(1)} %collective-permute-done.7, f32[1536]{0:T(1024)S(1)} %copy-done.1), kind=kLoop, calls=%fused_computation.1 | loop fusion | flops 122880 | bytes 153600 | tf_op jit(solution)/shard_map/convert_element_type | solution.py:238
  (2 shorter events, 0.0 us)
Async XLA Ops:
  0.0 13.5 %copy-start = (f32[6144]{0:T(1024)S(1)}, f32[6144]{0:T(1024)}, u32[]{:S(2)}) copy-start(f32[6144]{0:T(1024)} %param.9) | copy-start | bytes 73732
  1.0 7.3 %collective-permute-start = (bf16[16,1664]{1,0:T(8,128)(2,1)S(1)}, bf16[16,1664]{1,0:T(8,128)(2,1)S(1)}, u32[]{:S(2)}, u32[]{:S(2)}) collective-permute-start(bf16[16,1664]{1,0:T(8,128)(2,1)S(1)} %get-tuple-element.16), channel_id=1, source_target_pairs={{0,8},{4,12},{8,0},{12,4},{1,9},{5,13},{9,1},{13,5},{2,10},{6,14},... | collective-permute-start | bytes 159752 | tf_op jit(solution)/shard_map/ppermute | solution.py:194
  3.4 5.0 %collective-permute-start.1 = (bf16[16,1664]{1,0:T(8,128)(2,1)S(1)}, bf16[16,1664]{1,0:T(8,128)(2,1)S(1)}, u32[]{:S(2)}, u32[]{:S(2)}) collective-permute-start(bf16[16,1664]{1,0:T(8,128)(2,1)S(1)} %get-tuple-element.17), channel_id=1, source_target_pairs={{0,12},{4,8},{8,4},{12,0},{1,13},{5,9},{9,5},{13,1},{2,14},{6,10},... | collective-permute-start | bytes 159752 | tf_op jit(solution)/shard_map/ppermute | solution.py:194
  4.5 3.9 %collective-permute-start.2 = (bf16[16,1664]{1,0:T(8,128)(2,1)S(1)}, bf16[16,1664]{1,0:T(8,128)(2,1)S(1)}, u32[]{:S(2)}, u32[]{:S(2)}) collective-permute-start(bf16[16,1664]{1,0:T(8,128)(2,1)S(1)} %get-tuple-element.18), channel_id=1, source_target_pairs={{0,4},{4,0},{8,12},{12,8},{1,5},{5,1},{9,13},{13,9},{2,6},{6,2},{1... | collective-permute-start | bytes 159752 | tf_op jit(solution)/shard_map/ppermute | solution.py:194
  8.3 22.2 %copy-start.1 = (f32[1536]{0:T(1024)S(1)}, f32[1536]{0:T(1024)}, u32[]{:S(2)}) copy-start(f32[1536]{0:T(1024)} %param.11) | copy-start | bytes 18436
  9.7 7.3 %collective-permute-start.5 = (bf16[64,512]{1,0:T(8,128)(2,1)S(1)}, bf16[64,512]{1,0:T(8,128)(2,1)S(1)}, u32[]{:S(2)}, u32[]{:S(2)}) collective-permute-start(bf16[64,512]{1,0:T(8,128)(2,1)S(1)} %get-tuple-element.23.refs_3_), channel_id=1, source_target_pairs={{0,8},{4,12},{8,0},{12,4},{1,9},{5,13},{9,1},{13,5},{2,10},{6,14},... | collective-permute-start | bytes 196616 | tf_op jit(solution)/shard_map/ppermute | solution.py:211
  12.2 4.7 %collective-permute-start.4 = (bf16[64,512]{1,0:T(8,128)(2,1)S(1)}, bf16[64,512]{1,0:T(8,128)(2,1)S(1)}, u32[]{:S(2)}, u32[]{:S(2)}) collective-permute-start(bf16[64,512]{1,0:T(8,128)(2,1)S(1)} %get-tuple-element.23.refs_3_), channel_id=1, source_target_pairs={{0,4},{4,0},{8,12},{12,8},{1,5},{5,1},{9,13},{13,9},{2,6},{6,2},{1... | collective-permute-start | bytes 196616 | tf_op jit(solution)/shard_map/ppermute | solution.py:211
  12.4 5.5 %collective-permute-start.3 = (bf16[64,512]{1,0:T(8,128)(2,1)S(1)}, bf16[64,512]{1,0:T(8,128)(2,1)S(1)}, u32[]{:S(2)}, u32[]{:S(2)}) collective-permute-start(bf16[64,512]{1,0:T(8,128)(2,1)S(1)} %get-tuple-element.23.refs_3_), channel_id=1, source_target_pairs={{0,12},{4,8},{8,4},{12,0},{1,13},{5,9},{9,5},{13,1},{2,14},{6,10},... | collective-permute-start | bytes 196616 | tf_op jit(solution)/shard_map/ppermute | solution.py:211
  19.2 4.1 %collective-permute-start.6 = (f32[32,1536]{1,0:T(8,128)S(1)}, f32[32,1536]{1,0:T(8,128)S(1)}, u32[]{:S(2)}, u32[]{:S(2)}) collective-permute-start(f32[32,1536]{1,0:T(8,128)S(1)} %get-tuple-element.26), channel_id=1, source_target_pairs={{0,1},{1,0},{2,3},{3,2},{4,5},{5,4},{6,7},{7,6},{8,9},{9,8},{10,11... | collective-permute-start | bytes 589832 | tf_op jit(solution)/shard_map/ppermute | solution.py:226
  23.4 5.7 %collective-permute-start.7 = (bf16[16,1536]{1,0:T(8,128)(2,1)S(1)}, bf16[16,1536]{1,0:T(8,128)(2,1)S(1)}, u32[]{:S(2)}, u32[]{:S(2)}) collective-permute-start(bf16[16,1536]{1,0:T(8,128)(2,1)S(1)} %get-tuple-element.27), channel_id=1, source_target_pairs={{0,8},{1,12},{2,4},{3,0},{4,5},{5,9},{6,13},{7,1},{8,10},{9,2},{10... | collective-permute-start | bytes 147464 | tf_op jit(solution)/shard_map/ppermute | solution.py:235
  23.9 6.6 %collective-permute-start.8 = (bf16[16,1536]{1,0:T(8,128)(2,1)S(1)}, bf16[16,1536]{1,0:T(8,128)(2,1)S(1)}, u32[]{:S(2)}, u32[]{:S(2)}) collective-permute-start(bf16[16,1536]{1,0:T(8,128)(2,1)S(1)} %get-tuple-element.28), channel_id=1, source_target_pairs={{0,4},{1,0},{2,8},{3,12},{4,13},{5,1},{6,5},{7,9},{8,14},{9,6},{10... | collective-permute-start | bytes 147464 | tf_op jit(solution)/shard_map/ppermute | solution.py:235

commit v7 on v6

--- a/solution.py
+++ b/solution.py
@@ -157,8 +157,8 @@
 WAY_HOME = (
     ((2, 1), (3, 0), (1, 2), (0, 3)),
     ((1, 3), (2, 0), (3, 1), (0, 2)),
-    ((2, 3), (0, 1), (3, 2), (1, 0)),
-    ((3, 2), (0, 1), (2, 3), (1, 0)),
+    ((1, 0), (3, 2), (0, 1), (2, 3)),
+    ((1, 3), (2, 0), (3, 1), (0, 2)),
 )
 
 

time: 31.7 us -> 30.4 us (0.959); the launches traced: 31.2 us -> 30.2 us
  starting transfers between devices: 15.1 us -> 13 us
  waiting for transfers between devices: 4.6 us -> 5.75 us
    ppermute x2, starting transfers between devices: 4.58 us -> 2.47 us  [fast(): lax.ppermute(both[k * rows:(k + 1) * rows], ('store', 'tensor'), home(k))]
    ppermute x2, waiting for transfers between devices: 2.61 us -> 3.76 us  [fast(): lax.ppermute(both[k * rows:(k + 1) * rows], ('store', 'tensor'), home(k))]
where the time goes in v7:
time: 30.4 us; the launch traced here: 30.2 us
  starting transfers between devices  13 us (43%)
  Pallas kernels  10.7 us (35%)
  waiting for transfers between devices  5.75 us (19%)
  other arithmetic  0.66 us (2%)
    pallas_call x2, Pallas kernels, gather(): pl.pallas_call(functools.partial(gather_kernel, by_column), out_shape=[VM...  7.09 us
    ppermute x3, starting transfers between devices, fast(): lax.ppermute(pre, 'store', over_store(k))  3.8 us
    ppermute x2, waiting for transfers between devices, fast(): lax.ppermute(both[k * rows:(k + 1) * rows], ('store', 'tensor'), home(k))  3.76 us
    ppermute x3, starting transfers between devices, fast(): lax.ppermute(chunks[k], 'store', over_store(k))  3.67 us
    ppermute x1, starting transfers between devices, fast(): both = (keep + lax.ppermute(send, 'tensor', pair)).astype(BF16)  3.06 us
    ppermute x2, starting transfers between devices, fast(): lax.ppermute(both[k * rows:(k + 1) * rows], ('store', 'tensor'), home(k))  2.47 us
    pallas_call x1, Pallas kernels, fast(): pl.pallas_call(functools.partial(second_kernel, count, slots), out_shape=...  1.31 us
    pallas_call x1, Pallas kernels, fast(): pl.pallas_call(functools.partial(first_kernel, count, slots), out_shape=[...  1.3 us
  transfers between devices with their start and end apart: 9, of which 4 were waited for; matrix products, arithmetic and copies ran while one was open for 0% of the time, Pallas kernels for 23%

profile of v7, /device:TPU:3, one launch (start us, length us, event | category | flops | bytes accessed | tf_op | source)
XLA Modules:
  0.0 30.2 jit_solution(10846061914434622024)
XLA Ops:
  0.0 0.0 copy-start
  0.0 1.0 %split_states.1 = (bf16[16,1664]{1,0:T(8,128)(2,1)S(1)}, bf16[16,1664]{1,0:T(8,128)(2,1)S(1)}, bf16[16,1664]{1,0:T(8,128)(2,1)S(1)}, bf16[16,1664]{1,0:T(8,128)(2,1)S(1)}, s32[1,16]{1,0:T(1,128)S(1)}) custom-call(bf16[16,6144]{1,0:T(8,128)(2,1)} %states_ref.1, s32[4,16]{1,0:T(4,128)} %bitcast.8, s32[1,16]{1,0:T(1,128)} %union_ref.1), custom_call_target="tpu_custom_call" | custom-call | tf_op jit(solution)/shard_map/split_states/pallas_call | solution.py:181
  1.0 2.4 %collective-permute-start = (bf16[16,1664]{1,0:T(8,128)(2,1)S(1)}, bf16[16,1664]{1,0:T(8,128)(2,1)S(1)}, u32[]{:S(2)}, u32[]{:S(2)}) collective-permute-start(bf16[16,1664]{1,0:T(8,128)(2,1)S(1)} %get-tuple-element.16), channel_id=1, source_target_pairs={{0,8},{4,12},{8,0},{12,4},{1,9},{5,13},{9,1},{13,5},{2,10},{6,14},... | collective-permute-start | bytes 159752 | tf_op jit(solution)/shard_map/ppermute | solution.py:194
  3.4 1.1 %collective-permute-start.1 = (bf16[16,1664]{1,0:T(8,128)(2,1)S(1)}, bf16[16,1664]{1,0:T(8,128)(2,1)S(1)}, u32[]{:S(2)}, u32[]{:S(2)}) collective-permute-start(bf16[16,1664]{1,0:T(8,128)(2,1)S(1)} %get-tuple-element.17), channel_id=1, source_target_pairs={{0,12},{4,8},{8,4},{12,0},{1,13},{5,9},{9,5},{13,1},{2,14},{6,10},... | collective-permute-start | bytes 159752 | tf_op jit(solution)/shard_map/ppermute | solution.py:194
  4.5 0.2 collective-permute-start.2
  4.7 3.6 %gather_in.1.refs_4_ = bf16[1536,2048]{1,0:T(8,128)(2,1)S(1)} custom-call(s32[16]{0:T(128)S(1)} %bitcast.6, bf16[1536,6144]{1,0:T(8,128)(2,1)} %weight_ref.2), custom_call_target="tpu_custom_call" | custom-call | bytes 12582912 | tf_op jit(solution)/shard_map/gather_in/pallas_call | solution.py:85
  8.3 0.0 copy-start.1
  8.3 0.0 collective-permute-done.refs_0_
  8.4 0.0 collective-permute-done.1.refs_1_
  8.4 0.0 collective-permute-done.2.refs_2_
  8.4 1.3 %first_dot.1 = (bf16[64,512]{1,0:T(8,128)(2,1)S(1)}, f32[64,128]{1,0:T(8,128)S(1)}) custom-call(bf16[16,1664]{1,0:T(8,128)(2,1)S(1)} %collective-permute-done.refs_0_, bf16[16,1664]{1,0:T(8,128)(2,1)S(1)} %collective-permute-done.1.refs_1_, bf16[16,1664]{1,0:T(8,128)(2,1)S(1)} %collective-permute-done.2.refs_2_, ...), custom_call_target="tpu_custom_call" | custom-call | tf_op jit(solution)/shard_map/first_dot/pallas_call | solution.py:198
  9.7 2.5 %collective-permute-start.5 = (bf16[64,512]{1,0:T(8,128)(2,1)S(1)}, bf16[64,512]{1,0:T(8,128)(2,1)S(1)}, u32[]{:S(2)}, u32[]{:S(2)}) collective-permute-start(bf16[64,512]{1,0:T(8,128)(2,1)S(1)} %get-tuple-element.23.refs_3_), channel_id=1, source_target_pairs={{0,8},{4,12},{8,0},{12,4},{1,9},{5,13},{9,1},{13,5},{2,10},{6,14},... | collective-permute-start | bytes 196616 | tf_op jit(solution)/shard_map/ppermute | solution.py:211
  12.2 0.2 collective-permute-start.4
  12.4 1.1 %collective-permute-start.3 = (bf16[64,512]{1,0:T(8,128)(2,1)S(1)}, bf16[64,512]{1,0:T(8,128)(2,1)S(1)}, u32[]{:S(2)}, u32[]{:S(2)}) collective-permute-start(bf16[64,512]{1,0:T(8,128)(2,1)S(1)} %get-tuple-element.23.refs_3_), channel_id=1, source_target_pairs={{0,12},{4,8},{8,4},{12,0},{1,13},{5,9},{9,5},{13,1},{2,14},{6,10},... | collective-permute-start | bytes 196616 | tf_op jit(solution)/shard_map/ppermute | solution.py:211
  13.5 0.0 copy-done
  13.5 3.5 %gather_out.1 = (bf16[2048,1536]{1,0:T(8,128)(2,1)S(1)}, f32[16,128]{1,0:T(8,128)S(1)}) custom-call(s32[16]{0:T(128)S(1)} %bitcast.7, bf16[6144,1536]{1,0:T(8,128)(2,1)} %weight_ref.3, f32[48,128]{1,0:T(8,128)S(1)} %bitcast.5), custom_call_target="tpu_custom_call" | custom-call | bytes 12582912 | tf_op jit(solution)/shard_map/gather_out/pallas_call | solution.py:85
  16.9 0.0 collective-permute-done.5.refs_2_
  17.0 0.0 collective-permute-done.4.refs_1_
  17.0 0.9 %collective-permute-done.3.refs_0_ = bf16[64,512]{1,0:T(8,128)(2,1)S(1)} collective-permute-done((bf16[64,512]{1,0:T(8,128)(2,1)S(1)}, bf16[64,512]{1,0:T(8,128)(2,1)S(1)}, u32[]{:S(2)}, u32[]{:S(2)}) %collective-permute-start.3) | collective-permute-done | bytes 65568 | tf_op jit(solution)/shard_map/ppermute | solution.py:211
  17.9 1.3 %second_dot.1 = (f32[32,1536]{1,0:T(8,128)S(1)}, f32[32,1536]{1,0:T(8,128)S(1)}) custom-call(f32[64,128]{1,0:T(8,128)S(1)} %get-tuple-element.21.ids_ref, f32[16,128]{1,0:T(8,128)S(1)} %get-tuple-element.22.bias_ref, bf16[64,512]{1,0:T(8,128)(2,1)S(1)} %collective-permute-done.3.refs_0_, bf16[64,512]{1,0:T(8,128)(2,1)S(1)} %collective-permute-done.4.refs_1_, ...), custom_call_target="tpu_custom_call" | custom-call | tf_op jit(solution)/shard_map/second_dot/pallas_call | solution.py:215
  19.2 3.1 %collective-permute-start.6 = (f32[32,1536]{1,0:T(8,128)S(1)}, f32[32,1536]{1,0:T(8,128)S(1)}, u32[]{:S(2)}, u32[]{:S(2)}) collective-permute-start(f32[32,1536]{1,0:T(8,128)S(1)} %get-tuple-element.26), channel_id=1, source_target_pairs={{0,1},{1,0},{2,3},{3,2},{4,5},{5,4},{6,7},{7,6},{8,9},{9,8},{10,11... | collective-permute-start | bytes 589832 | tf_op jit(solution)/shard_map/ppermute | solution.py:226
  22.3 1.1 %collective-permute-done.6 = f32[32,1536]{1,0:T(8,128)S(1)} collective-permute-done((f32[32,1536]{1,0:T(8,128)S(1)}, f32[32,1536]{1,0:T(8,128)S(1)}, u32[]{:S(2)}, u32[]{:S(2)}) %collective-permute-start.6) | collective-permute-done | bytes 196640 | tf_op jit(solution)/shard_map/ppermute | solution.py:226
  23.4 0.6 %collective-permute-start.7 = (bf16[16,1536]{1,0:T(8,128)(2,1)S(1)}, bf16[16,1536]{1,0:T(8,128)(2,1)S(1)}, u32[]{:S(2)}, u32[]{:S(2)}) collective-permute-start(bf16[16,1536]{1,0:T(8,128)(2,1)S(1)} %get-tuple-element.27), channel_id=1, source_target_pairs={{0,8},{1,12},{2,4},{3,0},{4,5},{5,9},{6,13},{7,1},{8,6},{9,14},{10... | collective-permute-start | bytes 147464 | tf_op jit(solution)/shard_map/ppermute | solution.py:235
  23.9 1.9 %collective-permute-start.8 = (bf16[16,1536]{1,0:T(8,128)(2,1)S(1)}, bf16[16,1536]{1,0:T(8,128)(2,1)S(1)}, u32[]{:S(2)}, u32[]{:S(2)}) collective-permute-start(bf16[16,1536]{1,0:T(8,128)(2,1)S(1)} %get-tuple-element.28), channel_id=1, source_target_pairs={{0,4},{1,0},{2,8},{3,12},{4,13},{5,1},{6,5},{7,9},{8,2},{9,10},{10... | collective-permute-start | bytes 147464 | tf_op jit(solution)/shard_map/ppermute | solution.py:235
  25.8 2.4 %collective-permute-done.7 = bf16[16,1536]{1,0:T(8,128)(2,1)S(1)} collective-permute-done((bf16[16,1536]{1,0:T(8,128)(2,1)S(1)}, bf16[16,1536]{1,0:T(8,128)(2,1)S(1)}, u32[]{:S(2)}, u32[]{:S(2)}) %collective-permute-start.7) | collective-permute-done | bytes 49184 | tf_op jit(solution)/shard_map/ppermute | solution.py:235
  28.3 1.3 %collective-permute-done.8 = bf16[16,1536]{1,0:T(8,128)(2,1)S(1)} collective-permute-done((bf16[16,1536]{1,0:T(8,128)(2,1)S(1)}, bf16[16,1536]{1,0:T(8,128)(2,1)S(1)}, u32[]{:S(2)}, u32[]{:S(2)}) %collective-permute-start.8) | collective-permute-done | bytes 49184 | tf_op jit(solution)/shard_map/ppermute | solution.py:235
  29.6 0.0 copy-done.1
  29.6 0.6 %add_convert_fusion.1 = bf16[16,1536]{1,0:T(8,128)(2,1)} fusion(bf16[16,1536]{1,0:T(8,128)(2,1)S(1)} %collective-permute-done.8, bf16[16,1536]{1,0:T(8,128)(2,1)S(1)} %collective-permute-done.7, f32[1536]{0:T(1024)S(1)} %copy-done.1), kind=kLoop, calls=%fused_computation.1 | loop fusion | flops 122880 | bytes 153600 | tf_op jit(solution)/shard_map/convert_element_type | solution.py:238
  (2 shorter events, 0.0 us)
Async XLA Ops:
  0.0 13.5 %copy-start = (f32[6144]{0:T(1024)S(1)}, f32[6144]{0:T(1024)}, u32[]{:S(2)}) copy-start(f32[6144]{0:T(1024)} %param.9) | copy-start | bytes 73732
  1.0 7.3 %collective-permute-start = (bf16[16,1664]{1,0:T(8,128)(2,1)S(1)}, bf16[16,1664]{1,0:T(8,128)(2,1)S(1)}, u32[]{:S(2)}, u32[]{:S(2)}) collective-permute-start(bf16[16,1664]{1,0:T(8,128)(2,1)S(1)} %get-tuple-element.16), channel_id=1, source_target_pairs={{0,8},{4,12},{8,0},{12,4},{1,9},{5,13},{9,1},{13,5},{2,10},{6,14},... | collective-permute-start | bytes 159752 | tf_op jit(solution)/shard_map/ppermute | solution.py:194
  3.4 5.0 %collective-permute-start.1 = (bf16[16,1664]{1,0:T(8,128)(2,1)S(1)}, bf16[16,1664]{1,0:T(8,128)(2,1)S(1)}, u32[]{:S(2)}, u32[]{:S(2)}) collective-permute-start(bf16[16,1664]{1,0:T(8,128)(2,1)S(1)} %get-tuple-element.17), channel_id=1, source_target_pairs={{0,12},{4,8},{8,4},{12,0},{1,13},{5,9},{9,5},{13,1},{2,14},{6,10},... | collective-permute-start | bytes 159752 | tf_op jit(solution)/shard_map/ppermute | solution.py:194
  4.5 3.9 %collective-permute-start.2 = (bf16[16,1664]{1,0:T(8,128)(2,1)S(1)}, bf16[16,1664]{1,0:T(8,128)(2,1)S(1)}, u32[]{:S(2)}, u32[]{:S(2)}) collective-permute-start(bf16[16,1664]{1,0:T(8,128)(2,1)S(1)} %get-tuple-element.18), channel_id=1, source_target_pairs={{0,4},{4,0},{8,12},{12,8},{1,5},{5,1},{9,13},{13,9},{2,6},{6,2},{1... | collective-permute-start | bytes 159752 | tf_op jit(solution)/shard_map/ppermute | solution.py:194
  8.3 21.3 %copy-start.1 = (f32[1536]{0:T(1024)S(1)}, f32[1536]{0:T(1024)}, u32[]{:S(2)}) copy-start(f32[1536]{0:T(1024)} %param.11) | copy-start | bytes 18436
  9.7 7.3 %collective-permute-start.5 = (bf16[64,512]{1,0:T(8,128)(2,1)S(1)}, bf16[64,512]{1,0:T(8,128)(2,1)S(1)}, u32[]{:S(2)}, u32[]{:S(2)}) collective-permute-start(bf16[64,512]{1,0:T(8,128)(2,1)S(1)} %get-tuple-element.23.refs_3_), channel_id=1, source_target_pairs={{0,8},{4,12},{8,0},{12,4},{1,9},{5,13},{9,1},{13,5},{2,10},{6,14},... | collective-permute-start | bytes 196616 | tf_op jit(solution)/shard_map/ppermute | solution.py:211
  12.2 4.7 %collective-permute-start.4 = (bf16[64,512]{1,0:T(8,128)(2,1)S(1)}, bf16[64,512]{1,0:T(8,128)(2,1)S(1)}, u32[]{:S(2)}, u32[]{:S(2)}) collective-permute-start(bf16[64,512]{1,0:T(8,128)(2,1)S(1)} %get-tuple-element.23.refs_3_), channel_id=1, source_target_pairs={{0,4},{4,0},{8,12},{12,8},{1,5},{5,1},{9,13},{13,9},{2,6},{6,2},{1... | collective-permute-start | bytes 196616 | tf_op jit(solution)/shard_map/ppermute | solution.py:211
  12.4 5.5 %collective-permute-start.3 = (bf16[64,512]{1,0:T(8,128)(2,1)S(1)}, bf16[64,512]{1,0:T(8,128)(2,1)S(1)}, u32[]{:S(2)}, u32[]{:S(2)}) collective-permute-start(bf16[64,512]{1,0:T(8,128)(2,1)S(1)} %get-tuple-element.23.refs_3_), channel_id=1, source_target_pairs={{0,12},{4,8},{8,4},{12,0},{1,13},{5,9},{9,5},{13,1},{2,14},{6,10},... | collective-permute-start | bytes 196616 | tf_op jit(solution)/shard_map/ppermute | solution.py:211
  19.2 4.1 %collective-permute-start.6 = (f32[32,1536]{1,0:T(8,128)S(1)}, f32[32,1536]{1,0:T(8,128)S(1)}, u32[]{:S(2)}, u32[]{:S(2)}) collective-permute-start(f32[32,1536]{1,0:T(8,128)S(1)} %get-tuple-element.26), channel_id=1, source_target_pairs={{0,1},{1,0},{2,3},{3,2},{4,5},{5,4},{6,7},{7,6},{8,9},{9,8},{10,11... | collective-permute-start | bytes 589832 | tf_op jit(solution)/shard_map/ppermute | solution.py:226
  23.4 4.9 %collective-permute-start.7 = (bf16[16,1536]{1,0:T(8,128)(2,1)S(1)}, bf16[16,1536]{1,0:T(8,128)(2,1)S(1)}, u32[]{:S(2)}, u32[]{:S(2)}) collective-permute-start(bf16[16,1536]{1,0:T(8,128)(2,1)S(1)} %get-tuple-element.27), channel_id=1, source_target_pairs={{0,8},{1,12},{2,4},{3,0},{4,5},{5,9},{6,13},{7,1},{8,6},{9,14},{10... | collective-permute-start | bytes 147464 | tf_op jit(solution)/shard_map/ppermute | solution.py:235
  23.9 5.7 %collective-permute-start.8 = (bf16[16,1536]{1,0:T(8,128)(2,1)S(1)}, bf16[16,1536]{1,0:T(8,128)(2,1)S(1)}, u32[]{:S(2)}, u32[]{:S(2)}) collective-permute-start(bf16[16,1536]{1,0:T(8,128)(2,1)S(1)} %get-tuple-element.28), channel_id=1, source_target_pairs={{0,4},{1,0},{2,8},{3,12},{4,13},{5,1},{6,5},{7,9},{8,2},{9,10},{10... | collective-permute-start | bytes 147464 | tf_op jit(solution)/shard_map/ppermute | solution.py:235

commit v8 on v7

--- a/solution.py
+++ b/solution.py
@@ -11,15 +11,15 @@
 BF16 = jnp.bfloat16
 F32 = jnp.float32
 VMEM = pltpu.VMEM
-SMEM = pltpu.SMEM
-
-
-ORDER = (2, 3, 1)
-ORDER_TWO = (3, 1, 2)
-
-
-def by_partner(refs, order=ORDER):
-    return [refs[(order + (0,)).index(k)] for k in range(len(refs))]
+
+
+ROUND_ONE = ((2, 3, 1), (2, 3, 1))
+ROUND_TWO = ((1, 2, 3), (3, 1, 2))
+
+
+def partner(order, turn):
+    odd = lax.axis_index("tensor") & 1
+    return odd * order[1][turn] + (1 - odd) * order[0][turn]
 
 
 def whole(space):
@@ -32,11 +32,12 @@
     ids_copy = pltpu.make_async_copy(ids_ref, ids, sems.at[count])
     ids_copy.start()
     copies = []
-    for k in list(range(1, count)) + [0]:
-        start = pl.multiple_of((me ^ k) * width, BLOCK)
+    for turn in range(count):
+        other = me ^ partner(ROUND_ONE, turn) if turn < count - 1 else me
+        start = pl.multiple_of(other * width, BLOCK)
         copies.append(
             pltpu.make_async_copy(
-                states_ref.at[:, pl.ds(start, width)], out_refs[k].at[:, :width], sems.at[k]
+                states_ref.at[:, pl.ds(start, width)], out_refs[turn].at[:, :width], sems.at[turn]
             )
         )
         copies[-1].start()
@@ -60,10 +61,10 @@
 def gather_kernel(by_column, union_ref, weight_ref, *refs):
     *bias_refs, sems = refs
     out_ref = bias_refs.pop(len(bias_refs) // 2)
-    union = union_ref.shape[0]
+    union = union_ref.shape[1]
     copies = []
     for u in range(union):
-        block = pl.ds(pl.multiple_of(union_ref[u] * BLOCK, BLOCK), BLOCK)
+        block = pl.ds(pl.multiple_of(union_ref[0, u] * BLOCK, BLOCK), BLOCK)
         place = pl.ds(u * BLOCK, BLOCK)
         if by_column:
             source, target = weight_ref.at[:, block], out_ref.at[:, place]
@@ -74,18 +75,18 @@
     if bias_refs:
         bias_ref, bias_out = bias_refs
         for u in range(union):
-            bias_out[u : u + 1, :] = bias_ref[pl.ds(union_ref[u], 1), :]
+            bias_out[u : u + 1, :] = bias_ref[pl.ds(union_ref[0, u], 1), :]
     for copy in copies:
         copy.wait()
 
 
 def gather(by_column, union_ids, weight, name, *bias):
-    union = union_ids.shape[0]
+    union = union_ids.shape[1]
     shape = (weight.shape[0], union * BLOCK) if by_column else (union * BLOCK, weight.shape[1])
     return pl.pallas_call(
         functools.partial(gather_kernel, by_column),
         out_shape=[VMEM(shape, BF16)] + [VMEM((union, BLOCK), F32)] * len(bias),
-        in_specs=[whole(SMEM), whole(pltpu.HBM)] + [whole(VMEM)] * len(bias),
+        in_specs=[whole(VMEM), whole(pltpu.HBM)] + [whole(VMEM)] * len(bias),
         out_specs=[whole(VMEM)] * (1 + len(bias)),
         scratch_shapes=[pltpu.SemaphoreType.DMA((union,))],
         compiler_params=pltpu.CompilerParams(vmem_limit_bytes=40 * 2**20),
@@ -95,13 +96,17 @@
 
 
 def first_kernel(count, slots, *refs):
-    chunk_refs = by_partner(refs[:count])
-    win_ref, pre_ref, ids_ref, dense = refs[count:]
+    chunk_refs = refs[:count]
+    win_ref, pre_ref, ids_ref, dense, chunks = refs[count:]
     width, total = win_ref.shape
     rows = chunk_refs[0].shape[0]
     union = total // BLOCK
-    states = jnp.concatenate([c[:, :width] for c in chunk_refs], axis=0)
-    ids = jnp.concatenate([c[:, width:] for c in chunk_refs], axis=0).astype(F32)
+    for turn in range(count - 1):
+        place = pl.multiple_of(partner(ROUND_ONE, turn) * rows, rows)
+        chunks[pl.ds(place, rows), :] = chunk_refs[turn][...]
+    chunks[:rows, :] = chunk_refs[count - 1][...]
+    states = chunks[:, :width]
+    ids = chunks[:, width:].astype(F32)
     ids_ref[...] = ids
     step = 2 * BLOCK
     for n in range(0, total, step):
@@ -117,7 +122,8 @@
 
 
 def second_kernel(count, slots, ids_ref, bias_ref, *refs):
-    part_refs = by_partner(refs[:count], ORDER_TWO)
+    part_refs = refs[:count]
+    partners = [partner(ROUND_TWO, turn) for turn in range(count - 1)] + [0]
     wout_ref = refs[count]
     keep_ref, send_ref, spread, terms = refs[count + 1 :]
     store, tensor = lax.axis_index("store"), lax.axis_index("tensor")
@@ -132,8 +138,8 @@
             cols = slice(k * BLOCK, (k + 1) * BLOCK)
             pres.append(
                 sum(
-                    p[(j ^ i) * rows : ((j ^ i) + 1) * rows, cols].astype(F32)
-                    for i, p in enumerate(part_refs)
+                    p[pl.ds(pl.multiple_of((j ^ k_of) * rows, rows), rows), cols].astype(F32)
+                    for k_of, p in zip(partners, part_refs)
                 )
             )
         for u in range(union):
@@ -186,12 +192,17 @@
         scratch_shapes=[VMEM((slots, rows), jnp.int32), pltpu.SemaphoreType.DMA((count + 2,))],
         name="split_states",
     )(states, jnp.transpose(block_lists, (1, 2, 0))[0], union_blocks)
-    union_ids = union_ids[0]
-
-    def over_store(k):
-        return [(i, i ^ k) for i in range(count)]
-
-    got = [lax.ppermute(chunks[k], "store", over_store(k)) for k in ORDER] + [chunks[0]]
+
+    def over_store(order, turn):
+        return [
+            (s * count + t, (s ^ order[t & 1][turn]) * count + t)
+            for s in range(count) for t in range(count)
+        ]
+
+    got = [
+        lax.ppermute(chunks[turn], ("store", "tensor"), over_store(ROUND_ONE, turn))
+        for turn in range(count - 1)
+    ] + [chunks[count - 1]]
 
     (win,) = gather(True, union_ids, weight_in, "gather_in")
 
@@ -203,12 +214,15 @@
         ],
         in_specs=[whole(VMEM)] * (count + 1),
         out_specs=[whole(VMEM)] * 2,
-        scratch_shapes=[VMEM((count * rows, total), F32)],
+        scratch_shapes=[VMEM((count * rows, total), F32), VMEM((count * rows, width + BLOCK), BF16)],
         compiler_params=pltpu.CompilerParams(vmem_limit_bytes=40 * 2**20),
         name="first_dot",
     )(*got, win)
 
-    parts = [lax.ppermute(pre, "store", over_store(k)) for k in ORDER_TWO] + [pre]
+    parts = [
+        lax.ppermute(pre, ("store", "tensor"), over_store(ROUND_TWO, turn))
+        for turn in range(count - 1)
+    ] + [pre]
 
     wout, bias = gather(False, union_ids, weight_out, "gather_out", bias_in.reshape(-1, BLOCK))
 

time: 30.4 us -> 29.9 us (0.984)
  Pallas kernels: 10.7 us -> 9.73 us
    ppermute x6, waiting for transfers between devices: 0.92 us -> 2.08 us  [the longest x3 1.68 us: fast(): lax.ppermute(pre, ('store', 'tensor'), over_store(ROUND_TWO, turn))]
    ppermute x1, starting transfers between devices: 3.06 us -> 1.93 us  [fast(): both = (keep + lax.ppermute(send, 'tensor', pair)).astype(BF16)]
    pallas_call x2, Pallas kernels: 7.09 us -> 6.11 us  [gather(): pl.pallas_call(functools.partial(gather_kernel, by_column), out_shape=[VM...]
    ppermute x2, starting transfers between devices: 2.47 us -> 3.46 us  [fast(): lax.ppermute(both[k * rows:(k + 1) * rows], ('store', 'tensor'), home(k))]
    ppermute x2, waiting for transfers between devices: 3.76 us -> 2.86 us  [fast(): lax.ppermute(both[k * rows:(k + 1) * rows], ('store', 'tensor'), home(k))]
  transfers between devices with their start and end apart: 9 -> 9, of which waited for: 4 -> 5; matrix products, arithmetic and copies ran while one was open for 0% -> 0% of each run, Pallas kernels for 23% -> 21%
where the time goes in v8:
time: 29.9 us; the launch traced here: 29.5 us
  starting transfers between devices  13 us (43%)
  Pallas kernels  9.73 us (33%)
  waiting for transfers between devices  6.01 us (20%)
  other arithmetic  0.66 us (2%)
    pallas_call x2, Pallas kernels, gather(): pl.pallas_call(functools.partial(gather_kernel, by_column), out_shape=[VM...  6.11 us
    ppermute x3, starting transfers between devices, fast(): lax.ppermute(pre, ('store', 'tensor'), over_store(ROUND_TWO, turn))  3.91 us
    ppermute x3, starting transfers between devices, fast(): lax.ppermute(chunks[turn], ('store', 'tensor'), over_store(ROUND_ONE, turn))  3.67 us
    ppermute x2, starting transfers between devices, fast(): lax.ppermute(both[k * rows:(k + 1) * rows], ('store', 'tensor'), home(k))  3.46 us
    ppermute x2, waiting for transfers between devices, fast(): lax.ppermute(both[k * rows:(k + 1) * rows], ('store', 'tensor'), home(k))  2.86 us
    ppermute x1, starting transfers between devices, fast(): both = (keep + lax.ppermute(send, 'tensor', pair)).astype(BF16)  1.93 us
    ppermute x3, waiting for transfers between devices, fast(): lax.ppermute(pre, ('store', 'tensor'), over_store(ROUND_TWO, turn))  1.68 us
    pallas_call x1, Pallas kernels, fast(): pl.pallas_call(functools.partial(second_kernel, count, slots), out_shape=...  1.32 us
  transfers between devices with their start and end apart: 9, of which 5 were waited for; matrix products, arithmetic and copies ran while one was open for 0% of the time, Pallas kernels for 21%

profile of v8, /device:TPU:3, one launch (start us, length us, event | category | flops | bytes accessed | tf_op | source)
XLA Modules:
  0.0 29.5 jit_solution(1178469071801441693)
XLA Ops:
  0.0 0.0 copy-start
  0.0 1.0 %split_states.1 = (bf16[16,1664]{1,0:T(8,128)(2,1)S(1)}, bf16[16,1664]{1,0:T(8,128)(2,1)S(1)}, bf16[16,1664]{1,0:T(8,128)(2,1)S(1)}, bf16[16,1664]{1,0:T(8,128)(2,1)S(1)}, s32[1,16]{1,0:T(1,128)S(1)}) custom-call(bf16[16,6144]{1,0:T(8,128)(2,1)} %states_ref.1, s32[4,16]{1,0:T(4,128)} %bitcast.5, s32[1,16]{1,0:T(1,128)} %union_ref.1), custom_call_target="tpu_custom_call" | custom-call | tf_op jit(solution)/shard_map/split_states/pallas_call | solution.py:187
  1.0 2.4 %collective-permute-start = (bf16[16,1664]{1,0:T(8,128)(2,1)S(1)}, bf16[16,1664]{1,0:T(8,128)(2,1)S(1)}, u32[]{:S(2)}, u32[]{:S(2)}) collective-permute-start(bf16[16,1664]{1,0:T(8,128)(2,1)S(1)} %get-tuple-element.16), channel_id=1, source_target_pairs={{0,8},{1,9},{2,10},{3,11},{4,12},{5,13},{6,14},{7,15},{8,0},{9,1},... | collective-permute-start | bytes 159752 | tf_op jit(solution)/shard_map/ppermute | solution.py:203
  3.4 1.1 %collective-permute-start.1 = (bf16[16,1664]{1,0:T(8,128)(2,1)S(1)}, bf16[16,1664]{1,0:T(8,128)(2,1)S(1)}, u32[]{:S(2)}, u32[]{:S(2)}) collective-permute-start(bf16[16,1664]{1,0:T(8,128)(2,1)S(1)} %get-tuple-element.17), channel_id=1, source_target_pairs={{0,12},{1,13},{2,14},{3,15},{4,8},{5,9},{6,10},{7,11},{8,4},{9,5},... | collective-permute-start | bytes 159752 | tf_op jit(solution)/shard_map/ppermute | solution.py:203
  4.5 0.2 collective-permute-start.2
  4.7 3.1 %gather_in.1.refs_4_ = bf16[1536,2048]{1,0:T(8,128)(2,1)S(1)} custom-call(s32[1,16]{1,0:T(1,128)S(1)} %get-tuple-element.20.union_ref, bf16[1536,6144]{1,0:T(8,128)(2,1)} %weight_ref.2), custom_call_target="tpu_custom_call" | custom-call | bytes 12582912 | tf_op jit(solution)/shard_map/gather_in/pallas_call | solution.py:86
  7.8 0.0 copy-start.1
  7.8 0.0 collective-permute-done.refs_0_
  7.9 0.4 %collective-permute-done.1.refs_1_ = bf16[16,1664]{1,0:T(8,128)(2,1)S(1)} collective-permute-done((bf16[16,1664]{1,0:T(8,128)(2,1)S(1)}, bf16[16,1664]{1,0:T(8,128)(2,1)S(1)}, u32[]{:S(2)}, u32[]{:S(2)}) %collective-permute-start.1) | collective-permute-done | bytes 53280 | tf_op jit(solution)/shard_map/ppermute | solution.py:203
  8.3 0.0 collective-permute-done.2.refs_2_
  8.3 1.3 %first_dot.1 = (bf16[64,512]{1,0:T(8,128)(2,1)S(1)}, f32[64,128]{1,0:T(8,128)S(1)}) custom-call(bf16[16,1664]{1,0:T(8,128)(2,1)S(1)} %collective-permute-done.refs_0_, bf16[16,1664]{1,0:T(8,128)(2,1)S(1)} %collective-permute-done.1.refs_1_, bf16[16,1664]{1,0:T(8,128)(2,1)S(1)} %collective-permute-done.2.refs_2_, ...), custom_call_target="tpu_custom_call" | custom-call | tf_op jit(solution)/shard_map/first_dot/pallas_call | solution.py:209
  9.6 2.6 %collective-permute-start.5 = (bf16[64,512]{1,0:T(8,128)(2,1)S(1)}, bf16[64,512]{1,0:T(8,128)(2,1)S(1)}, u32[]{:S(2)}, u32[]{:S(2)}) collective-permute-start(bf16[64,512]{1,0:T(8,128)(2,1)S(1)} %get-tuple-element.23.refs_3_), channel_id=1, source_target_pairs={{0,12},{1,9},{2,14},{3,11},{4,8},{5,13},{6,10},{7,15},{8,4},{9,1},... | collective-permute-start | bytes 196616 | tf_op jit(solution)/shard_map/ppermute | solution.py:223
  12.2 0.0 collective-permute-start.4
  12.2 1.3 %collective-permute-start.3 = (bf16[64,512]{1,0:T(8,128)(2,1)S(1)}, bf16[64,512]{1,0:T(8,128)(2,1)S(1)}, u32[]{:S(2)}, u32[]{:S(2)}) collective-permute-start(bf16[64,512]{1,0:T(8,128)(2,1)S(1)} %get-tuple-element.23.refs_3_), channel_id=1, source_target_pairs={{0,4},{1,13},{2,6},{3,15},{4,0},{5,9},{6,2},{7,11},{8,12},{9,5},{1... | collective-permute-start | bytes 196616 | tf_op jit(solution)/shard_map/ppermute | solution.py:223
  13.5 0.0 copy-done
  13.5 3.0 %gather_out.1 = (bf16[2048,1536]{1,0:T(8,128)(2,1)S(1)}, f32[16,128]{1,0:T(8,128)S(1)}) custom-call(s32[1,16]{1,0:T(1,128)S(1)} %get-tuple-element.20.union_ref, bf16[6144,1536]{1,0:T(8,128)(2,1)} %weight_ref.3, f32[48,128]{1,0:T(8,128)S(1)} %bitcast.4), custom_call_target="tpu_custom_call" | custom-call | bytes 12582912 | tf_op jit(solution)/shard_map/gather_out/pallas_call | solution.py:86
  16.4 0.0 collective-permute-done.5.refs_2_
  16.5 0.0 collective-permute-done.4.refs_1_
  16.5 1.7 %collective-permute-done.3.refs_0_ = bf16[64,512]{1,0:T(8,128)(2,1)S(1)} collective-permute-done((bf16[64,512]{1,0:T(8,128)(2,1)S(1)}, bf16[64,512]{1,0:T(8,128)(2,1)S(1)}, u32[]{:S(2)}, u32[]{:S(2)}) %collective-permute-start.3) | collective-permute-done | bytes 65568 | tf_op jit(solution)/shard_map/ppermute | solution.py:223
  18.1 1.3 %second_dot.1 = (f32[32,1536]{1,0:T(8,128)S(1)}, f32[32,1536]{1,0:T(8,128)S(1)}) custom-call(f32[64,128]{1,0:T(8,128)S(1)} %get-tuple-element.21.ids_ref, f32[16,128]{1,0:T(8,128)S(1)} %get-tuple-element.22.bias_ref, bf16[64,512]{1,0:T(8,128)(2,1)S(1)} %collective-permute-done.3.refs_0_, bf16[64,512]{1,0:T(8,128)(2,1)S(1)} %collective-permute-done.4.refs_1_, ...), custom_call_target="tpu_custom_call" | custom-call | tf_op jit(solution)/shard_map/second_dot/pallas_call | solution.py:229
  19.5 1.9 %collective-permute-start.6 = (f32[32,1536]{1,0:T(8,128)S(1)}, f32[32,1536]{1,0:T(8,128)S(1)}, u32[]{:S(2)}, u32[]{:S(2)}) collective-permute-start(f32[32,1536]{1,0:T(8,128)S(1)} %get-tuple-element.26), channel_id=1, source_target_pairs={{0,1},{1,0},{2,3},{3,2},{4,5},{5,4},{6,7},{7,6},{8,9},{9,8},{10,11... | collective-permute-start | bytes 589832 | tf_op jit(solution)/shard_map/ppermute | solution.py:240
  21.4 1.1 %collective-permute-done.6 = f32[32,1536]{1,0:T(8,128)S(1)} collective-permute-done((f32[32,1536]{1,0:T(8,128)S(1)}, f32[32,1536]{1,0:T(8,128)S(1)}, u32[]{:S(2)}, u32[]{:S(2)}) %collective-permute-start.6) | collective-permute-done | bytes 196640 | tf_op jit(solution)/shard_map/ppermute | solution.py:240
  22.5 0.6 %collective-permute-start.7 = (bf16[16,1536]{1,0:T(8,128)(2,1)S(1)}, bf16[16,1536]{1,0:T(8,128)(2,1)S(1)}, u32[]{:S(2)}, u32[]{:S(2)}) collective-permute-start(bf16[16,1536]{1,0:T(8,128)(2,1)S(1)} %get-tuple-element.27), channel_id=1, source_target_pairs={{0,8},{1,12},{2,4},{3,0},{4,5},{5,9},{6,13},{7,1},{8,6},{9,14},{10... | collective-permute-start | bytes 147464 | tf_op jit(solution)/shard_map/ppermute | solution.py:249
  23.1 2.9 %collective-permute-start.8 = (bf16[16,1536]{1,0:T(8,128)(2,1)S(1)}, bf16[16,1536]{1,0:T(8,128)(2,1)S(1)}, u32[]{:S(2)}, u32[]{:S(2)}) collective-permute-start(bf16[16,1536]{1,0:T(8,128)(2,1)S(1)} %get-tuple-element.28), channel_id=1, source_target_pairs={{0,4},{1,0},{2,8},{3,12},{4,13},{5,1},{6,5},{7,9},{8,2},{9,10},{10... | collective-permute-start | bytes 147464 | tf_op jit(solution)/shard_map/ppermute | solution.py:249
  26.0 1.4 %collective-permute-done.7 = bf16[16,1536]{1,0:T(8,128)(2,1)S(1)} collective-permute-done((bf16[16,1536]{1,0:T(8,128)(2,1)S(1)}, bf16[16,1536]{1,0:T(8,128)(2,1)S(1)}, u32[]{:S(2)}, u32[]{:S(2)}) %collective-permute-start.7) | collective-permute-done | bytes 49184 | tf_op jit(solution)/shard_map/ppermute | solution.py:249
  27.4 1.4 %collective-permute-done.8 = bf16[16,1536]{1,0:T(8,128)(2,1)S(1)} collective-permute-done((bf16[16,1536]{1,0:T(8,128)(2,1)S(1)}, bf16[16,1536]{1,0:T(8,128)(2,1)S(1)}, u32[]{:S(2)}, u32[]{:S(2)}) %collective-permute-start.8) | collective-permute-done | bytes 49184 | tf_op jit(solution)/shard_map/ppermute | solution.py:249
  28.8 0.0 copy-done.1
  28.8 0.6 %add_convert_fusion.1 = bf16[16,1536]{1,0:T(8,128)(2,1)} fusion(bf16[16,1536]{1,0:T(8,128)(2,1)S(1)} %collective-permute-done.8, bf16[16,1536]{1,0:T(8,128)(2,1)S(1)} %collective-permute-done.7, f32[1536]{0:T(1024)S(1)} %copy-done.1), kind=kLoop, calls=%fused_computation.1 | loop fusion | flops 122880 | bytes 153600 | tf_op jit(solution)/shard_map/convert_element_type | solution.py:252
  (2 shorter events, 0.0 us)
Async XLA Ops:
  0.0 13.5 %copy-start = (f32[6144]{0:T(1024)S(1)}, f32[6144]{0:T(1024)}, u32[]{:S(2)}) copy-start(f32[6144]{0:T(1024)} %param.9) | copy-start | bytes 73732
  1.0 6.8 %collective-permute-start = (bf16[16,1664]{1,0:T(8,128)(2,1)S(1)}, bf16[16,1664]{1,0:T(8,128)(2,1)S(1)}, u32[]{:S(2)}, u32[]{:S(2)}) collective-permute-start(bf16[16,1664]{1,0:T(8,128)(2,1)S(1)} %get-tuple-element.16), channel_id=1, source_target_pairs={{0,8},{1,9},{2,10},{3,11},{4,12},{5,13},{6,14},{7,15},{8,0},{9,1},... | collective-permute-start | bytes 159752 | tf_op jit(solution)/shard_map/ppermute | solution.py:203
  3.4 4.9 %collective-permute-start.1 = (bf16[16,1664]{1,0:T(8,128)(2,1)S(1)}, bf16[16,1664]{1,0:T(8,128)(2,1)S(1)}, u32[]{:S(2)}, u32[]{:S(2)}) collective-permute-start(bf16[16,1664]{1,0:T(8,128)(2,1)S(1)} %get-tuple-element.17), channel_id=1, source_target_pairs={{0,12},{1,13},{2,14},{3,15},{4,8},{5,9},{6,10},{7,11},{8,4},{9,5},... | collective-permute-start | bytes 159752 | tf_op jit(solution)/shard_map/ppermute | solution.py:203
  4.5 3.8 %collective-permute-start.2 = (bf16[16,1664]{1,0:T(8,128)(2,1)S(1)}, bf16[16,1664]{1,0:T(8,128)(2,1)S(1)}, u32[]{:S(2)}, u32[]{:S(2)}) collective-permute-start(bf16[16,1664]{1,0:T(8,128)(2,1)S(1)} %get-tuple-element.18), channel_id=1, source_target_pairs={{0,4},{1,5},{2,6},{3,7},{4,0},{5,1},{6,2},{7,3},{8,12},{9,13},{10,... | collective-permute-start | bytes 159752 | tf_op jit(solution)/shard_map/ppermute | solution.py:203
  7.8 21.0 %copy-start.1 = (f32[1536]{0:T(1024)S(1)}, f32[1536]{0:T(1024)}, u32[]{:S(2)}) copy-start(f32[1536]{0:T(1024)} %param.11) | copy-start | bytes 18436
  9.6 6.9 %collective-permute-start.5 = (bf16[64,512]{1,0:T(8,128)(2,1)S(1)}, bf16[64,512]{1,0:T(8,128)(2,1)S(1)}, u32[]{:S(2)}, u32[]{:S(2)}) collective-permute-start(bf16[64,512]{1,0:T(8,128)(2,1)S(1)} %get-tuple-element.23.refs_3_), channel_id=1, source_target_pairs={{0,12},{1,9},{2,14},{3,11},{4,8},{5,13},{6,10},{7,15},{8,4},{9,1},... | collective-permute-start | bytes 196616 | tf_op jit(solution)/shard_map/ppermute | solution.py:223
  12.2 4.2 %collective-permute-start.4 = (bf16[64,512]{1,0:T(8,128)(2,1)S(1)}, bf16[64,512]{1,0:T(8,128)(2,1)S(1)}, u32[]{:S(2)}, u32[]{:S(2)}) collective-permute-start(bf16[64,512]{1,0:T(8,128)(2,1)S(1)} %get-tuple-element.23.refs_3_), channel_id=1, source_target_pairs={{0,8},{1,5},{2,10},{3,7},{4,12},{5,1},{6,14},{7,3},{8,0},{9,13},{1... | collective-permute-start | bytes 196616 | tf_op jit(solution)/shard_map/ppermute | solution.py:223
  12.2 5.9 %collective-permute-start.3 = (bf16[64,512]{1,0:T(8,128)(2,1)S(1)}, bf16[64,512]{1,0:T(8,128)(2,1)S(1)}, u32[]{:S(2)}, u32[]{:S(2)}) collective-permute-start(bf16[64,512]{1,0:T(8,128)(2,1)S(1)} %get-tuple-element.23.refs_3_), channel_id=1, source_target_pairs={{0,4},{1,13},{2,6},{3,15},{4,0},{5,9},{6,2},{7,11},{8,12},{9,5},{1... | collective-permute-start | bytes 196616 | tf_op jit(solution)/shard_map/ppermute | solution.py:223
  19.5 3.0 %collective-permute-start.6 = (f32[32,1536]{1,0:T(8,128)S(1)}, f32[32,1536]{1,0:T(8,128)S(1)}, u32[]{:S(2)}, u32[]{:S(2)}) collective-permute-start(f32[32,1536]{1,0:T(8,128)S(1)} %get-tuple-element.26), channel_id=1, source_target_pairs={{0,1},{1,0},{2,3},{3,2},{4,5},{5,4},{6,7},{7,6},{8,9},{9,8},{10,11... | collective-permute-start | bytes 589832 | tf_op jit(solution)/shard_map/ppermute | solution.py:240
  22.5 4.9 %collective-permute-start.7 = (bf16[16,1536]{1,0:T(8,128)(2,1)S(1)}, bf16[16,1536]{1,0:T(8,128)(2,1)S(1)}, u32[]{:S(2)}, u32[]{:S(2)}) collective-permute-start(bf16[16,1536]{1,0:T(8,128)(2,1)S(1)} %get-tuple-element.27), channel_id=1, source_target_pairs={{0,8},{1,12},{2,4},{3,0},{4,5},{5,9},{6,13},{7,1},{8,6},{9,14},{10... | collective-permute-start | bytes 147464 | tf_op jit(solution)/shard_map/ppermute | solution.py:249
  23.1 5.7 %collective-permute-start.8 = (bf16[16,1536]{1,0:T(8,128)(2,1)S(1)}, bf16[16,1536]{1,0:T(8,128)(2,1)S(1)}, u32[]{:S(2)}, u32[]{:S(2)}) collective-permute-start(bf16[16,1536]{1,0:T(8,128)(2,1)S(1)} %get-tuple-element.28), channel_id=1, source_target_pairs={{0,4},{1,0},{2,8},{3,12},{4,13},{5,1},{6,5},{7,9},{8,2},{9,10},{10... | collective-permute-start | bytes 147464 | tf_op jit(solution)/shard_map/ppermute | solution.py:249

commit v9 on v8

--- a/solution.py
+++ b/solution.py
@@ -164,7 +164,7 @@
     ((2, 1), (3, 0), (1, 2), (0, 3)),
     ((1, 3), (2, 0), (3, 1), (0, 2)),
     ((1, 0), (3, 2), (0, 1), (2, 3)),
-    ((1, 3), (2, 0), (3, 1), (0, 2)),
+    ((1, 3), (0, 2), (3, 1), (2, 0)),
 )
 
 

time: 29.9 us -> 29.7 us (level)
  the two profiles are of different devices: /device:TPU:3 before, /device:TPU:2 now
where the time goes in v9:
time: 29.7 us; the launch traced here: 29.5 us
  starting transfers between devices  11.6 us (39%)
  Pallas kernels  9.72 us (33%)
  waiting for transfers between devices  7.4 us (25%)
  other arithmetic  0.66 us (2%)
    pallas_call x2, Pallas kernels, gather(): pl.pallas_call(functools.partial(gather_kernel, by_column), out_shape=[VM...  6.11 us
    ppermute x3, starting transfers between devices, fast(): lax.ppermute(pre, ('store', 'tensor'), over_store(ROUND_TWO, turn))  4.45 us
    ppermute x3, starting transfers between devices, fast(): lax.ppermute(chunks[turn], ('store', 'tensor'), over_store(ROUND_ONE, turn))  4.23 us
    ppermute x2, waiting for transfers between devices, fast(): lax.ppermute(both[k * rows:(k + 1) * rows], ('store', 'tensor'), home(k))  3.79 us
    ppermute x2, starting transfers between devices, fast(): lax.ppermute(both[k * rows:(k + 1) * rows], ('store', 'tensor'), home(k))  2.84 us
    ppermute x1, waiting for transfers between devices, fast(): both = (keep + lax.ppermute(send, 'tensor', pair)).astype(BF16)  1.43 us
    pallas_call x1, Pallas kernels, fast(): pl.pallas_call(functools.partial(second_kernel, count, slots), out_shape=...  1.31 us
    pallas_call x1, Pallas kernels, fast(): pl.pallas_call(functools.partial(first_kernel, count, slots), out_shape=[...  1.3 us
  transfers between devices with their start and end apart: 9, of which 5 were waited for; matrix products, arithmetic and copies ran while one was open for 0% of the time, Pallas kernels for 21%

profile of v9, /device:TPU:2, one launch (start us, length us, event | category | flops | bytes accessed | tf_op | source)
XLA Modules:
  0.0 29.5 jit_solution(16144113716733491202)
XLA Ops:
  0.0 0.0 copy-start
  0.0 1.0 %split_states.1 = (bf16[16,1664]{1,0:T(8,128)(2,1)S(1)}, bf16[16,1664]{1,0:T(8,128)(2,1)S(1)}, bf16[16,1664]{1,0:T(8,128)(2,1)S(1)}, bf16[16,1664]{1,0:T(8,128)(2,1)S(1)}, s32[1,16]{1,0:T(1,128)S(1)}) custom-call(bf16[16,6144]{1,0:T(8,128)(2,1)} %states_ref.1, s32[4,16]{1,0:T(4,128)} %bitcast.5, s32[1,16]{1,0:T(1,128)} %union_ref.1), custom_call_target="tpu_custom_call" | custom-call | tf_op jit(solution)/shard_map/split_states/pallas_call | solution.py:187
  1.0 2.7 %collective-permute-start = (bf16[16,1664]{1,0:T(8,128)(2,1)S(1)}, bf16[16,1664]{1,0:T(8,128)(2,1)S(1)}, u32[]{:S(2)}, u32[]{:S(2)}) collective-permute-start(bf16[16,1664]{1,0:T(8,128)(2,1)S(1)} %get-tuple-element.16), channel_id=1, source_target_pairs={{0,8},{1,9},{2,10},{3,11},{4,12},{5,13},{6,14},{7,15},{8,0},{9,1},... | collective-permute-start | bytes 159752 | tf_op jit(solution)/shard_map/ppermute | solution.py:203
  3.7 1.3 %collective-permute-start.1 = (bf16[16,1664]{1,0:T(8,128)(2,1)S(1)}, bf16[16,1664]{1,0:T(8,128)(2,1)S(1)}, u32[]{:S(2)}, u32[]{:S(2)}) collective-permute-start(bf16[16,1664]{1,0:T(8,128)(2,1)S(1)} %get-tuple-element.17), channel_id=1, source_target_pairs={{0,12},{1,13},{2,14},{3,15},{4,8},{5,9},{6,10},{7,11},{8,4},{9,5},... | collective-permute-start | bytes 159752 | tf_op jit(solution)/shard_map/ppermute | solution.py:203
  5.0 0.2 collective-permute-start.2
  5.2 3.1 %gather_in.1.refs_4_ = bf16[1536,2048]{1,0:T(8,128)(2,1)S(1)} custom-call(s32[1,16]{1,0:T(1,128)S(1)} %get-tuple-element.20.union_ref, bf16[1536,6144]{1,0:T(8,128)(2,1)} %weight_ref.2), custom_call_target="tpu_custom_call" | custom-call | bytes 12582912 | tf_op jit(solution)/shard_map/gather_in/pallas_call | solution.py:86
  8.4 0.0 copy-start.1
  8.4 0.0 collective-permute-done.refs_0_
  8.4 1.3 %collective-permute-done.1.refs_1_ = bf16[16,1664]{1,0:T(8,128)(2,1)S(1)} collective-permute-done((bf16[16,1664]{1,0:T(8,128)(2,1)S(1)}, bf16[16,1664]{1,0:T(8,128)(2,1)S(1)}, u32[]{:S(2)}, u32[]{:S(2)}) %collective-permute-start.1) | collective-permute-done | bytes 53280 | tf_op jit(solution)/shard_map/ppermute | solution.py:203
  9.7 0.0 collective-permute-done.2.refs_2_
  9.7 1.3 %first_dot.1 = (bf16[64,512]{1,0:T(8,128)(2,1)S(1)}, f32[64,128]{1,0:T(8,128)S(1)}) custom-call(bf16[16,1664]{1,0:T(8,128)(2,1)S(1)} %collective-permute-done.refs_0_, bf16[16,1664]{1,0:T(8,128)(2,1)S(1)} %collective-permute-done.1.refs_1_, bf16[16,1664]{1,0:T(8,128)(2,1)S(1)} %collective-permute-done.2.refs_2_, ...), custom_call_target="tpu_custom_call" | custom-call | tf_op jit(solution)/shard_map/first_dot/pallas_call | solution.py:209
  11.0 2.5 %collective-permute-start.5 = (bf16[64,512]{1,0:T(8,128)(2,1)S(1)}, bf16[64,512]{1,0:T(8,128)(2,1)S(1)}, u32[]{:S(2)}, u32[]{:S(2)}) collective-permute-start(bf16[64,512]{1,0:T(8,128)(2,1)S(1)} %get-tuple-element.23.refs_3_), channel_id=1, source_target_pairs={{0,12},{1,9},{2,14},{3,11},{4,8},{5,13},{6,10},{7,15},{8,4},{9,1},... | collective-permute-start | bytes 196616 | tf_op jit(solution)/shard_map/ppermute | solution.py:223
  13.6 0.0 collective-permute-start.4
  13.6 1.9 %collective-permute-start.3 = (bf16[64,512]{1,0:T(8,128)(2,1)S(1)}, bf16[64,512]{1,0:T(8,128)(2,1)S(1)}, u32[]{:S(2)}, u32[]{:S(2)}) collective-permute-start(bf16[64,512]{1,0:T(8,128)(2,1)S(1)} %get-tuple-element.23.refs_3_), channel_id=1, source_target_pairs={{0,4},{1,13},{2,6},{3,15},{4,0},{5,9},{6,2},{7,11},{8,12},{9,5},{1... | collective-permute-start | bytes 196616 | tf_op jit(solution)/shard_map/ppermute | solution.py:223
  15.5 0.0 copy-done
  15.5 3.0 %gather_out.1 = (bf16[2048,1536]{1,0:T(8,128)(2,1)S(1)}, f32[16,128]{1,0:T(8,128)S(1)}) custom-call(s32[1,16]{1,0:T(1,128)S(1)} %get-tuple-element.20.union_ref, bf16[6144,1536]{1,0:T(8,128)(2,1)} %weight_ref.3, f32[48,128]{1,0:T(8,128)S(1)} %bitcast.4), custom_call_target="tpu_custom_call" | custom-call | bytes 12582912 | tf_op jit(solution)/shard_map/gather_out/pallas_call | solution.py:86
  18.5 0.0 collective-permute-done.5.refs_2_
  18.5 0.9 %collective-permute-done.4.refs_1_ = bf16[64,512]{1,0:T(8,128)(2,1)S(1)} collective-permute-done((bf16[64,512]{1,0:T(8,128)(2,1)S(1)}, bf16[64,512]{1,0:T(8,128)(2,1)S(1)}, u32[]{:S(2)}, u32[]{:S(2)}) %collective-permute-start.4) | collective-permute-done | bytes 65568 | tf_op jit(solution)/shard_map/ppermute | solution.py:223
  19.3 0.0 collective-permute-done.3.refs_0_
  19.3 1.3 %second_dot.1 = (f32[32,1536]{1,0:T(8,128)S(1)}, f32[32,1536]{1,0:T(8,128)S(1)}) custom-call(f32[64,128]{1,0:T(8,128)S(1)} %get-tuple-element.21.ids_ref, f32[16,128]{1,0:T(8,128)S(1)} %get-tuple-element.22.bias_ref, bf16[64,512]{1,0:T(8,128)(2,1)S(1)} %collective-permute-done.3.refs_0_, bf16[64,512]{1,0:T(8,128)(2,1)S(1)} %collective-permute-done.4.refs_1_, ...), custom_call_target="tpu_custom_call" | custom-call | tf_op jit(solution)/shard_map/second_dot/pallas_call | solution.py:229
  20.7 0.1 collective-permute-start.6
  20.7 1.4 %collective-permute-done.6 = f32[32,1536]{1,0:T(8,128)S(1)} collective-permute-done((f32[32,1536]{1,0:T(8,128)S(1)}, f32[32,1536]{1,0:T(8,128)S(1)}, u32[]{:S(2)}, u32[]{:S(2)}) %collective-permute-start.6) | collective-permute-done | bytes 196640 | tf_op jit(solution)/shard_map/ppermute | solution.py:240
  22.2 0.4 %collective-permute-start.7 = (bf16[16,1536]{1,0:T(8,128)(2,1)S(1)}, bf16[16,1536]{1,0:T(8,128)(2,1)S(1)}, u32[]{:S(2)}, u32[]{:S(2)}) collective-permute-start(bf16[16,1536]{1,0:T(8,128)(2,1)S(1)} %get-tuple-element.27), channel_id=1, source_target_pairs={{0,8},{1,12},{2,4},{3,0},{4,5},{5,9},{6,13},{7,1},{8,6},{9,14},{10... | collective-permute-start | bytes 147464 | tf_op jit(solution)/shard_map/ppermute | solution.py:249
  22.6 2.4 %collective-permute-start.8 = (bf16[16,1536]{1,0:T(8,128)(2,1)S(1)}, bf16[16,1536]{1,0:T(8,128)(2,1)S(1)}, u32[]{:S(2)}, u32[]{:S(2)}) collective-permute-start(bf16[16,1536]{1,0:T(8,128)(2,1)S(1)} %get-tuple-element.28), channel_id=1, source_target_pairs={{0,4},{1,0},{2,8},{3,12},{4,13},{5,1},{6,5},{7,9},{8,2},{9,10},{10... | collective-permute-start | bytes 147464 | tf_op jit(solution)/shard_map/ppermute | solution.py:249
  25.0 2.2 %collective-permute-done.7 = bf16[16,1536]{1,0:T(8,128)(2,1)S(1)} collective-permute-done((bf16[16,1536]{1,0:T(8,128)(2,1)S(1)}, bf16[16,1536]{1,0:T(8,128)(2,1)S(1)}, u32[]{:S(2)}, u32[]{:S(2)}) %collective-permute-start.7) | collective-permute-done | bytes 49184 | tf_op jit(solution)/shard_map/ppermute | solution.py:249
  27.3 1.6 %collective-permute-done.8 = bf16[16,1536]{1,0:T(8,128)(2,1)S(1)} collective-permute-done((bf16[16,1536]{1,0:T(8,128)(2,1)S(1)}, bf16[16,1536]{1,0:T(8,128)(2,1)S(1)}, u32[]{:S(2)}, u32[]{:S(2)}) %collective-permute-start.8) | collective-permute-done | bytes 49184 | tf_op jit(solution)/shard_map/ppermute | solution.py:249
  28.8 0.0 copy-done.1
  28.8 0.6 %add_convert_fusion.1 = bf16[16,1536]{1,0:T(8,128)(2,1)} fusion(bf16[16,1536]{1,0:T(8,128)(2,1)S(1)} %collective-permute-done.8, bf16[16,1536]{1,0:T(8,128)(2,1)S(1)} %collective-permute-done.7, f32[1536]{0:T(1024)S(1)} %copy-done.1), kind=kLoop, calls=%fused_computation.1 | loop fusion | flops 122880 | bytes 153600 | tf_op jit(solution)/shard_map/convert_element_type | solution.py:252
  (2 shorter events, 0.0 us)
Async XLA Ops:
  0.0 15.5 %copy-start = (f32[6144]{0:T(1024)S(1)}, f32[6144]{0:T(1024)}, u32[]{:S(2)}) copy-start(f32[6144]{0:T(1024)} %param.9) | copy-start | bytes 73732
  1.0 7.4 %collective-permute-start = (bf16[16,1664]{1,0:T(8,128)(2,1)S(1)}, bf16[16,1664]{1,0:T(8,128)(2,1)S(1)}, u32[]{:S(2)}, u32[]{:S(2)}) collective-permute-start(bf16[16,1664]{1,0:T(8,128)(2,1)S(1)} %get-tuple-element.16), channel_id=1, source_target_pairs={{0,8},{1,9},{2,10},{3,11},{4,12},{5,13},{6,14},{7,15},{8,0},{9,1},... | collective-permute-start | bytes 159752 | tf_op jit(solution)/shard_map/ppermute | solution.py:203
  3.7 6.0 %collective-permute-start.1 = (bf16[16,1664]{1,0:T(8,128)(2,1)S(1)}, bf16[16,1664]{1,0:T(8,128)(2,1)S(1)}, u32[]{:S(2)}, u32[]{:S(2)}) collective-permute-start(bf16[16,1664]{1,0:T(8,128)(2,1)S(1)} %get-tuple-element.17), channel_id=1, source_target_pairs={{0,12},{1,13},{2,14},{3,15},{4,8},{5,9},{6,10},{7,11},{8,4},{9,5},... | collective-permute-start | bytes 159752 | tf_op jit(solution)/shard_map/ppermute | solution.py:203
  5.0 4.7 %collective-permute-start.2 = (bf16[16,1664]{1,0:T(8,128)(2,1)S(1)}, bf16[16,1664]{1,0:T(8,128)(2,1)S(1)}, u32[]{:S(2)}, u32[]{:S(2)}) collective-permute-start(bf16[16,1664]{1,0:T(8,128)(2,1)S(1)} %get-tuple-element.18), channel_id=1, source_target_pairs={{0,4},{1,5},{2,6},{3,7},{4,0},{5,1},{6,2},{7,3},{8,12},{9,13},{10,... | collective-permute-start | bytes 159752 | tf_op jit(solution)/shard_map/ppermute | solution.py:203
  8.4 20.4 %copy-start.1 = (f32[1536]{0:T(1024)S(1)}, f32[1536]{0:T(1024)}, u32[]{:S(2)}) copy-start(f32[1536]{0:T(1024)} %param.11) | copy-start | bytes 18436
  11.0 7.4 %collective-permute-start.5 = (bf16[64,512]{1,0:T(8,128)(2,1)S(1)}, bf16[64,512]{1,0:T(8,128)(2,1)S(1)}, u32[]{:S(2)}, u32[]{:S(2)}) collective-permute-start(bf16[64,512]{1,0:T(8,128)(2,1)S(1)} %get-tuple-element.23.refs_3_), channel_id=1, source_target_pairs={{0,12},{1,9},{2,14},{3,11},{4,8},{5,13},{6,10},{7,15},{8,4},{9,1},... | collective-permute-start | bytes 196616 | tf_op jit(solution)/shard_map/ppermute | solution.py:223
  13.6 5.8 %collective-permute-start.4 = (bf16[64,512]{1,0:T(8,128)(2,1)S(1)}, bf16[64,512]{1,0:T(8,128)(2,1)S(1)}, u32[]{:S(2)}, u32[]{:S(2)}) collective-permute-start(bf16[64,512]{1,0:T(8,128)(2,1)S(1)} %get-tuple-element.23.refs_3_), channel_id=1, source_target_pairs={{0,8},{1,5},{2,10},{3,7},{4,12},{5,1},{6,14},{7,3},{8,0},{9,13},{1... | collective-permute-start | bytes 196616 | tf_op jit(solution)/shard_map/ppermute | solution.py:223
  13.6 5.8 %collective-permute-start.3 = (bf16[64,512]{1,0:T(8,128)(2,1)S(1)}, bf16[64,512]{1,0:T(8,128)(2,1)S(1)}, u32[]{:S(2)}, u32[]{:S(2)}) collective-permute-start(bf16[64,512]{1,0:T(8,128)(2,1)S(1)} %get-tuple-element.23.refs_3_), channel_id=1, source_target_pairs={{0,4},{1,13},{2,6},{3,15},{4,0},{5,9},{6,2},{7,11},{8,12},{9,5},{1... | collective-permute-start | bytes 196616 | tf_op jit(solution)/shard_map/ppermute | solution.py:223
  20.7 1.5 %collective-permute-start.6 = (f32[32,1536]{1,0:T(8,128)S(1)}, f32[32,1536]{1,0:T(8,128)S(1)}, u32[]{:S(2)}, u32[]{:S(2)}) collective-permute-start(f32[32,1536]{1,0:T(8,128)S(1)} %get-tuple-element.26), channel_id=1, source_target_pairs={{0,1},{1,0},{2,3},{3,2},{4,5},{5,4},{6,7},{7,6},{8,9},{9,8},{10,11... | collective-permute-start | bytes 589832 | tf_op jit(solution)/shard_map/ppermute | solution.py:240
  22.2 5.1 %collective-permute-start.7 = (bf16[16,1536]{1,0:T(8,128)(2,1)S(1)}, bf16[16,1536]{1,0:T(8,128)(2,1)S(1)}, u32[]{:S(2)}, u32[]{:S(2)}) collective-permute-start(bf16[16,1536]{1,0:T(8,128)(2,1)S(1)} %get-tuple-element.27), channel_id=1, source_target_pairs={{0,8},{1,12},{2,4},{3,0},{4,5},{5,9},{6,13},{7,1},{8,6},{9,14},{10... | collective-permute-start | bytes 147464 | tf_op jit(solution)/shard_map/ppermute | solution.py:249
  22.6 6.2 %collective-permute-start.8 = (bf16[16,1536]{1,0:T(8,128)(2,1)S(1)}, bf16[16,1536]{1,0:T(8,128)(2,1)S(1)}, u32[]{:S(2)}, u32[]{:S(2)}) collective-permute-start(bf16[16,1536]{1,0:T(8,128)(2,1)S(1)} %get-tuple-element.28), channel_id=1, source_target_pairs={{0,4},{1,0},{2,8},{3,12},{4,13},{5,1},{6,5},{7,9},{8,2},{9,10},{10... | collective-permute-start | bytes 147464 | tf_op jit(solution)/shard_map/ppermute | solution.py:249
